TPU v7x, 512 devices: a whole 4x4x16 slice. The times are simulated.
512 devices in a mesh: seq: 64 (over z_lo, x, core), inner: 8 (over y, z_hi).
Axes of the slice: x: 4, y: 4, z: 16 (z_hi: 2, z_lo: 8; z = z_hi * 8 + z_lo), core: 2. Of those that a mesh axis runs over, the one named last changes fastest.
Arguments:
- tokens: bfloat16 [196608, 1280], P(('seq', 'inner')), may hold values from -320 to 320
- slot_embed: bfloat16 [1280, 512], replicated, may hold values from -1 to 1
- up_codes: bfloat16 [64, 1280, 5120], P('seq', None, 'inner'), may hold values from -128 to 127
- up_scale: float32 [64, 5120], P('seq', 'inner'), may hold values from 0.00036336103 to 0.0015093458
- down_codes: bfloat16 [64, 5120, 1280], P('seq', 'inner'), may hold values from -128 to 127
- down_scale: float32 [64, 1280], P('seq'), may hold values from 0.00018866823 to 0.0007546729
Outputs:
- mixed_out: bfloat16 [196608, 1280], P(('seq', 'inner'))
All inputs are finite; a program needn't handle non-finite values.
Results may differ from a plain program's by a relative error of at most 0.0066.
Values may be sent and summed in bfloat16 or wider, within the bound.
No kernel may reach another device: no remote copies, remote signals or barrier semaphores. Data moves between devices by JAX's collectives and lax.ppermute only.
A program may use at most 64 MiB of HBM per device.

v0:
```python
import jax
import jax.numpy as jnp
from jax import lax
from jax.sharding import PartitionSpec as P


def per_device(tokens, slot_embed, up_codes, up_scale, down_codes, down_scale):
    model_width = tokens.shape[1]
    logits = jnp.dot(tokens, slot_embed, preferred_element_type=jnp.float32)
    local_max = jnp.max(logits, axis=0)
    slot_max = lax.pmax(local_max, ("seq", "inner"))
    shifted = jnp.exp(logits - slot_max)
    slot_total = lax.psum(jnp.sum(shifted, axis=0), ("seq", "inner"))
    dispatch = shifted.astype(jnp.bfloat16)
    row_max = jnp.max(logits, axis=1, keepdims=True)
    row_exp = jnp.exp(logits - row_max)
    combine = (row_exp / jnp.sum(row_exp, axis=1, keepdims=True)).astype(jnp.bfloat16)
    seq_count = lax.axis_size("seq")
    slot_count = slot_embed.shape[1]
    own_count = slot_count // seq_count
    experts_here = up_codes.shape[0]
    own_first = lax.axis_index("seq") * own_count
    own_total = lax.dynamic_slice_in_dim(slot_total, own_first, own_count, 0)
    selected = dispatch
    seq_share = lax.psum_scatter(
        lax.dot_general(
            selected, tokens, (((0,), (0,)), ((), ())), preferred_element_type=jnp.float32
        ),
        "seq",
        scatter_dimension=0,
        tiled=True,
    )
    pooled = lax.psum(seq_share, "inner")
    slot_inputs = (pooled / own_total[:, None]).astype(jnp.bfloat16)
    grouped = slot_inputs.reshape(experts_here, -1, model_width)
    raised = jnp.einsum("esd,edf->esf", grouped, up_codes, preferred_element_type=jnp.float32)
    hidden = jax.nn.gelu(raised * up_scale[:, None, :], approximate=False).astype(jnp.bfloat16)
    partial_out = jnp.einsum("esf,efd->esd", hidden, down_codes, preferred_element_type=jnp.float32)
    expert_sum = lax.psum(partial_out, "inner")
    slot_outputs = (
        (expert_sum * down_scale[:, None, :]).astype(jnp.bfloat16).reshape(-1, model_width)
    )
    selected = combine
    mixed_out = jnp.dot(
        selected,
        lax.all_gather(slot_outputs, "seq", axis=0, tiled=True),
        preferred_element_type=jnp.float32,
    )
    return mixed_out.astype(jnp.bfloat16)


def solution(mesh):
    in_specs = (
        P(("seq", "inner"), None),
        P(),
        P("seq", None, "inner"),
        P("seq", "inner"),
        P("seq", "inner", None),
        P("seq", None),
    )
    out_specs = P(("seq", "inner"), None)
    return jax.shard_map(
        per_device, mesh=mesh, in_specs=in_specs, out_specs=out_specs, check_vma=False
    )
```

profile of v0, /device:TPU:1, one launch (start us, length us, event | category | flops | bytes accessed | tf_op | source)
XLA Modules:
  0.0 824.5 jit_solution(1229056875165322808)
XLA Ops:
  6.5 0.0 copy-start
  6.5 0.0 copy-start.1
  6.5 0.0 reduce-scatter.2.cloned.1.call-start
  6.5 2.5 fusion.91
  9.1 111.1 %pmax.7 = f32[512]{0:T(512)S(1)} all-reduce(f32[512]{0:T(512)S(1)} %get-tuple-element.8), channel_id=1, replica_groups=mesh['seq'=64,'inner'=8] {'seq','inner'}, use_global_device_ids=true, to_apply=%region_3.0 | all-reduce | flops 512 | bytes 4096 | tf_op jit(solution)/shard_map/pmax | solution.py:11
  120.1 0.0 copy-done.1
  120.1 2.4 fusion.10
  122.5 0.0 copy-start.3
  122.5 0.0 copy-start.2
  122.5 0.0 reduce-scatter.2.cloned.1.call-update
  122.6 0.0 all-gather.3.cloned.1.call-start
  122.6 0.6 copy-done.3
  123.2 0.0 copy-done.2
  123.3 0.3 fusion.7
  123.6 98.3 %psum.22 = f32[512]{0:T(512)S(1)} all-reduce(f32[512]{0:T(512)S(1)} %get-tuple-element.6), channel_id=1, replica_groups=mesh['seq'=64,'inner'=8] {'seq','inner'}, use_global_device_ids=true, to_apply=%region_7.0 | all-reduce | flops 512 | bytes 4096 | tf_op jit(solution)/shard_map/psum | solution.py:13
  221.9 0.1 dynamic_slice.3
  222.0 324.7 %reduce-scatter.2.cloned.1.call-done = f32[8,1280]{1,0:T(8,128)} async-done(((f32[512,1280]{1,0:T(8,128)}), f32[8,1280]{1,0:T(8,128)}) %reduce-scatter.2.cloned.1.call-update) | async-done | bytes 40976 | tf_op jit(solution)/shard_map/reduce_scatter | solution.py:25
  546.7 71.5 %psum.21 = f32[8,1280]{1,0:T(8,128)S(1)} all-reduce(f32[8,1280]{1,0:T(8,128)} %reduce-scatter.2.cloned.1.call-done), channel_id=1, replica_groups=mesh['seq'=64,'inner'=8] {'inner'}, use_global_device_ids=true, to_apply=%region_5.0 | all-reduce | flops 10240 | bytes 81920 | tf_op jit(solution)/shard_map/psum | solution.py:33
  618.2 0.0 copy-done
  618.2 2.1 convolution_bitcast_fusion
  620.3 59.2 %psum.23 = f32[1,8,1280]{2,1,0:T(8,128)S(1)} all-reduce(f32[1,8,1280]{2,1,0:T(8,128)S(1)} %convolution_bitcast_fusion), channel_id=1, replica_groups=mesh['seq'=64,'inner'=8] {'inner'}, use_global_device_ids=true, to_apply=%region_8.0 | all-reduce | flops 10240 | bytes 81920 | tf_op jit(solution)/shard_map/psum | solution.py:39
  679.5 0.6 multiply_convert_fusion
  680.2 0.0 all-gather.3.cloned.1.call-update
  680.2 134.5 %all-gather.3.cloned.1.call-done = bf16[1,512,1280]{2,1,0:T(8,128)(2,1)} async-done(((bf16[1,8,1280]{2,1,0:T(8,128)(2,1)}), bf16[1,512,1280]{2,1,0:T(8,128)(2,1)}) %all-gather.3.cloned.1.call-update) | async-done | bytes 1310736 | tf_op jit(solution)/shard_map/all_gather | solution.py:46
  814.6 3.0 convolution_convert_fusion
  (2 shorter events, 0.0 us)
Async XLA Ops:
  6.5 611.6 %copy-start = (bf16[1,640,1280]{2,1,0:T(8,128)(2,1)S(1)}, bf16[1,640,1280]{2,1,0:T(8,128)(2,1)}, u32[]{:S(2)}) copy-start(bf16[1,640,1280]{2,1,0:T(8,128)(2,1)} %param.10) | copy-start | bytes 4915204
  6.5 113.6 %copy-start.1 = (bf16[384,1280]{1,0:T(8,128)(2,1)S(1)}, bf16[384,1280]{1,0:T(8,128)(2,1)}, u32[]{:S(2)}) copy-start(bf16[384,1280]{1,0:T(8,128)(2,1)} %param.6) | copy-start | bytes 2949124
  6.5 540.2 %reduce-scatter.2.cloned.1.call-start = ((), (), s32[]{:S(2)}) async-start(), calls=%async_computation.1 | async-start | bytes 2662400 | tf_op jit(solution)/shard_map/reduce_scatter | solution.py:25
  122.5 0.7 copy-start.3
  122.5 0.7 copy-start.2
  122.6 692.1 %all-gather.3.cloned.1.call-start = ((), (), s32[]{:S(2)}) async-start(), calls=%async_computation.2 | async-start | bytes 1331200 | tf_op jit(solution)/shard_map/all_gather | solution.py:46
Sparse Core Ops, SparseCore 0:
  122.7 423.9 reduce-scatter.1
  680.3 134.2 all-gather.2
where the time goes:
time: 825 us
  waiting for transfers between devices  459 us (56%)
  blocking collectives  340 us (41%)
  between operations  13.4 us (2%)
  matrix products  10.1 us (1%)
    reduce_scatter x1, waiting for transfers between devices, per_device(): lax.psum_scatter(lax.dot_general(selected, tokens, (((0,), (0,)), ((), ()...  325 us
    all_gather x1, waiting for transfers between devices, per_device(): lax.all_gather(slot_outputs, 'seq', axis=0, tiled=True)  134 us
    pmax x1, blocking collectives, per_device(): slot_max = lax.pmax(local_max, ('seq', 'inner'))  111 us
    psum x1, blocking collectives, per_device(): slot_total = lax.psum(jnp.sum(shifted, axis=0), ('seq', 'inner'))  98.3 us
    psum x1, blocking collectives, per_device(): pooled = lax.psum(seq_share, 'inner')  71.5 us
    psum x1, blocking collectives, per_device(): expert_sum = lax.psum(partial_out, 'inner')  59.2 us
  transfers between devices with their start and end apart: 2, of which 2 were waited for; matrix products, arithmetic and copies ran while one was open for 0% of the time, Pallas kernels for 0%

commit v1 on v0

v1 whole, which is shorter than its diff:
```python
import jax
import jax.numpy as jnp
from jax import lax
from jax.sharding import Mesh, PartitionSpec as P

BF = jnp.bfloat16
F32 = jnp.float32
ZL, X, C, Y, ZH = 8, 4, 2, 4, 2
SEQ = ("zl", "x", "c")
INNER = ("y", "zh")
PAD = 128


def split_pair(v):
    hi = lax.reduce_precision(v, 8, 7)
    lo = lax.reduce_precision(v - hi, 8, 7)
    return hi, lo


def pack(acc, m_hi, m_lo, total):
    t_hi, t_lo = split_pair(total)
    tail = jnp.stack([m_hi, m_lo, t_hi, t_lo], axis=-1).astype(BF)
    tail = jnp.pad(tail, [(0, 0)] * (tail.ndim - 1) + [(0, PAD - 4)])
    return jnp.concatenate([acc.astype(BF), tail], axis=-1)


def merge(parts, width):
    f = parts[:, :, width : width + 4].astype(F32)
    shift = f[:, :, 0] + f[:, :, 1]
    total = f[:, :, 2] + f[:, :, 3]
    top = jnp.max(shift, axis=0)
    weight = jnp.exp(shift - top[None])
    acc = jnp.sum(parts[:, :, :width].astype(F32) * weight[:, :, None], axis=0)
    return acc, top, jnp.sum(total * weight, axis=0)


def per_device(tokens, slot_embed, up_codes, up_scale, down_codes, down_scale):
    width = tokens.shape[1]
    slots = slot_embed.shape[1]
    core = lax.axis_index("c")
    n = lax.broadcasted_iota(jnp.int32, (slots, slots), 1)
    k = lax.broadcasted_iota(jnp.int32, (slots, slots), 0)
    place = (
        ((n >> 1) & 7) * 64
        + ((n >> 6) & 3) * 16
        + (((n >> 8) & 1) ^ core) * 8
        + ((n >> 4) & 3) * 2
        + (n & 1)
    )
    order = (k == place).astype(BF)
    embed = jnp.dot(slot_embed, order, preferred_element_type=F32).astype(BF)

    logits = jnp.dot(tokens, embed, preferred_element_type=F32)
    m_hi, m_lo = split_pair(jnp.max(logits, axis=0))
    shift = m_hi + m_lo
    shifted = jnp.exp(logits - shift)
    total = jnp.sum(shifted, axis=0)
    dispatch = shifted.astype(BF)
    row_max = jnp.max(logits, axis=1, keepdims=True)
    row_exp = jnp.exp(logits - row_max)
    combine = (row_exp / jnp.sum(row_exp, axis=1, keepdims=True)).astype(BF)

    def pooled(lo, hi):
        acc = lax.dot_general(
            dispatch[:, lo:hi], tokens, (((0,), (0,)), ((), ())), preferred_element_type=F32
        )
        return pack(acc, m_hi[lo:hi], m_lo[lo:hi], total[lo:hi])

    half = slots // 2
    swap = [(0, 1), (1, 0)]
    with jax.named_scope("sum_core"):
        other = lax.ppermute(pooled(half, slots), "c", swap)
        own = pooled(0, half)
        acc, top, total = merge(jnp.stack([own, other]), width)
        part = pack(acc, *split_pair(top), total)
    with jax.named_scope("sum_xy"):
        got = lax.all_to_all(part, ("x", "y"), 0, 0, tiled=True)
        acc, top, total = merge(got.reshape(X * Y, ZL * 2, width + PAD), width)
        part = pack(acc, *split_pair(top), total)
    with jax.named_scope("sum_z"):
        part = jnp.broadcast_to(part.reshape(ZL, 1, 2, width + PAD), (ZL, ZH, 2, width + PAD))
        got = lax.all_to_all(part.reshape(ZL * ZH, 2, width + PAD), ("zl", "zh"), 0, 0, tiled=True)
        acc, top, total = merge(got, width)
        slot_pair = (acc / total[:, None]).astype(BF)
    with jax.named_scope("gather_y"):
        spread = jnp.broadcast_to(slot_pair[None], (Y, 2, width))
        slot_inputs = lax.all_to_all(spread, "y", 0, 0, tiled=True).reshape(Y * 2, width)

    raised = jnp.dot(slot_inputs, up_codes[0], preferred_element_type=F32)
    hidden = jax.nn.gelu(raised * up_scale, approximate=False).astype(BF)
    partial_out = jnp.dot(hidden, down_codes[0], preferred_element_type=F32) * down_scale
    with jax.named_scope("out_y"):
        got = lax.all_to_all(partial_out.reshape(Y, 2, width), "y", 0, 0, tiled=True)
        pair_out = jnp.sum(got, axis=0).astype(BF)
    with jax.named_scope("out_z"):
        spread = jnp.broadcast_to(pair_out[None], (ZL * ZH, 2, width))
        got = lax.all_to_all(spread, ("zl", "zh"), 0, 0, tiled=True)
        got = got.reshape(ZL, ZH, 2, width).astype(F32)
        rows = jnp.sum(got, axis=1).astype(BF).reshape(ZL * 2, width)
    with jax.named_scope("out_xy"):
        spread = jnp.broadcast_to(rows[None], (X * Y, ZL * 2, width))
        own = lax.all_to_all(spread, ("x", "y"), 0, 0, tiled=True).reshape(half, width)
    with jax.named_scope("out_core"):
        other = lax.ppermute(own, "c", swap)
    with jax.named_scope("mix"):
        mixed = jnp.dot(combine[:, :half], own, preferred_element_type=F32)
        mixed += jnp.dot(combine[:, half:], other, preferred_element_type=F32)
    return mixed.astype(BF)


def solution(mesh):
    fine = Mesh(mesh.devices.reshape(ZL, X, C, Y, ZH), SEQ + INNER)
    in_specs = (
        P(SEQ + INNER, None),
        P(),
        P(SEQ, None, INNER),
        P(SEQ, INNER),
        P(SEQ, INNER, None),
        P(SEQ, None),
    )
    out_specs = P(SEQ + INNER, None)
    return jax.shard_map(
        per_device, mesh=fine, in_specs=in_specs, out_specs=out_specs, check_vma=False
    )
```

time: 825 us -> 123 us (0.15)
  waiting for transfers between devices: 459 us -> 5.64 us
  blocking collectives: 340 us -> 74.8 us
  starting transfers between devices: 0.04 us -> 22 us
  between operations: 13.4 us -> 0.36 us
    reduce_scatter x1 -> x0, waiting for transfers between devices: 325 us -> none  [per_device(): lax.psum_scatter(lax.dot_general(selected, tokens, (((0,), (0,)), ((), ()...]
    psum x3 -> x0, blocking collectives: 229 us -> none  [the longest x1 98.3 us: per_device(): slot_total = lax.psum(jnp.sum(shifted, axis=0), ('seq', 'inner'))]
    all_gather x1 -> x0, waiting for transfers between devices: 134 us -> none  [per_device(): lax.all_gather(slot_outputs, 'seq', axis=0, tiled=True)]
    pmax x1 -> x0, blocking collectives: 111 us -> none  [per_device(): slot_max = lax.pmax(local_max, ('seq', 'inner'))]
    all_to_all x0 -> x5, blocking collectives: none -> 74.8 us  [the longest x1 25.4 us: per_device(): lax.all_to_all(part.reshape(ZL * ZH, 2, width + PAD), ('zl', 'zh'), 0, 0,...]
    ppermute x0 -> x2, starting transfers between devices: none -> 18.7 us  [the longest x1 9.92 us: per_device(): other = lax.ppermute(own, 'c', swap)]
  transfers between devices with their start and end apart: 2 -> 3, of which waited for: 2 -> 3; matrix products, arithmetic and copies ran while one was open for 0% -> 2% of each run, Pallas kernels for 0% -> 0%
where the time goes in v1:
time: 123 us; the launch traced here: 122 us
  blocking collectives  74.8 us (61%)
  starting transfers between devices  22 us (18%)
  matrix products  10.2 us (8%)
  other arithmetic  6.88 us (6%)
  waiting for transfers between devices  5.64 us (5%)
  local copies, waits for them, and re-layouts  2.1 us (2%)
    all_to_all x1, blocking collectives, per_device(): lax.all_to_all(part.reshape(ZL * ZH, 2, width + PAD), ('zl', 'zh'), 0, 0,...  25.4 us
    all_to_all x1, blocking collectives, per_device(): got = lax.all_to_all(part, ('x', 'y'), 0, 0, tiled=True)  15.4 us
    all_to_all x1, blocking collectives, per_device(): got = lax.all_to_all(spread, ('zl', 'zh'), 0, 0, tiled=True)  14.7 us
    all_to_all x1, blocking collectives, per_device(): lax.all_to_all(spread, ('x', 'y'), 0, 0, tiled=True).reshape(half, width)  12.6 us
    ppermute x1, starting transfers between devices, per_device(): other = lax.ppermute(own, 'c', swap)  9.92 us
    ppermute x1, starting transfers between devices, per_device(): other = lax.ppermute(pooled(half, slots), 'c', swap)  8.78 us
    all_to_all x1, blocking collectives, per_device(): lax.all_to_all(partial_out.reshape(Y, 2, width), 'y', 0, 0, tiled=True)  6.7 us
    all_to_all x1, waiting for transfers between devices, per_device(): lax.all_to_all(spread, 'y', 0, 0, tiled=True).reshape(Y * 2, width)  4.13 us
  transfers between devices with their start and end apart: 3, of which 3 were waited for; matrix products, arithmetic and copies ran while one was open for 2% of the time, Pallas kernels for 0%

profile of v1, /device:TPU:1, one launch (start us, length us, event | category | flops | bytes accessed | tf_op | source)
XLA Modules:
  0.0 122.0 jit_solution(4719343014154626004)
XLA Ops:
  0.0 3.4 %fusion.142 = (f32[384]{0:T(512)S(1)}, f32[512]{0:T(512)S(1)}, f32[512,384]{1,0:T(8,128)S(1)}) fusion(bf16[384,1280]{1,0:T(8,128)(2,1)} %param.6, bf16[1280,512]{1,0:T(8,128)(2,1)} %param.7, s32[512]{0:T(512)S(1)} %fusion.88), kind=kOutput, calls=%fused_computation.195 | convolution fusion | flops 1175977088 | bytes 3085824 | tf_op jit(solution)/shard_map/dot_general | solution.py:53
  3.5 1.0 fusion.17
  4.5 0.1 copy.87
  4.6 1.4 %convolution_convert_fusion.1 = bf16[256,1280]{1,0:T(8,128)(2,1)S(1)} fusion(bf16[384,1280]{1,0:T(8,128)(2,1)S(1)} %copy-done.1, bf16[384,512]{0,1:T(8,128)(2,1)} %get-tuple-element.15), kind=kOutput, calls=%fused_computation.4 | convolution fusion | flops 251985920 | bytes 1835008 | tf_op jit(solution)/shard_map/sum_core/dot_general | solution.py:64
  6.1 0.9 fusion.15
  7.0 8.8 %collective-permute-start = (bf16[256,1408]{1,0:T(8,128)(2,1)}, bf16[256,1408]{1,0:T(8,128)(2,1)}, u32[]{:S(2)}, u32[]{:S(2)}) collective-permute-start(bf16[256,1408]{1,0:T(8,128)(2,1)} %fusion.15), channel_id=1, source_target_pairs={{0,8},{8,0},{1,9},{9,1},{2,10},{10,2},{3,11},{11,3},{4,12},{12,4},... | collective-permute-start | bytes 2162696 | tf_op jit(solution)/shard_map/sum_core/ppermute | solution.py:72
  15.8 0.1 copy.86
  16.0 1.4 %convolution_convert_fusion.2 = bf16[256,1280]{1,0:T(8,128)(2,1)S(1)} fusion(bf16[384,1280]{1,0:T(8,128)(2,1)S(1)} %copy-done.1, bf16[384,512]{0,1:T(8,128)(2,1)} %get-tuple-element.15), kind=kOutput, calls=%fused_computation.5 | convolution fusion | flops 251985920 | bytes 1835008 | tf_op jit(solution)/shard_map/sum_core/dot_general | solution.py:64
  17.4 0.1 fusion.14
  17.5 0.4 collective-permute-done
  17.9 0.9 fusion.33
  18.8 0.2 fusion.141
  19.0 0.6 exponential_reduce_fusion
  19.6 1.4 %multiply_reduce_fusion = bf16[256,1280]{1,0:T(8,128)(2,1)S(1)} fusion(bf16[1,256,1408]{2,1,0:T(8,128)(2,1)S(1)} %fusion.14, bf16[1,256,1408]{2,1,0:T(8,128)(2,1)} %bitcast.3, f32[2,256]{1,0:T(2,128)S(1)} %get-tuple-element.9), kind=kLoop, calls=%fused_computation.3 | loop fusion | flops 3604480 | bytes 2099200 | tf_op jit(solution)/shard_map/sum_core/reduce_sum | solution.py:33
  21.1 0.1 copy.99
  21.2 0.1 fusion.16
  21.3 15.4 %all_to_all.34 = bf16[16,16,1408]{2,1,0:T(8,128)(2,1)S(1)} all-to-all(bf16[16,16,1408]{2,1,0:T(8,128)(2,1)S(1)} %bitcast.53), channel_id=1, replica_groups=mesh['zl'=8,'x'=4,'c'=2,'y'=4,'zh'=2] {'x','y'}, dimensions={0} | all-to-all | bytes 1441792 | tf_op jit(solution)/shard_map/sum_xy/all_to_all | solution.py:77
  36.7 0.2 fusion.139
  36.9 0.3 exponential_reduce_fusion.1
  37.3 0.1 copy.100
  37.4 0.2 multiply_reduce_fusion.1
  37.6 0.0 copy-start.3
  37.6 0.0 copy-start.2
  37.7 0.1 broadcast_in_dim.13
  37.7 25.4 %all_to_all.35 = bf16[16,2,1408]{2,1,0:T(2,128)(2,1)S(1)} all-to-all(bf16[16,2,1408]{2,1,0:T(2,128)(2,1)S(1)} %bitcast.56), channel_id=1, replica_groups=mesh['zl'=8,'x'=4,'c'=2,'y'=4,'zh'=2] {'zl','zh'}, dimensions={0} | all-to-all | bytes 180224 | tf_op jit(solution)/shard_map/sum_z/all_to_all | solution.py:82
  63.1 0.1 copy.98
  63.2 0.1 fusion.137
  63.3 0.2 fusion.101
  63.5 0.1 exponential_bitcast_fusion
  63.6 0.1 copy.91
  63.7 0.2 multiply_reduce_fusion.2
  63.9 0.3 copy.96
  64.1 0.1 divide_convert_fusion.1
  64.2 0.2 copy.93
  64.4 0.6 broadcast_in_dim.14
  65.0 3.3 %all-to-all-start.2 = ((bf16[4,2,1280]{2,1,0:T(2,128)(2,1)}), bf16[4,2,1280]{2,1,0:T(2,128)(2,1)S(1)}, u32[]{:S(2)}, u32[]{:S(2)}) async-start(bf16[4,2,1280]{2,1,0:T(2,128)(2,1)} %broadcast_in_dim.14), calls=%async_computation.2 | async-start | bytes 40960 | tf_op jit(solution)/shard_map/gather_y/all_to_all | solution.py:87
  68.3 0.0 copy-done.3
  68.3 4.1 %all-to-all-done.2 = bf16[4,2,1280]{2,1,0:T(2,128)(2,1)S(1)} async-done(((bf16[4,2,1280]{2,1,0:T(2,128)(2,1)}), bf16[4,2,1280]{2,1,0:T(2,128)(2,1)S(1)}, u32[]{:S(2)}, u32[]{:S(2)}) %all-to-all-start.2) | async-done | bytes 20512 | tf_op jit(solution)/shard_map/gather_y/all_to_all | solution.py:87
  72.5 2.1 %convolution_multiply_fusion = f32[8,1280]{1,0:T(8,128)S(1)} fusion(bf16[1,640,1280]{2,1,0:T(8,128)(2,1)S(1)} %copy-done, f32[1280]{0:T(1024)S(1)} %reduce.15, bf16[8,1280]{1,0:T(8,128)(2,1)S(1)} %reshape.142, bf16[1,1280,640]{2,1,0:T(8,128)(2,1)} %param.8, f32[640]{0:T(1024)S(1)} %reduce.14), kind=kOutput, calls=%fused_computation.6 | convolution fusion | flops 26562560 | bytes 3345920 | tf_op jit(solution)/shard_map/dot_general | solution.py:91
  74.6 6.7 %all_to_all.36 = f32[4,2,1280]{2,1,0:T(2,128)S(1)} all-to-all(f32[4,2,1280]{2,1,0:T(2,128)S(1)} %reshape.143), channel_id=1, replica_groups=mesh['zl'=8,'x'=4,'c'=2,'y'=4,'zh'=2] {'y'}, dimensions={0} | all-to-all | bytes 81920 | tf_op jit(solution)/shard_map/out_y/all_to_all | solution.py:93
  81.4 14.7 %all_to_all.37 = bf16[16,2,1280]{2,1,0:T(2,128)(2,1)S(1)} all-to-all(bf16[16,2,1280]{2,1,0:T(2,128)(2,1)S(1)} %broadcast_in_dim.15), channel_id=1, replica_groups=mesh['zl'=8,'x'=4,'c'=2,'y'=4,'zh'=2] {'zl','zh'}, dimensions={0} | all-to-all | bytes 163840 | tf_op jit(solution)/shard_map/out_z/all_to_all | solution.py:97
  96.1 0.1 bitcast_reduce_fusion
  96.3 12.6 %all_to_all.38 = bf16[16,16,1280]{2,1,0:T(8,128)(2,1)S(1)} all-to-all(bf16[16,16,1280]{2,1,0:T(8,128)(2,1)S(1)} %broadcast_in_dim.17), channel_id=1, replica_groups=mesh['zl'=8,'x'=4,'c'=2,'y'=4,'zh'=2] {'x','y'}, dimensions={0} | all-to-all | bytes 1310720 | tf_op jit(solution)/shard_map/out_xy/all_to_all | solution.py:102
  108.9 9.9 %collective-permute-start.1 = (bf16[256,1280]{1,0:T(8,128)(2,1)S(1)}, bf16[256,1280]{1,0:T(8,128)(2,1)S(1)}, u32[]{:S(2)}, u32[]{:S(2)}) collective-permute-start(bf16[256,1280]{1,0:T(8,128)(2,1)S(1)} %bitcast.54), channel_id=1, source_target_pairs={{0,8},{8,0},{1,9},{9,1},{2,10},{10,2},{3,11},{11,3},{4,12},{12,4},... | collective-permute-start | bytes 1966088 | tf_op jit(solution)/shard_map/out_core/ppermute | solution.py:104
  118.8 0.1 fusion.25
  119.0 0.5 fusion.30
  119.5 1.1 collective-permute-done.1
  120.5 1.4 %fusion = bf16[384,1280]{1,0:T(8,128)(2,1)} fusion(f32[384,1280]{1,0:T(8,128)S(1)} %fusion.30, bf16[256,1280]{1,0:T(8,128)(2,1)S(1)} %collective-permute-done.1, bf16[384,512]{0,1:T(8,128)(2,1)S(1)} %fusion.25), kind=kOutput, calls=%fused_computation.2 | convolution fusion | flops 252641280 | bytes 3801088 | tf_op jit(solution)/shard_map/mix/dot_general | solution.py:107
  (40 shorter events, 0.5 us)
Async XLA Ops:
  0.0 72.5 %copy-start = (bf16[1,640,1280]{2,1,0:T(8,128)(2,1)S(1)}, bf16[1,640,1280]{2,1,0:T(8,128)(2,1)}, u32[]{:S(2)}) copy-start(bf16[1,640,1280]{2,1,0:T(8,128)(2,1)} %param.10) | copy-start | bytes 4915204
  3.4 1.2 %copy-start.1 = (bf16[384,1280]{1,0:T(8,128)(2,1)S(1)}, bf16[384,1280]{1,0:T(8,128)(2,1)}, u32[]{:S(2)}) copy-start(bf16[384,1280]{1,0:T(8,128)(2,1)} %param.6) | copy-start | bytes 2949124
  7.0 10.9 %collective-permute-start = (bf16[256,1408]{1,0:T(8,128)(2,1)}, bf16[256,1408]{1,0:T(8,128)(2,1)}, u32[]{:S(2)}, u32[]{:S(2)}) collective-permute-start(bf16[256,1408]{1,0:T(8,128)(2,1)} %fusion.15), channel_id=1, source_target_pairs={{0,8},{8,0},{1,9},{9,1},{2,10},{10,2},{3,11},{11,3},{4,12},{12,4},... | collective-permute-start | bytes 2162696 | tf_op jit(solution)/shard_map/sum_core/ppermute | solution.py:72
  37.6 30.7 %copy-start.3 = (f32[1,640]{1,0:T(1,128)S(1)}, f32[1,640]{1,0:T(1,128)}, u32[]{:S(2)}) copy-start(f32[1,640]{1,0:T(1,128)} %param.9) | copy-start | bytes 7684
  37.6 30.7 %copy-start.2 = (f32[1,1280]{1,0:T(1,128)S(1)}, f32[1,1280]{1,0:T(1,128)}, u32[]{:S(2)}) copy-start(f32[1,1280]{1,0:T(1,128)} %param.11) | copy-start | bytes 15364
  65.0 7.5 %all-to-all-start.2 = ((bf16[4,2,1280]{2,1,0:T(2,128)(2,1)}), bf16[4,2,1280]{2,1,0:T(2,128)(2,1)S(1)}, u32[]{:S(2)}, u32[]{:S(2)}) async-start(bf16[4,2,1280]{2,1,0:T(2,128)(2,1)} %broadcast_in_dim.14), calls=%async_computation.2 | async-start | bytes 40960 | tf_op jit(solution)/shard_map/gather_y/all_to_all | solution.py:87
  108.9 11.6 %collective-permute-start.1 = (bf16[256,1280]{1,0:T(8,128)(2,1)S(1)}, bf16[256,1280]{1,0:T(8,128)(2,1)S(1)}, u32[]{:S(2)}, u32[]{:S(2)}) collective-permute-start(bf16[256,1280]{1,0:T(8,128)(2,1)S(1)} %bitcast.54), channel_id=1, source_target_pairs={{0,8},{8,0},{1,9},{9,1},{2,10},{10,2},{3,11},{11,3},{4,12},{12,4},... | collective-permute-start | bytes 1966088 | tf_op jit(solution)/shard_map/out_core/ppermute | solution.py:104

commit v2 on v1

v2 whole, which is shorter than its diff:
```python
import jax
import jax.numpy as jnp
from jax import lax
from jax.experimental import pallas as pl
from jax.experimental.pallas import tpu as pltpu
from jax.sharding import Mesh, PartitionSpec as P

BF = jnp.bfloat16
F32 = jnp.float32
ZL, X, C, Y, ZH = 8, 4, 2, 4, 2
SEQ = ("zl", "x", "c")
INNER = ("y", "zh")
TAIL = 128
NT = (((1,), (1,)), ((), ()))


def split_pair(v):
    hi = lax.reduce_precision(v, 8, 7)
    lo = lax.reduce_precision(v - hi, 8, 7)
    return hi, lo


def slot_order(core, slots):
    n = lax.broadcasted_iota(jnp.int32, (slots, 1), 0)
    k = lax.broadcasted_iota(jnp.int32, (slots, slots), 1)
    place = (
        ((n >> 1) & 7) * 64
        + ((n >> 6) & 3) * 16
        + (((n >> 8) & 1) ^ core) * 8
        + ((n >> 4) & 3) * 2
        + (n & 1)
    )
    return jnp.where(k == place, 1.0, 0.0).astype(BF)


def tail_lanes(top, total):
    lane = lax.broadcasted_iota(jnp.int32, (top.shape[0], TAIL), 1)
    m_hi, m_lo = split_pair(top)
    t_hi, t_lo = split_pair(total)
    tail = jnp.where(lane == 0, m_hi, jnp.where(lane == 1, m_lo, 0.0))
    return jnp.where(lane == 2, t_hi, jnp.where(lane == 3, t_lo, tail))


def read_tail(tail):
    return tail[:, 0:1] + tail[:, 1:2], tail[:, 2:3] + tail[:, 3:4]


def front_kernel(core_ref, tok_ref, emb_ref, send_ref, own_ref, tail_ref, logits_ref):
    slots = emb_ref.shape[1]
    half = slots // 2
    width = tok_ref.shape[1]
    tokens = tok_ref[...]
    logits = jnp.dot(tokens, emb_ref[...], preferred_element_type=F32)
    logits_ref[...] = logits
    m_hi, m_lo = split_pair(jnp.max(logits, axis=0, keepdims=True))
    shifted = jnp.exp(logits - (m_hi + m_lo))
    t_hi, t_lo = split_pair(jnp.sum(shifted, axis=0, keepdims=True))
    row = lax.broadcasted_iota(jnp.int32, (TAIL, slots), 0)
    stats = jnp.where(row == 0, m_hi, jnp.where(row == 1, m_lo, 0.0))
    stats = jnp.where(row == 2, t_hi, jnp.where(row == 3, t_lo, stats)).astype(BF)
    order = slot_order(core_ref[0], slots)
    weights = lax.dot_general(
        order, shifted.astype(BF), NT, preferred_element_type=F32
    ).astype(BF)
    tail = lax.dot_general(order, stats, NT, preferred_element_type=F32)
    acc = jnp.dot(weights[half:], tokens, preferred_element_type=F32)
    send_ref[:, :width] = acc.astype(BF)
    send_ref[:, width:] = tail[half:].astype(BF)
    own_ref[...] = weights[:half]
    tail_ref[...] = tail[:half]


def own_kernel(core_ref, tok_ref, own_ref, logits_ref, acc_ref, combine_ref):
    acc_ref[...] = jnp.dot(own_ref[...], tok_ref[...], preferred_element_type=F32)
    logits = logits_ref[...]
    row_exp = jnp.exp(logits - jnp.max(logits, axis=1, keepdims=True))
    combine = (row_exp / jnp.sum(row_exp, axis=1, keepdims=True)).astype(BF)
    order = slot_order(core_ref[0], logits.shape[1])
    combine_ref[...] = lax.dot_general(combine, order, NT, preferred_element_type=F32).astype(BF)


def core_kernel(acc_ref, tail_ref, got_ref, part_ref):
    width = acc_ref.shape[1]
    shift_a, total_a = read_tail(tail_ref[...])
    shift_b, total_b = read_tail(got_ref[:, width:].astype(F32))
    top = jnp.maximum(shift_a, shift_b)
    weight_a = jnp.exp(shift_a - top)
    weight_b = jnp.exp(shift_b - top)
    acc = acc_ref[...] * weight_a + got_ref[:, :width].astype(F32) * weight_b
    part_ref[:, :width] = acc.astype(BF)
    part_ref[:, width:] = tail_lanes(top, total_a * weight_a + total_b * weight_b).astype(BF)


def plane_kernel(got_ref, part_ref):
    rows = part_ref.shape[0]
    width = part_ref.shape[1] - TAIL
    count = got_ref.shape[0] // rows
    stats = [
        read_tail(got_ref[k * rows : (k + 1) * rows, width:].astype(F32)) for k in range(count)
    ]
    top = stats[0][0]
    for shift, _ in stats[1:]:
        top = jnp.maximum(top, shift)
    acc = jnp.zeros((rows, width), F32)
    total = jnp.zeros((rows, 1), F32)
    for k, (shift, part_total) in enumerate(stats):
        weight = jnp.exp(shift - top)
        acc += got_ref[k * rows : (k + 1) * rows, :width].astype(F32) * weight
        total += part_total * weight
    part_ref[:, :width] = acc.astype(BF)
    part_ref[:, width:] = tail_lanes(top, total).astype(BF)


def line_kernel(got_ref, out_ref):
    width = out_ref.shape[1]
    groups = [slice(8 * g, 8 * g + 8) for g in range(got_ref.shape[0] // 8)]
    stats = []
    for g in groups:
        shift, total = read_tail(got_ref[g, width:].astype(F32))
        stats.append((jnp.broadcast_to(shift, (8, TAIL)), jnp.broadcast_to(total, (8, TAIL))))
    top = stats[0][0]
    for shift, _ in stats[1:]:
        top = jnp.maximum(top, shift)
    for step in (2, 4):
        top = jnp.maximum(top, pltpu.roll(top, step, 0))
    acc = jnp.zeros((8, width), F32)
    total = jnp.zeros((8, TAIL), F32)
    for g, (shift, part_total) in zip(groups, stats):
        weight = jnp.exp(shift - top)
        acc += got_ref[g, :width].astype(F32) * weight[:, 0:1]
        total += part_total * weight
    for step in (2, 4):
        acc += pltpu.roll(acc, step, 0)
        total += pltpu.roll(total, step, 0)
    out_ref[...] = acc / total[:, 0:1]


def call(kernel, out_shape, *args, scalars=0, mib=16, flops=0, moved=0):
    vmem = pl.BlockSpec(memory_space=pltpu.VMEM)
    smem = pl.BlockSpec(memory_space=pltpu.SMEM)
    many = isinstance(out_shape, (list, tuple))
    return pl.pallas_call(
        kernel,
        out_shape=out_shape,
        in_specs=[smem] * scalars + [vmem] * (len(args) - scalars),
        out_specs=[vmem] * len(out_shape) if many else vmem,
        compiler_params=pltpu.CompilerParams(vmem_limit_bytes=mib << 20),
        cost_estimate=pl.CostEstimate(flops=flops, bytes_accessed=moved, transcendentals=0),
    )(*args)


def shape(dims, dtype):
    return jax.ShapeDtypeStruct(dims, dtype)


def per_device(tokens, slot_embed, up_codes, up_scale, down_codes, down_scale):
    count, width = tokens.shape
    slots = slot_embed.shape[1]
    half = slots // 2
    full = width + TAIL
    core = lax.axis_index("c").astype(jnp.int32).reshape(1)
    swap = [(0, 1), (1, 0)]

    with jax.named_scope("front"):
        send, own, tail, logits = call(
            front_kernel,
            (
                shape((half, full), BF),
                shape((half, count), BF),
                shape((half, TAIL), F32),
                shape((count, slots), F32),
            ),
            core,
            tokens,
            slot_embed,
            scalars=1,
            mib=24,
            flops=10**9,
            moved=4 << 20,
        )
    with jax.named_scope("sum_core"):
        other = lax.ppermute(send, "c", swap)
        acc, combine = call(
            own_kernel,
            (shape((half, width), F32), shape((count, slots), BF)),
            core,
            tokens,
            own,
            logits,
            scalars=1,
            mib=24,
            flops=5 * 10**8,
            moved=4 << 20,
        )
        part = call(core_kernel, shape((half, full), BF), acc, tail, other, moved=3 << 20)
    with jax.named_scope("sum_xy"):
        got = lax.all_to_all(part.reshape(X * Y, ZL * 2, full), ("x", "y"), 0, 0, tiled=True)
        part = call(
            plane_kernel, shape((ZL * 2, full), BF), got.reshape(half, full), mib=8, moved=1 << 20
        )
    with jax.named_scope("sum_z"):
        part = jnp.broadcast_to(part.reshape(ZL, 1, 2, full), (ZL, ZH, 2, full))
        got = lax.all_to_all(part.reshape(ZL * ZH, 2, full), ("zl", "zh"), 0, 0, tiled=True)
        pairs = call(
            line_kernel, shape((Y * 2, width), F32), got.reshape(ZL * ZH * 2, full), mib=8
        )
    with jax.named_scope("gather_y"):
        spread = pairs.astype(BF).reshape(Y, 2, width)
        slot_inputs = lax.all_to_all(spread, "y", 0, 0, tiled=True).reshape(Y * 2, width)

    raised = jnp.dot(slot_inputs, up_codes[0], preferred_element_type=F32)
    hidden = jax.nn.gelu(raised * up_scale, approximate=False).astype(BF)
    partial_out = jnp.dot(hidden, down_codes[0], preferred_element_type=F32) * down_scale
    with jax.named_scope("out_y"):
        got = lax.all_to_all(partial_out.reshape(Y, 2, width), "y", 0, 0, tiled=True)
        pair_out = jnp.sum(got, axis=0).astype(BF)
    with jax.named_scope("out_z"):
        spread = jnp.broadcast_to(pair_out[None], (ZL * ZH, 2, width))
        got = lax.all_to_all(spread, ("zl", "zh"), 0, 0, tiled=True)
        got = got.reshape(ZL, ZH, 2, width).astype(F32)
        rows = jnp.sum(got, axis=1).astype(BF).reshape(ZL * 2, width)
    with jax.named_scope("out_xy"):
        spread = jnp.broadcast_to(rows[None], (X * Y, ZL * 2, width))
        own = lax.all_to_all(spread, ("x", "y"), 0, 0, tiled=True).reshape(half, width)
    with jax.named_scope("out_core"):
        other = lax.ppermute(own, "c", swap)
    with jax.named_scope("mix"):
        mixed = jnp.dot(combine[:, :half], own, preferred_element_type=F32)
        mixed += jnp.dot(combine[:, half:], other, preferred_element_type=F32)
    return mixed.astype(BF)


def solution(mesh):
    fine = Mesh(mesh.devices.reshape(ZL, X, C, Y, ZH), SEQ + INNER)
    in_specs = (
        P(SEQ + INNER, None),
        P(),
        P(SEQ, None, INNER),
        P(SEQ, INNER),
        P(SEQ, INNER, None),
        P(SEQ, None),
    )
    out_specs = P(SEQ + INNER, None)
    return jax.shard_map(
        per_device, mesh=fine, in_specs=in_specs, out_specs=out_specs, check_vma=False
    )
```

time: 123 us -> 115 us (0.935)
  other arithmetic: 6.88 us -> 0.16 us
  matrix products: 10.2 us -> 3.91 us
  Pallas kernels: 0 us -> 3.87 us
  local copies, waits for them, and re-layouts: 2.1 us -> 3.56 us
    dot_general x3 -> x0, matrix products: 6.25 us -> none  [the longest x1 3.38 us: per_device(): logits = jnp.dot(tokens, embed, preferred_element_type=F32)]
    pallas_call x0 -> x5, Pallas kernels: none -> 3.87 us  [call(): pl.pallas_call(kernel, out_shape=out_shape, in_specs=[smem] * scalars + [...]
    reduce_sum x7 -> x0, other arithmetic: 3.01 us -> none  [the longest x3 1.79 us: merge(): acc = jnp.sum(parts[:, :, :width].astype(F32) * weight[:, :, None], axis=0)]
    unnamed x12 -> x10, local copies, waits for them, and re-layouts: 0.62 us -> 2.66 us
  transfers between devices with their start and end apart: 3 -> 3, of which waited for: 3 -> 3; matrix products, arithmetic and copies ran while one was open for 2% -> 0% of each run, Pallas kernels for 0% -> 1%
where the time goes in v2:
time: 115 us
  blocking collectives  74.8 us (65%)
  starting transfers between devices  22 us (19%)
  waiting for transfers between devices  6.36 us (6%)
  matrix products  3.91 us (3%)
  Pallas kernels  3.87 us (3%)
  local copies, waits for them, and re-layouts  3.56 us (3%)
    all_to_all x1, blocking collectives, per_device(): lax.all_to_all(part.reshape(ZL * ZH, 2, full), ('zl', 'zh'), 0, 0, tiled=...  25.4 us
    all_to_all x1, blocking collectives, per_device(): lax.all_to_all(part.reshape(X * Y, ZL * 2, full), ('x', 'y'), 0, 0, tiled...  15.4 us
    all_to_all x1, blocking collectives, per_device(): got = lax.all_to_all(spread, ('zl', 'zh'), 0, 0, tiled=True)  14.7 us
    all_to_all x1, blocking collectives, per_device(): lax.all_to_all(spread, ('x', 'y'), 0, 0, tiled=True).reshape(half, width)  12.6 us
    ppermute x1, starting transfers between devices, per_device(): other = lax.ppermute(own, 'c', swap)  9.92 us
    ppermute x1, starting transfers between devices, per_device(): other = lax.ppermute(send, 'c', swap)  8.78 us
    all_to_all x1, blocking collectives, per_device(): lax.all_to_all(partial_out.reshape(Y, 2, width), 'y', 0, 0, tiled=True)  6.7 us
    all_to_all x1, waiting for transfers between devices, per_device(): lax.all_to_all(spread, 'y', 0, 0, tiled=True).reshape(Y * 2, width)  4.13 us
  transfers between devices with their start and end apart: 3, of which 3 were waited for; matrix products, arithmetic and copies ran while one was open for 0% of the time, Pallas kernels for 1%

profile of v2, /device:TPU:1, one launch (start us, length us, event | category | flops | bytes accessed | tf_op | source)
XLA Modules:
  0.0 114.8 jit_solution(13073589772476205143)
XLA Ops:
  0.0 0.0 copy-start
  0.0 0.0 copy-start.1
  0.0 1.3 %copy-done.1 = bf16[384,1280]{1,0:T(8,128)(2,1)S(1)} copy-done((bf16[384,1280]{1,0:T(8,128)(2,1)S(1)}, bf16[384,1280]{1,0:T(8,128)(2,1)}, u32[]{:S(2)}) %copy-start.1) | copy-done | bytes 983064
  1.3 0.0 copy-start.2
  1.3 1.3 %copy-done.2 = bf16[1280,512]{1,0:T(8,128)(2,1)S(1)} copy-done((bf16[1280,512]{1,0:T(8,128)(2,1)S(1)}, bf16[1280,512]{1,0:T(8,128)(2,1)}, u32[]{:S(2)}) %copy-start.2) | copy-done | bytes 1310744
  2.6 1.8 %front.1 = (bf16[256,1408]{1,0:T(8,128)(2,1)S(1)}, bf16[256,384]{1,0:T(8,128)(2,1)S(1)}, f32[256,128]{1,0:T(8,128)S(1)}, f32[384,512]{1,0:T(8,128)S(1)}) custom-call(s32[1]{0:T(128)} %bitcast.core_ref, bf16[384,1280]{1,0:T(8,128)(2,1)S(1)} %copy-done.1, bf16[1280,512]{1,0:T(8,128)(2,1)S(1)} %copy-done.2), custom_call_target="tpu_custom_call" | custom-call | flops 1000000000 | bytes 4194304 | tf_op jit(solution)/shard_map/front/pallas_call | solution.py:142
  4.5 8.8 %collective-permute-start = (bf16[256,1408]{1,0:T(8,128)(2,1)S(1)}, bf16[256,1408]{1,0:T(8,128)(2,1)S(1)}, u32[]{:S(2)}, u32[]{:S(2)}) collective-permute-start(bf16[256,1408]{1,0:T(8,128)(2,1)S(1)} %get-tuple-element.16), channel_id=1, source_target_pairs={{0,8},{8,0},{1,9},{9,1},{2,10},{10,2},{3,11},{11,3},{4,12},{12,4},... | collective-permute-start | bytes 2162696 | tf_op jit(solution)/shard_map/sum_core/ppermute | solution.py:182
  13.3 0.8 sum_core.2
  14.1 1.0 collective-permute-done.got_ref
  15.0 0.6 sum_core.3
  15.7 0.0 copy-start.4
  15.7 0.0 copy-start.3
  15.7 15.4 %all_to_all.30 = bf16[16,16,1408]{2,1,0:T(8,128)(2,1)S(1)} all-to-all(bf16[16,16,1408]{2,1,0:T(8,128)(2,1)S(1)} %bitcast.23), channel_id=1, replica_groups=mesh['zl'=8,'x'=4,'c'=2,'y'=4,'zh'=2] {'x','y'}, dimensions={0} | all-to-all | bytes 1441792 | tf_op jit(solution)/shard_map/sum_xy/all_to_all | solution.py:197
  31.1 0.3 sum_xy.1
  31.5 0.1 broadcast_in_dim.21
  31.6 25.4 %all_to_all.31 = bf16[16,2,1408]{2,1,0:T(2,128)(2,1)S(1)} all-to-all(bf16[16,2,1408]{2,1,0:T(2,128)(2,1)S(1)} %bitcast.26), channel_id=1, replica_groups=mesh['zl'=8,'x'=4,'c'=2,'y'=4,'zh'=2] {'zl','zh'}, dimensions={0} | all-to-all | bytes 180224 | tf_op jit(solution)/shard_map/sum_z/all_to_all | solution.py:203
  57.0 0.2 sum_z.1
  57.2 0.6 reshape.42
  57.9 3.3 %all-to-all-start.2 = ((bf16[4,2,1280]{2,1,0:T(2,128)(2,1)}), bf16[4,2,1280]{2,1,0:T(2,128)(2,1)S(1)}, u32[]{:S(2)}, u32[]{:S(2)}) async-start(bf16[4,2,1280]{2,1,0:T(2,128)(2,1)} %reshape.42), calls=%async_computation.2 | async-start | bytes 40960 | tf_op jit(solution)/shard_map/gather_y/all_to_all | solution.py:209
  61.1 0.0 copy-done.4
  61.2 0.0 copy-done.3
  61.2 4.1 %all-to-all-done.2 = bf16[4,2,1280]{2,1,0:T(2,128)(2,1)S(1)} async-done(((bf16[4,2,1280]{2,1,0:T(2,128)(2,1)}), bf16[4,2,1280]{2,1,0:T(2,128)(2,1)S(1)}, u32[]{:S(2)}, u32[]{:S(2)}) %all-to-all-start.2) | async-done | bytes 20512 | tf_op jit(solution)/shard_map/gather_y/all_to_all | solution.py:209
  65.3 0.0 copy-done
  65.4 2.1 %convolution_multiply_fusion = f32[8,1280]{1,0:T(8,128)S(1)} fusion(bf16[1,640,1280]{2,1,0:T(8,128)(2,1)S(1)} %copy-done, f32[1280]{0:T(1024)S(1)} %reduce.2, bf16[8,1280]{1,0:T(8,128)(2,1)S(1)} %reshape.43, bf16[1,1280,640]{2,1,0:T(8,128)(2,1)} %param.8, f32[640]{0:T(1024)S(1)} %reduce.1), kind=kOutput, calls=%fused_computation.2 | convolution fusion | flops 26562560 | bytes 3345920 | tf_op jit(solution)/shard_map/dot_general | solution.py:213
  67.5 6.7 %all_to_all.32 = f32[4,2,1280]{2,1,0:T(2,128)S(1)} all-to-all(f32[4,2,1280]{2,1,0:T(2,128)S(1)} %reshape.44), channel_id=1, replica_groups=mesh['zl'=8,'x'=4,'c'=2,'y'=4,'zh'=2] {'y'}, dimensions={0} | all-to-all | bytes 81920 | tf_op jit(solution)/shard_map/out_y/all_to_all | solution.py:215
  74.3 14.7 %all_to_all.33 = bf16[16,2,1280]{2,1,0:T(2,128)(2,1)S(1)} all-to-all(bf16[16,2,1280]{2,1,0:T(2,128)(2,1)S(1)} %broadcast_in_dim.22), channel_id=1, replica_groups=mesh['zl'=8,'x'=4,'c'=2,'y'=4,'zh'=2] {'zl','zh'}, dimensions={0} | all-to-all | bytes 163840 | tf_op jit(solution)/shard_map/out_z/all_to_all | solution.py:219
  89.0 0.1 bitcast_reduce_fusion
  89.2 12.6 %all_to_all.34 = bf16[16,16,1280]{2,1,0:T(8,128)(2,1)S(1)} all-to-all(bf16[16,16,1280]{2,1,0:T(8,128)(2,1)S(1)} %broadcast_in_dim.24), channel_id=1, replica_groups=mesh['zl'=8,'x'=4,'c'=2,'y'=4,'zh'=2] {'x','y'}, dimensions={0} | all-to-all | bytes 1310720 | tf_op jit(solution)/shard_map/out_xy/all_to_all | solution.py:224
  101.8 9.9 %collective-permute-start.1 = (bf16[256,1280]{1,0:T(8,128)(2,1)S(1)}, bf16[256,1280]{1,0:T(8,128)(2,1)S(1)}, u32[]{:S(2)}, u32[]{:S(2)}) collective-permute-start(bf16[256,1280]{1,0:T(8,128)(2,1)S(1)} %bitcast.24), channel_id=1, source_target_pairs={{0,8},{8,0},{1,9},{9,1},{2,10},{10,2},{3,11},{11,3},{4,12},{12,4},... | collective-permute-start | bytes 1966088 | tf_op jit(solution)/shard_map/out_core/ppermute | solution.py:226
  111.7 0.4 fusion.8
  112.1 1.3 %collective-permute-done.1 = bf16[256,1280]{1,0:T(8,128)(2,1)S(1)} collective-permute-done((bf16[256,1280]{1,0:T(8,128)(2,1)S(1)}, bf16[256,1280]{1,0:T(8,128)(2,1)S(1)}, u32[]{:S(2)}, u32[]{:S(2)}) %collective-permute-start.1) | collective-permute-done | bytes 655392 | tf_op jit(solution)/shard_map/out_core/ppermute | solution.py:226
  113.4 1.4 %fusion = bf16[384,1280]{1,0:T(8,128)(2,1)} fusion(f32[384,1280]{1,0:T(8,128)S(1)} %fusion.8, bf16[256,1280]{1,0:T(8,128)(2,1)S(1)} %collective-permute-done.1, bf16[384,512]{1,0:T(8,128)(2,1)S(1)} %get-tuple-element.13), kind=kOutput, calls=%fused_computation.1 | convolution fusion | flops 252641280 | bytes 3801088 | tf_op jit(solution)/shard_map/mix/dot_general | solution.py:229
  (11 shorter events, 0.3 us)
Async XLA Ops:
  0.0 65.3 %copy-start = (bf16[1,640,1280]{2,1,0:T(8,128)(2,1)S(1)}, bf16[1,640,1280]{2,1,0:T(8,128)(2,1)}, u32[]{:S(2)}) copy-start(bf16[1,640,1280]{2,1,0:T(8,128)(2,1)} %param.10) | copy-start | bytes 4915204
  0.0 1.3 %copy-start.1 = (bf16[384,1280]{1,0:T(8,128)(2,1)S(1)}, bf16[384,1280]{1,0:T(8,128)(2,1)}, u32[]{:S(2)}) copy-start(bf16[384,1280]{1,0:T(8,128)(2,1)} %tok_ref.3) | copy-start | bytes 2949124
  1.3 1.3 %copy-start.2 = (bf16[1280,512]{1,0:T(8,128)(2,1)S(1)}, bf16[1280,512]{1,0:T(8,128)(2,1)}, u32[]{:S(2)}) copy-start(bf16[1280,512]{1,0:T(8,128)(2,1)} %emb_ref.1) | copy-start | bytes 3932164
  4.5 10.6 %collective-permute-start = (bf16[256,1408]{1,0:T(8,128)(2,1)S(1)}, bf16[256,1408]{1,0:T(8,128)(2,1)S(1)}, u32[]{:S(2)}, u32[]{:S(2)}) collective-permute-start(bf16[256,1408]{1,0:T(8,128)(2,1)S(1)} %get-tuple-element.16), channel_id=1, source_target_pairs={{0,8},{8,0},{1,9},{9,1},{2,10},{10,2},{3,11},{11,3},{4,12},{12,4},... | collective-permute-start | bytes 2162696 | tf_op jit(solution)/shard_map/sum_core/ppermute | solution.py:182
  15.7 45.4 %copy-start.4 = (f32[1,640]{1,0:T(1,128)S(1)}, f32[1,640]{1,0:T(1,128)}, u32[]{:S(2)}) copy-start(f32[1,640]{1,0:T(1,128)} %param.9) | copy-start | bytes 7684
  15.7 45.5 %copy-start.3 = (f32[1,1280]{1,0:T(1,128)S(1)}, f32[1,1280]{1,0:T(1,128)}, u32[]{:S(2)}) copy-start(f32[1,1280]{1,0:T(1,128)} %param.11) | copy-start | bytes 15364
  57.9 7.5 %all-to-all-start.2 = ((bf16[4,2,1280]{2,1,0:T(2,128)(2,1)}), bf16[4,2,1280]{2,1,0:T(2,128)(2,1)S(1)}, u32[]{:S(2)}, u32[]{:S(2)}) async-start(bf16[4,2,1280]{2,1,0:T(2,128)(2,1)} %reshape.42), calls=%async_computation.2 | async-start | bytes 40960 | tf_op jit(solution)/shard_map/gather_y/all_to_all | solution.py:209
  101.8 11.6 %collective-permute-start.1 = (bf16[256,1280]{1,0:T(8,128)(2,1)S(1)}, bf16[256,1280]{1,0:T(8,128)(2,1)S(1)}, u32[]{:S(2)}, u32[]{:S(2)}) collective-permute-start(bf16[256,1280]{1,0:T(8,128)(2,1)S(1)} %bitcast.24), channel_id=1, source_target_pairs={{0,8},{8,0},{1,9},{9,1},{2,10},{10,2},{3,11},{11,3},{4,12},{12,4},... | collective-permute-start | bytes 1966088 | tf_op jit(solution)/shard_map/out_core/ppermute | solution.py:226

commit v3 on v2

--- a/solution.py
+++ b/solution.py
@@ -45,10 +45,27 @@
     return tail[:, 0:1] + tail[:, 1:2], tail[:, 2:3] + tail[:, 3:4]
 
 
-def front_kernel(core_ref, tok_ref, emb_ref, send_ref, own_ref, tail_ref, logits_ref):
+def piece(ref, k, count):
+    rows = ref.shape[0] // count
+    return ref.at[k * rows : (k + 1) * rows]
+
+
+def front_kernel(
+    core_ref, tok_hbm, emb_hbm, send_ref, own_ref, tail_ref, logits_ref, tok_ref, emb_ref, sems
+):
     slots = emb_ref.shape[1]
     half = slots // 2
     width = tok_ref.shape[1]
+    copies = [
+        pltpu.make_async_copy(piece(src, k, 4), piece(dst, k, 4), sems.at[i, k])
+        for i, (src, dst) in enumerate(((emb_hbm, emb_ref), (tok_hbm, tok_ref)))
+        for k in range(4)
+    ]
+    for copy in copies:
+        copy.start()
+    order = slot_order(core_ref[0], slots)
+    for copy in copies:
+        copy.wait()
     tokens = tok_ref[...]
     logits = jnp.dot(tokens, emb_ref[...], preferred_element_type=F32)
     logits_ref[...] = logits
@@ -58,7 +75,6 @@
     row = lax.broadcasted_iota(jnp.int32, (TAIL, slots), 0)
     stats = jnp.where(row == 0, m_hi, jnp.where(row == 1, m_lo, 0.0))
     stats = jnp.where(row == 2, t_hi, jnp.where(row == 3, t_lo, stats)).astype(BF)
-    order = slot_order(core_ref[0], slots)
     weights = lax.dot_general(
         order, shifted.astype(BF), NT, preferred_element_type=F32
     ).astype(BF)
@@ -135,15 +151,54 @@
     out_ref[...] = acc / total[:, 0:1]
 
 
-def call(kernel, out_shape, *args, scalars=0, mib=16, flops=0, moved=0):
+def expert_kernel(in_ref, up_ref, up_scale_ref, down_ref, down_scale_ref, out_ref):
+    raised = jnp.dot(in_ref[...], up_ref[...], preferred_element_type=F32) * up_scale_ref[...]
+    hidden = (raised * (1.0 + lax.erf(raised * 0.5**0.5)) * 0.5).astype(BF)
+    out = jnp.dot(hidden, down_ref[...], preferred_element_type=F32)
+    out_ref[...] = out * down_scale_ref[...]
+
+
+def mix_own_kernel(combine_ref, rows_ref, out_ref):
+    half = rows_ref.shape[0]
+    out_ref[...] = jnp.dot(combine_ref[:, :half], rows_ref[...], preferred_element_type=F32)
+
+
+def mix_kernel(own_ref, combine_ref, rows_ref, out_hbm, out_ref, sems):
+    half = rows_ref.shape[0]
+    copies = []
+    for k in range(4):
+        mixed = jnp.dot(
+            piece(combine_ref, k, 4)[:, half:], rows_ref[...], preferred_element_type=F32
+        )
+        piece(out_ref, k, 4)[...] = (mixed + piece(own_ref, k, 4)[...]).astype(BF)
+        copies.append(pltpu.make_async_copy(piece(out_ref, k, 4), piece(out_hbm, k, 4), sems.at[k]))
+        copies[-1].start()
+    for copy in copies:
+        copy.wait()
+
+
+def call(
+    kernel,
+    out_shape,
+    *args,
+    scalars=0,
+    hbm=0,
+    hbm_out=False,
+    scratch=(),
+    mib=16,
+    flops=0,
+    moved=0,
+):
     vmem = pl.BlockSpec(memory_space=pltpu.VMEM)
     smem = pl.BlockSpec(memory_space=pltpu.SMEM)
+    far = pl.BlockSpec(memory_space=pltpu.HBM)
     many = isinstance(out_shape, (list, tuple))
     return pl.pallas_call(
         kernel,
         out_shape=out_shape,
-        in_specs=[smem] * scalars + [vmem] * (len(args) - scalars),
-        out_specs=[vmem] * len(out_shape) if many else vmem,
+        in_specs=[smem] * scalars + [far] * hbm + [vmem] * (len(args) - scalars - hbm),
+        out_specs=[vmem] * len(out_shape) if many else (far if hbm_out else vmem),
+        scratch_shapes=list(scratch),
         compiler_params=pltpu.CompilerParams(vmem_limit_bytes=mib << 20),
         cost_estimate=pl.CostEstimate(flops=flops, bytes_accessed=moved, transcendentals=0),
     )(*args)
@@ -171,9 +226,15 @@
                 shape((count, slots), F32),
             ),
             core,
-            tokens,
-            slot_embed,
+            pltpu.with_memory_space_constraint(tokens, pltpu.HBM),
+            pltpu.with_memory_space_constraint(slot_embed, pltpu.HBM),
             scalars=1,
+            hbm=2,
+            scratch=(
+                pltpu.VMEM(tokens.shape, BF),
+                pltpu.VMEM(slot_embed.shape, BF),
+                pltpu.SemaphoreType.DMA((2, 4)),
+            ),
             mib=24,
             flops=10**9,
             moved=4 << 20,
@@ -208,9 +269,17 @@
         spread = pairs.astype(BF).reshape(Y, 2, width)
         slot_inputs = lax.all_to_all(spread, "y", 0, 0, tiled=True).reshape(Y * 2, width)
 
-    raised = jnp.dot(slot_inputs, up_codes[0], preferred_element_type=F32)
-    hidden = jax.nn.gelu(raised * up_scale, approximate=False).astype(BF)
-    partial_out = jnp.dot(hidden, down_codes[0], preferred_element_type=F32) * down_scale
+    with jax.named_scope("expert"):
+        partial_out = call(
+            expert_kernel,
+            shape((Y * 2, width), F32),
+            slot_inputs,
+            up_codes[0],
+            up_scale,
+            down_codes[0],
+            down_scale,
+            moved=4 << 20,
+        )
     with jax.named_scope("out_y"):
         got = lax.all_to_all(partial_out.reshape(Y, 2, width), "y", 0, 0, tiled=True)
         pair_out = jnp.sum(got, axis=0).astype(BF)
@@ -225,9 +294,19 @@
     with jax.named_scope("out_core"):
         other = lax.ppermute(own, "c", swap)
     with jax.named_scope("mix"):
-        mixed = jnp.dot(combine[:, :half], own, preferred_element_type=F32)
-        mixed += jnp.dot(combine[:, half:], other, preferred_element_type=F32)
-    return mixed.astype(BF)
+        mixed = call(
+            mix_own_kernel, shape((count, width), F32), combine, own, flops=3 * 10**8, moved=3 << 20
+        )
+        return call(
+            mix_kernel,
+            shape((count, width), BF),
+            mixed,
+            combine,
+            other,
+            hbm_out=True,
+            scratch=(pltpu.VMEM((count, width), BF), pltpu.SemaphoreType.DMA((4,))),
+            moved=3 << 20,
+        )
 
 
 def solution(mesh):

time: 115 us -> 112 us (0.974)
  blocking collectives: 74.8 us -> 81.7 us
  waiting for transfers between devices: 6.36 us -> 2.21 us
  Pallas kernels: 3.87 us -> 7.87 us
  matrix products: 3.91 us -> 0 us
  local copies, waits for them, and re-layouts: 3.56 us -> 0.33 us
  starting transfers between devices: 22 us -> 18.8 us
    all_to_all x0 -> x1, blocking collectives: none -> 6.71 us  [per_device(): lax.all_to_all(spread, 'y', 0, 0, tiled=True).reshape(Y * 2, width)]
    all_to_all x1 -> x0, waiting for transfers between devices: 4.13 us -> none  [per_device(): lax.all_to_all(spread, 'y', 0, 0, tiled=True).reshape(Y * 2, width)]
    pallas_call x5 -> x8, Pallas kernels: 3.87 us -> 7.87 us  [call(): pl.pallas_call(kernel, out_shape=out_shape, in_specs=[smem] * scalars + [...]
    dot_general x3 -> x0, matrix products: 3.91 us -> none  [the longest x1 2.1 us: per_device(): jnp.dot(hidden, down_codes[0], preferred_element_type=F32) * down_scale]
    all_to_all x1 -> x0, starting transfers between devices: 3.26 us -> none  [per_device(): lax.all_to_all(spread, 'y', 0, 0, tiled=True).reshape(Y * 2, width)]
    unnamed x10 -> x14, local copies, waits for them, and re-layouts: 2.66 us -> 0.04 us
  transfers between devices with their start and end apart: 3 -> 2, of which waited for: 3 -> 2; matrix products, arithmetic and copies ran while one was open for 0% -> 0% of each run, Pallas kernels for 1% -> 1%
where the time goes in v3:
time: 112 us; the launch traced here: 111 us
  blocking collectives  81.7 us (73%)
  starting transfers between devices  18.8 us (17%)
  Pallas kernels  7.87 us (7%)
  waiting for transfers between devices  2.21 us (2%)
    all_to_all x1, blocking collectives, per_device(): lax.all_to_all(part.reshape(ZL * ZH, 2, full), ('zl', 'zh'), 0, 0, tiled=...  25.4 us
    all_to_all x1, blocking collectives, per_device(): lax.all_to_all(part.reshape(X * Y, ZL * 2, full), ('x', 'y'), 0, 0, tiled...  15.5 us
    all_to_all x1, blocking collectives, per_device(): got = lax.all_to_all(spread, ('zl', 'zh'), 0, 0, tiled=True)  14.8 us
    all_to_all x1, blocking collectives, per_device(): lax.all_to_all(spread, ('x', 'y'), 0, 0, tiled=True).reshape(half, width)  12.4 us
    ppermute x1, starting transfers between devices, per_device(): other = lax.ppermute(own, 'c', swap)  10 us
    ppermute x1, starting transfers between devices, per_device(): other = lax.ppermute(send, 'c', swap)  8.79 us
    pallas_call x8, Pallas kernels, call(): pl.pallas_call(kernel, out_shape=out_shape, in_specs=[smem] * scalars + [...  7.87 us
    all_to_all x1, blocking collectives, per_device(): lax.all_to_all(partial_out.reshape(Y, 2, width), 'y', 0, 0, tiled=True)  6.83 us
  transfers between devices with their start and end apart: 2, of which 2 were waited for; matrix products, arithmetic and copies ran while one was open for 0% of the time, Pallas kernels for 1%

profile of v3, /device:TPU:1, one launch (start us, length us, event | category | flops | bytes accessed | tf_op | source)
XLA Modules:
  0.0 111.3 jit_solution(15595263096308569572)
XLA Ops:
  0.0 0.0 copy-start.4
  0.0 3.4 %front.1 = (bf16[256,1408]{1,0:T(8,128)(2,1)S(1)}, bf16[256,384]{1,0:T(8,128)(2,1)S(1)}, f32[256,128]{1,0:T(8,128)S(1)}, f32[384,512]{1,0:T(8,128)S(1)}) custom-call(s32[1]{0:T(128)} %bitcast.core_ref, bf16[384,1280]{1,0:T(8,128)(2,1)} %tok_ref.1, bf16[1280,512]{1,0:T(8,128)(2,1)} %emb_hbm.1), custom_call_target="tpu_custom_call" | custom-call | flops 1000000000 | bytes 4194304 | tf_op jit(solution)/shard_map/front/pallas_call | solution.py:196
  3.4 8.8 %collective-permute-start = (bf16[256,1408]{1,0:T(8,128)(2,1)S(1)}, bf16[256,1408]{1,0:T(8,128)(2,1)S(1)}, u32[]{:S(2)}, u32[]{:S(2)}) collective-permute-start(bf16[256,1408]{1,0:T(8,128)(2,1)S(1)} %get-tuple-element.16), channel_id=1, source_target_pairs={{0,8},{8,0},{1,9},{9,1},{2,10},{10,2},{3,11},{11,3},{4,12},{12,4},... | collective-permute-start | bytes 2162696 | tf_op jit(solution)/shard_map/sum_core/ppermute | solution.py:243
  12.2 0.0 copy-done.4
  12.2 0.8 sum_core.2
  13.1 0.0 copy-start.2
  13.1 0.9 collective-permute-done.got_ref
  14.0 0.0 copy-start.1
  14.0 0.7 sum_core.3
  14.7 0.0 copy-start
  14.7 0.0 copy-start.5
  14.7 0.0 copy-start.6
  14.7 15.5 %all_to_all.30 = bf16[16,16,1408]{2,1,0:T(8,128)(2,1)S(1)} all-to-all(bf16[16,16,1408]{2,1,0:T(8,128)(2,1)S(1)} %bitcast.10), channel_id=1, replica_groups=mesh['zl'=8,'x'=4,'c'=2,'y'=4,'zh'=2] {'x','y'}, dimensions={0} | all-to-all | bytes 1441792 | tf_op jit(solution)/shard_map/sum_xy/all_to_all | solution.py:258
  30.3 0.0 copy-done.2
  30.3 0.3 sum_xy.1
  30.7 0.1 broadcast_in_dim.21
  30.7 25.4 %all_to_all.31 = bf16[16,2,1408]{2,1,0:T(2,128)(2,1)S(1)} all-to-all(bf16[16,2,1408]{2,1,0:T(2,128)(2,1)S(1)} %bitcast.15), channel_id=1, replica_groups=mesh['zl'=8,'x'=4,'c'=2,'y'=4,'zh'=2] {'zl','zh'}, dimensions={0} | all-to-all | bytes 180224 | tf_op jit(solution)/shard_map/sum_z/all_to_all | solution.py:264
  56.1 0.2 sum_z.1
  56.4 6.7 %all_to_all.32 = bf16[4,2,1280]{2,1,0:T(2,128)(2,1)S(1)} all-to-all(bf16[4,2,1280]{2,1,0:T(2,128)(2,1)S(1)} %reshape.42), channel_id=1, replica_groups=mesh['zl'=8,'x'=4,'c'=2,'y'=4,'zh'=2] {'y'}, dimensions={0} | all-to-all | bytes 40960 | tf_op jit(solution)/shard_map/gather_y/all_to_all | solution.py:270
  63.1 0.0 copy-done.1
  63.1 0.0 copy-done
  63.2 0.0 copy-done.5
  63.2 0.0 copy-done.6
  63.2 0.7 expert.1
  63.8 0.0 copy-start.3
  63.9 6.8 %all_to_all.33 = f32[4,2,1280]{2,1,0:T(2,128)S(1)} all-to-all(f32[4,2,1280]{2,1,0:T(2,128)S(1)} %reshape.44), channel_id=1, replica_groups=mesh['zl'=8,'x'=4,'c'=2,'y'=4,'zh'=2] {'y'}, dimensions={0} | all-to-all | bytes 81920 | tf_op jit(solution)/shard_map/out_y/all_to_all | solution.py:284
  70.8 14.8 %all_to_all.34 = bf16[16,2,1280]{2,1,0:T(2,128)(2,1)S(1)} all-to-all(bf16[16,2,1280]{2,1,0:T(2,128)(2,1)S(1)} %broadcast_in_dim.22), channel_id=1, replica_groups=mesh['zl'=8,'x'=4,'c'=2,'y'=4,'zh'=2] {'zl','zh'}, dimensions={0} | all-to-all | bytes 163840 | tf_op jit(solution)/shard_map/out_z/all_to_all | solution.py:288
  85.6 0.1 bitcast_reduce_fusion
  85.8 12.4 %all_to_all.35 = bf16[16,16,1280]{2,1,0:T(8,128)(2,1)S(1)} all-to-all(bf16[16,16,1280]{2,1,0:T(8,128)(2,1)S(1)} %broadcast_in_dim.24), channel_id=1, replica_groups=mesh['zl'=8,'x'=4,'c'=2,'y'=4,'zh'=2] {'x','y'}, dimensions={0} | all-to-all | bytes 1310720 | tf_op jit(solution)/shard_map/out_xy/all_to_all | solution.py:293
  98.2 10.0 %collective-permute-start.1 = (bf16[256,1280]{1,0:T(8,128)(2,1)S(1)}, bf16[256,1280]{1,0:T(8,128)(2,1)S(1)}, u32[]{:S(2)}, u32[]{:S(2)}) collective-permute-start(bf16[256,1280]{1,0:T(8,128)(2,1)S(1)} %bitcast.11), channel_id=1, source_target_pairs={{0,8},{8,0},{1,9},{9,1},{2,10},{10,2},{3,11},{11,3},{4,12},{12,4},... | collective-permute-start | bytes 1966088 | tf_op jit(solution)/shard_map/out_core/ppermute | solution.py:295
  108.3 0.0 copy-done.3
  108.3 0.4 mix.2.own_ref
  108.7 1.3 %collective-permute-done.1.rows_ref = bf16[256,1280]{1,0:T(8,128)(2,1)S(1)} collective-permute-done((bf16[256,1280]{1,0:T(8,128)(2,1)S(1)}, bf16[256,1280]{1,0:T(8,128)(2,1)S(1)}, u32[]{:S(2)}, u32[]{:S(2)}) %collective-permute-start.1) | collective-permute-done | bytes 655392 | tf_op jit(solution)/shard_map/out_core/ppermute | solution.py:295
  110.0 1.3 %mix.3 = bf16[384,1280]{1,0:T(8,128)(2,1)} custom-call(f32[384,1280]{1,0:T(8,128)S(1)} %mix.2.own_ref, bf16[384,512]{1,0:T(8,128)(2,1)S(1)} %copy-done.3, bf16[256,1280]{1,0:T(8,128)(2,1)S(1)} %collective-permute-done.1.rows_ref), custom_call_target="tpu_custom_call" | custom-call | bytes 3145728 | tf_op jit(solution)/shard_map/mix/pallas_call | solution.py:196
  (10 shorter events, 0.3 us)
Async XLA Ops:
  0.0 12.2 %copy-start.4 = (bf16[384,1280]{1,0:T(8,128)(2,1)S(1)}, bf16[384,1280]{1,0:T(8,128)(2,1)}, u32[]{:S(2)}) copy-start(bf16[384,1280]{1,0:T(8,128)(2,1)} %tok_ref.1) | copy-start | bytes 2949124
  3.4 10.6 %collective-permute-start = (bf16[256,1408]{1,0:T(8,128)(2,1)S(1)}, bf16[256,1408]{1,0:T(8,128)(2,1)S(1)}, u32[]{:S(2)}, u32[]{:S(2)}) collective-permute-start(bf16[256,1408]{1,0:T(8,128)(2,1)S(1)} %get-tuple-element.16), channel_id=1, source_target_pairs={{0,8},{8,0},{1,9},{9,1},{2,10},{10,2},{3,11},{11,3},{4,12},{12,4},... | collective-permute-start | bytes 2162696 | tf_op jit(solution)/shard_map/sum_core/ppermute | solution.py:243
  13.1 17.2 %copy-start.2 = (bf16[384,512]{1,0:T(8,128)(2,1)}, bf16[384,512]{1,0:T(8,128)(2,1)S(1)}, u32[]{:S(2)}) copy-start(bf16[384,512]{1,0:T(8,128)(2,1)S(1)} %get-tuple-element.13.combine_ref) | copy-start | bytes 1179652
  14.0 49.1 %copy-start.1 = (bf16[1,640,1280]{2,1,0:T(8,128)(2,1)S(1)}, bf16[1,640,1280]{2,1,0:T(8,128)(2,1)}, u32[]{:S(2)}) copy-start(bf16[1,640,1280]{2,1,0:T(8,128)(2,1)} %param.10) | copy-start | bytes 4915204
  14.7 48.4 %copy-start = (bf16[1,1280,640]{2,1,0:T(8,128)(2,1)S(1)}, bf16[1,1280,640]{2,1,0:T(8,128)(2,1)}, u32[]{:S(2)}) copy-start(bf16[1,1280,640]{2,1,0:T(8,128)(2,1)} %param.8) | copy-start | bytes 4915204
  14.7 48.4 %copy-start.5 = (f32[1,1280]{1,0:T(1,128)S(1)}, f32[1,1280]{1,0:T(1,128)}, u32[]{:S(2)}) copy-start(f32[1,1280]{1,0:T(1,128)} %down_scale_ref.1) | copy-start | bytes 15364
  14.7 48.4 %copy-start.6 = (f32[1,640]{1,0:T(1,128)S(1)}, f32[1,640]{1,0:T(1,128)}, u32[]{:S(2)}) copy-start(f32[1,640]{1,0:T(1,128)} %up_scale_ref.1) | copy-start | bytes 7684
  63.8 44.4 %copy-start.3 = (bf16[384,512]{1,0:T(8,128)(2,1)S(1)}, bf16[384,512]{1,0:T(8,128)(2,1)}, u32[]{:S(2)}) copy-start(bf16[384,512]{1,0:T(8,128)(2,1)} %copy-done.2) | copy-start | bytes 1179652
  98.2 11.7 %collective-permute-start.1 = (bf16[256,1280]{1,0:T(8,128)(2,1)S(1)}, bf16[256,1280]{1,0:T(8,128)(2,1)S(1)}, u32[]{:S(2)}, u32[]{:S(2)}) collective-permute-start(bf16[256,1280]{1,0:T(8,128)(2,1)S(1)} %bitcast.11), channel_id=1, source_target_pairs={{0,8},{8,0},{1,9},{9,1},{2,10},{10,2},{3,11},{11,3},{4,12},{12,4},... | collective-permute-start | bytes 1966088 | tf_op jit(solution)/shard_map/out_core/ppermute | solution.py:295

commit v4 on v3

--- a/solution.py
+++ b/solution.py
@@ -50,12 +50,8 @@
     return ref.at[k * rows : (k + 1) * rows]
 
 
-def front_kernel(
-    core_ref, tok_hbm, emb_hbm, send_ref, own_ref, tail_ref, logits_ref, tok_ref, emb_ref, sems
-):
+def front_kernel(core_ref, tok_hbm, emb_hbm, combine_ref, rows_ref, tok_ref, emb_ref, sems):
     slots = emb_ref.shape[1]
-    half = slots // 2
-    width = tok_ref.shape[1]
     copies = [
         pltpu.make_async_copy(piece(src, k, 4), piece(dst, k, 4), sems.at[i, k])
         for i, (src, dst) in enumerate(((emb_hbm, emb_ref), (tok_hbm, tok_ref)))
@@ -64,47 +60,35 @@
     for copy in copies:
         copy.start()
     order = slot_order(core_ref[0], slots)
-    for copy in copies:
+    for copy in copies[:4]:
         copy.wait()
-    tokens = tok_ref[...]
-    logits = jnp.dot(tokens, emb_ref[...], preferred_element_type=F32)
-    logits_ref[...] = logits
-    m_hi, m_lo = split_pair(jnp.max(logits, axis=0, keepdims=True))
-    shifted = jnp.exp(logits - (m_hi + m_lo))
-    t_hi, t_lo = split_pair(jnp.sum(shifted, axis=0, keepdims=True))
-    row = lax.broadcasted_iota(jnp.int32, (TAIL, slots), 0)
-    stats = jnp.where(row == 0, m_hi, jnp.where(row == 1, m_lo, 0.0))
-    stats = jnp.where(row == 2, t_hi, jnp.where(row == 3, t_lo, stats)).astype(BF)
-    weights = lax.dot_general(
-        order, shifted.astype(BF), NT, preferred_element_type=F32
+    rows_ref[...] = lax.dot_general(
+        order[: slots // 2], emb_ref[...], NT, preferred_element_type=F32
     ).astype(BF)
-    tail = lax.dot_general(order, stats, NT, preferred_element_type=F32)
-    acc = jnp.dot(weights[half:], tokens, preferred_element_type=F32)
-    send_ref[:, :width] = acc.astype(BF)
-    send_ref[:, width:] = tail[half:].astype(BF)
-    own_ref[...] = weights[:half]
-    tail_ref[...] = tail[:half]
-
-
-def own_kernel(core_ref, tok_ref, own_ref, logits_ref, acc_ref, combine_ref):
-    acc_ref[...] = jnp.dot(own_ref[...], tok_ref[...], preferred_element_type=F32)
-    logits = logits_ref[...]
+    for copy in copies[4:]:
+        copy.wait()
+    logits = jnp.dot(tok_ref[...], emb_ref[...], preferred_element_type=F32)
     row_exp = jnp.exp(logits - jnp.max(logits, axis=1, keepdims=True))
     combine = (row_exp / jnp.sum(row_exp, axis=1, keepdims=True)).astype(BF)
-    order = slot_order(core_ref[0], logits.shape[1])
     combine_ref[...] = lax.dot_general(combine, order, NT, preferred_element_type=F32).astype(BF)
 
 
-def core_kernel(acc_ref, tail_ref, got_ref, part_ref):
-    width = acc_ref.shape[1]
-    shift_a, total_a = read_tail(tail_ref[...])
-    shift_b, total_b = read_tail(got_ref[:, width:].astype(F32))
-    top = jnp.maximum(shift_a, shift_b)
-    weight_a = jnp.exp(shift_a - top)
-    weight_b = jnp.exp(shift_b - top)
-    acc = acc_ref[...] * weight_a + got_ref[:, :width].astype(F32) * weight_b
+def pool_kernel(rows_ref, own_ref, other_ref, part_ref):
+    width = own_ref.shape[1]
+    rows = rows_ref[...]
+    blocks = [own_ref[...], other_ref[...]]
+    logits = [lax.dot_general(rows, block, NT, preferred_element_type=F32) for block in blocks]
+    tops = [jnp.max(part, axis=1, keepdims=True) for part in logits]
+    m_hi, m_lo = split_pair(jnp.maximum(*tops))
+    shift = m_hi + m_lo
+    total = jnp.zeros_like(shift)
+    acc = jnp.zeros((rows.shape[0], width), F32)
+    for part, block in zip(logits, blocks):
+        weights = jnp.exp(part - shift)
+        total += jnp.sum(weights, axis=1, keepdims=True)
+        acc += jnp.dot(weights.astype(BF), block, preferred_element_type=F32)
     part_ref[:, :width] = acc.astype(BF)
-    part_ref[:, width:] = tail_lanes(top, total_a * weight_a + total_b * weight_b).astype(BF)
+    part_ref[:, width:] = tail_lanes(shift, total).astype(BF)
 
 
 def plane_kernel(got_ref, part_ref):
@@ -216,15 +200,12 @@
     core = lax.axis_index("c").astype(jnp.int32).reshape(1)
     swap = [(0, 1), (1, 0)]
 
+    with jax.named_scope("swap_tokens"):
+        other = lax.ppermute(tokens, "c", swap)
     with jax.named_scope("front"):
-        send, own, tail, logits = call(
+        combine, rows = call(
             front_kernel,
-            (
-                shape((half, full), BF),
-                shape((half, count), BF),
-                shape((half, TAIL), F32),
-                shape((count, slots), F32),
-            ),
+            (shape((count, slots), BF), shape((half, width), BF)),
             core,
             pltpu.with_memory_space_constraint(tokens, pltpu.HBM),
             pltpu.with_memory_space_constraint(slot_embed, pltpu.HBM),
@@ -239,21 +220,17 @@
             flops=10**9,
             moved=4 << 20,
         )
-    with jax.named_scope("sum_core"):
-        other = lax.ppermute(send, "c", swap)
-        acc, combine = call(
-            own_kernel,
-            (shape((half, width), F32), shape((count, slots), BF)),
-            core,
+    with jax.named_scope("pool"):
+        part = call(
+            pool_kernel,
+            shape((half, full), BF),
+            rows,
             tokens,
-            own,
-            logits,
-            scalars=1,
+            other,
             mib=24,
-            flops=5 * 10**8,
-            moved=4 << 20,
-        )
-        part = call(core_kernel, shape((half, full), BF), acc, tail, other, moved=3 << 20)
+            flops=10**9,
+            moved=3 << 20,
+        )
     with jax.named_scope("sum_xy"):
         got = lax.all_to_all(part.reshape(X * Y, ZL * 2, full), ("x", "y"), 0, 0, tiled=True)
         part = call(

time: 112 us -> 112 us (level)
    pallas_call x8 -> x7, Pallas kernels: 7.87 us -> 8.06 us  [call(): pl.pallas_call(kernel, out_shape=out_shape, in_specs=[smem] * scalars + [...]
  transfers between devices with their start and end apart: 2 -> 2, of which waited for: 2 -> 1; matrix products, arithmetic and copies ran while one was open for 0% -> 0% of each run, Pallas kernels for 1% -> 3%
where the time goes in v4:
time: 112 us; the launch traced here: 111 us
  blocking collectives  82.6 us (74%)
  starting transfers between devices  17.9 us (16%)
  Pallas kernels  8.06 us (7%)
  waiting for transfers between devices  1.27 us (1%)
    all_to_all x1, blocking collectives, per_device(): lax.all_to_all(part.reshape(ZL * ZH, 2, full), ('zl', 'zh'), 0, 0, tiled=...  25.4 us
    all_to_all x1, blocking collectives, per_device(): lax.all_to_all(part.reshape(X * Y, ZL * 2, full), ('x', 'y'), 0, 0, tiled...  15.9 us
    all_to_all x1, blocking collectives, per_device(): got = lax.all_to_all(spread, ('zl', 'zh'), 0, 0, tiled=True)  14.8 us
    all_to_all x1, blocking collectives, per_device(): lax.all_to_all(spread, ('x', 'y'), 0, 0, tiled=True).reshape(half, width)  13 us
    ppermute x1, starting transfers between devices, per_device(): other = lax.ppermute(own, 'c', swap)  9.1 us
    ppermute x1, starting transfers between devices, per_device(): other = lax.ppermute(tokens, 'c', swap)  8.77 us
    pallas_call x7, Pallas kernels, call(): pl.pallas_call(kernel, out_shape=out_shape, in_specs=[smem] * scalars + [...  8.06 us
    all_to_all x1, blocking collectives, per_device(): lax.all_to_all(partial_out.reshape(Y, 2, width), 'y', 0, 0, tiled=True)  6.83 us
  transfers between devices with their start and end apart: 2, of which 1 were waited for; matrix products, arithmetic and copies ran while one was open for 0% of the time, Pallas kernels for 3%

profile of v4, /device:TPU:1, one launch (start us, length us, event | category | flops | bytes accessed | tf_op | source)
XLA Modules:
  0.0 111.2 jit_solution(12985782015893749897)
XLA Ops:
  0.0 8.8 %collective-permute-start = (bf16[384,1280]{1,0:T(8,128)(2,1)}, bf16[384,1280]{1,0:T(8,128)(2,1)S(1)}, u32[]{:S(2)}, u32[]{:S(2)}) collective-permute-start(bf16[384,1280]{1,0:T(8,128)(2,1)} %own_ref.1), channel_id=1, source_target_pairs={{0,8},{8,0},{1,9},{9,1},{2,10},{10,2},{3,11},{11,3},{4,12},{12,4},... | collective-permute-start | bytes 2949128 | tf_op jit(solution)/shard_map/swap_tokens/ppermute | solution.py:204
  8.8 0.0 copy-start.6
  8.8 3.1 %front.1 = (bf16[384,512]{1,0:T(8,128)(2,1)S(1)}, bf16[256,1280]{1,0:T(8,128)(2,1)S(1)}) custom-call(s32[1]{0:T(128)} %bitcast.core_ref, bf16[384,1280]{1,0:T(8,128)(2,1)} %own_ref.1, bf16[1280,512]{1,0:T(8,128)(2,1)} %emb_hbm.1), custom_call_target="tpu_custom_call" | custom-call | flops 1000000000 | bytes 4194304 | tf_op jit(solution)/shard_map/front/pallas_call | solution.py:180
  11.9 0.0 copy-start.2
  11.9 0.7 copy-done.2
  12.7 0.0 collective-permute-done.other_ref
  12.7 0.0 copy-done.6
  12.7 0.0 copy-start.1
  12.7 2.0 %pool.1 = bf16[256,1408]{1,0:T(8,128)(2,1)S(1)} custom-call(bf16[256,1280]{1,0:T(8,128)(2,1)S(1)} %get-tuple-element.8.rows_ref, bf16[384,1280]{1,0:T(8,128)(2,1)S(1)} %copy-done.6, bf16[384,1280]{1,0:T(8,128)(2,1)S(1)} %collective-permute-done.other_ref), custom_call_target="tpu_custom_call" | custom-call | flops 1000000000 | bytes 3145728 | tf_op jit(solution)/shard_map/pool/pallas_call | solution.py:180
  14.7 0.0 copy-start
  14.7 0.0 copy-start.4
  14.7 0.0 copy-start.5
  14.7 15.9 %all_to_all.30 = bf16[16,16,1408]{2,1,0:T(8,128)(2,1)S(1)} all-to-all(bf16[16,16,1408]{2,1,0:T(8,128)(2,1)S(1)} %bitcast.14), channel_id=1, replica_groups=mesh['zl'=8,'x'=4,'c'=2,'y'=4,'zh'=2] {'x','y'}, dimensions={0} | all-to-all | bytes 1441792 | tf_op jit(solution)/shard_map/sum_xy/all_to_all | solution.py:235
  30.7 0.3 sum_xy.1
  31.0 0.1 broadcast_in_dim.21
  31.1 25.4 %all_to_all.31 = bf16[16,2,1408]{2,1,0:T(2,128)(2,1)S(1)} all-to-all(bf16[16,2,1408]{2,1,0:T(2,128)(2,1)S(1)} %bitcast.15), channel_id=1, replica_groups=mesh['zl'=8,'x'=4,'c'=2,'y'=4,'zh'=2] {'zl','zh'}, dimensions={0} | all-to-all | bytes 180224 | tf_op jit(solution)/shard_map/sum_z/all_to_all | solution.py:241
  56.5 0.2 sum_z.1
  56.8 6.6 %all_to_all.32 = bf16[4,2,1280]{2,1,0:T(2,128)(2,1)S(1)} all-to-all(bf16[4,2,1280]{2,1,0:T(2,128)(2,1)S(1)} %reshape.42), channel_id=1, replica_groups=mesh['zl'=8,'x'=4,'c'=2,'y'=4,'zh'=2] {'y'}, dimensions={0} | all-to-all | bytes 40960 | tf_op jit(solution)/shard_map/gather_y/all_to_all | solution.py:247
  63.4 0.0 copy-done.1
  63.4 0.0 copy-done
  63.4 0.0 copy-done.4
  63.4 0.0 copy-done.5
  63.5 0.7 expert.1
  64.1 0.0 copy-start.3
  64.2 6.8 %all_to_all.33 = f32[4,2,1280]{2,1,0:T(2,128)S(1)} all-to-all(f32[4,2,1280]{2,1,0:T(2,128)S(1)} %reshape.44), channel_id=1, replica_groups=mesh['zl'=8,'x'=4,'c'=2,'y'=4,'zh'=2] {'y'}, dimensions={0} | all-to-all | bytes 81920 | tf_op jit(solution)/shard_map/out_y/all_to_all | solution.py:261
  71.1 14.8 %all_to_all.34 = bf16[16,2,1280]{2,1,0:T(2,128)(2,1)S(1)} all-to-all(bf16[16,2,1280]{2,1,0:T(2,128)(2,1)S(1)} %broadcast_in_dim.22), channel_id=1, replica_groups=mesh['zl'=8,'x'=4,'c'=2,'y'=4,'zh'=2] {'zl','zh'}, dimensions={0} | all-to-all | bytes 163840 | tf_op jit(solution)/shard_map/out_z/all_to_all | solution.py:265
  85.9 0.1 bitcast_reduce_fusion
  86.1 13.0 %all_to_all.35 = bf16[16,16,1280]{2,1,0:T(8,128)(2,1)S(1)} all-to-all(bf16[16,16,1280]{2,1,0:T(8,128)(2,1)S(1)} %broadcast_in_dim.24), channel_id=1, replica_groups=mesh['zl'=8,'x'=4,'c'=2,'y'=4,'zh'=2] {'x','y'}, dimensions={0} | all-to-all | bytes 1310720 | tf_op jit(solution)/shard_map/out_xy/all_to_all | solution.py:270
  99.1 9.1 %collective-permute-start.1 = (bf16[256,1280]{1,0:T(8,128)(2,1)S(1)}, bf16[256,1280]{1,0:T(8,128)(2,1)S(1)}, u32[]{:S(2)}, u32[]{:S(2)}) collective-permute-start(bf16[256,1280]{1,0:T(8,128)(2,1)S(1)} %bitcast.10), channel_id=1, source_target_pairs={{0,8},{8,0},{1,9},{9,1},{2,10},{10,2},{3,11},{11,3},{4,12},{12,4},... | collective-permute-start | bytes 1966088 | tf_op jit(solution)/shard_map/out_core/ppermute | solution.py:272
  108.2 0.0 copy-done.3
  108.2 0.4 mix.2.own_ref
  108.6 1.3 %collective-permute-done.1.rows_ref = bf16[256,1280]{1,0:T(8,128)(2,1)S(1)} collective-permute-done((bf16[256,1280]{1,0:T(8,128)(2,1)S(1)}, bf16[256,1280]{1,0:T(8,128)(2,1)S(1)}, u32[]{:S(2)}, u32[]{:S(2)}) %collective-permute-start.1) | collective-permute-done | bytes 655392 | tf_op jit(solution)/shard_map/out_core/ppermute | solution.py:272
  109.9 1.3 %mix.3 = bf16[384,1280]{1,0:T(8,128)(2,1)} custom-call(f32[384,1280]{1,0:T(8,128)S(1)} %mix.2.own_ref, bf16[384,512]{1,0:T(8,128)(2,1)S(1)} %copy-done.3, bf16[256,1280]{1,0:T(8,128)(2,1)S(1)} %collective-permute-done.1.rows_ref), custom_call_target="tpu_custom_call" | custom-call | bytes 3145728 | tf_op jit(solution)/shard_map/mix/pallas_call | solution.py:180
  (10 shorter events, 0.3 us)
Async XLA Ops:
  0.0 12.7 %collective-permute-start = (bf16[384,1280]{1,0:T(8,128)(2,1)}, bf16[384,1280]{1,0:T(8,128)(2,1)S(1)}, u32[]{:S(2)}, u32[]{:S(2)}) collective-permute-start(bf16[384,1280]{1,0:T(8,128)(2,1)} %own_ref.1), channel_id=1, source_target_pairs={{0,8},{8,0},{1,9},{9,1},{2,10},{10,2},{3,11},{11,3},{4,12},{12,4},... | collective-permute-start | bytes 2949128 | tf_op jit(solution)/shard_map/swap_tokens/ppermute | solution.py:204
  8.8 3.9 %copy-start.6 = (bf16[384,1280]{1,0:T(8,128)(2,1)S(1)}, bf16[384,1280]{1,0:T(8,128)(2,1)}, u32[]{:S(2)}) copy-start(bf16[384,1280]{1,0:T(8,128)(2,1)} %own_ref.1) | copy-start | bytes 2949124
  11.9 0.7 copy-start.2
  12.7 50.7 %copy-start.1 = (bf16[1,640,1280]{2,1,0:T(8,128)(2,1)S(1)}, bf16[1,640,1280]{2,1,0:T(8,128)(2,1)}, u32[]{:S(2)}) copy-start(bf16[1,640,1280]{2,1,0:T(8,128)(2,1)} %param.10) | copy-start | bytes 4915204
  14.7 48.7 %copy-start = (bf16[1,1280,640]{2,1,0:T(8,128)(2,1)S(1)}, bf16[1,1280,640]{2,1,0:T(8,128)(2,1)}, u32[]{:S(2)}) copy-start(bf16[1,1280,640]{2,1,0:T(8,128)(2,1)} %param.8) | copy-start | bytes 4915204
  14.7 48.7 %copy-start.4 = (f32[1,1280]{1,0:T(1,128)S(1)}, f32[1,1280]{1,0:T(1,128)}, u32[]{:S(2)}) copy-start(f32[1,1280]{1,0:T(1,128)} %down_scale_ref.1) | copy-start | bytes 15364
  14.7 48.7 %copy-start.5 = (f32[1,640]{1,0:T(1,128)S(1)}, f32[1,640]{1,0:T(1,128)}, u32[]{:S(2)}) copy-start(f32[1,640]{1,0:T(1,128)} %up_scale_ref.1) | copy-start | bytes 7684
  64.1 44.1 %copy-start.3 = (bf16[384,512]{1,0:T(8,128)(2,1)S(1)}, bf16[384,512]{1,0:T(8,128)(2,1)}, u32[]{:S(2)}) copy-start(bf16[384,512]{1,0:T(8,128)(2,1)} %copy-done.2) | copy-start | bytes 1179652
  99.1 10.8 %collective-permute-start.1 = (bf16[256,1280]{1,0:T(8,128)(2,1)S(1)}, bf16[256,1280]{1,0:T(8,128)(2,1)S(1)}, u32[]{:S(2)}, u32[]{:S(2)}) collective-permute-start(bf16[256,1280]{1,0:T(8,128)(2,1)S(1)} %bitcast.10), channel_id=1, source_target_pairs={{0,8},{8,0},{1,9},{9,1},{2,10},{10,2},{3,11},{11,3},{4,12},{12,4},... | collective-permute-start | bytes 1966088 | tf_op jit(solution)/shard_map/out_core/ppermute | solution.py:272

commit v5 on v4

--- a/solution.py
+++ b/solution.py
@@ -20,9 +20,9 @@
     return hi, lo
 
 
-def slot_order(core, slots):
-    n = lax.broadcasted_iota(jnp.int32, (slots, 1), 0)
-    k = lax.broadcasted_iota(jnp.int32, (slots, slots), 1)
+def slot_order(core, slots, rows):
+    n = lax.broadcasted_iota(jnp.int32, (rows, 1), 0)
+    k = lax.broadcasted_iota(jnp.int32, (rows, slots), 1)
     place = (
         ((n >> 1) & 7) * 64
         + ((n >> 6) & 3) * 16
@@ -50,7 +50,26 @@
     return ref.at[k * rows : (k + 1) * rows]
 
 
-def front_kernel(core_ref, tok_hbm, emb_hbm, combine_ref, rows_ref, tok_ref, emb_ref, sems):
+def pool(rows, tokens):
+    logits = lax.dot_general(rows, tokens, NT, preferred_element_type=F32)
+    m_hi, m_lo = split_pair(jnp.max(logits, axis=1, keepdims=True))
+    shift = m_hi + m_lo
+    weights = jnp.exp(logits - shift)
+    total = jnp.sum(weights, axis=1, keepdims=True)
+    return shift, total, jnp.dot(weights.astype(BF), tokens, preferred_element_type=F32)
+
+
+def combine_weights(tokens, embed, core):
+    logits = jnp.dot(tokens, embed, preferred_element_type=F32)
+    row_exp = jnp.exp(logits - jnp.max(logits, axis=1, keepdims=True))
+    combine = (row_exp / jnp.sum(row_exp, axis=1, keepdims=True)).astype(BF)
+    order = slot_order(core, embed.shape[1], embed.shape[1])
+    return lax.dot_general(combine, order, NT, preferred_element_type=F32).astype(BF)
+
+
+def front_kernel(
+    core_ref, tok_hbm, emb_hbm, rows_ref, acc_ref, stat_ref, tok_ref, emb_ref, sems
+):
     slots = emb_ref.shape[1]
     copies = [
         pltpu.make_async_copy(piece(src, k, 4), piece(dst, k, 4), sems.at[i, k])
@@ -59,36 +78,33 @@
     ]
     for copy in copies:
         copy.start()
-    order = slot_order(core_ref[0], slots)
+    order = slot_order(core_ref[0], slots, slots // 2)
     for copy in copies[:4]:
         copy.wait()
-    rows_ref[...] = lax.dot_general(
-        order[: slots // 2], emb_ref[...], NT, preferred_element_type=F32
-    ).astype(BF)
+    rows = lax.dot_general(order, emb_ref[...], NT, preferred_element_type=F32).astype(BF)
+    rows_ref[...] = rows
     for copy in copies[4:]:
         copy.wait()
-    logits = jnp.dot(tok_ref[...], emb_ref[...], preferred_element_type=F32)
-    row_exp = jnp.exp(logits - jnp.max(logits, axis=1, keepdims=True))
-    combine = (row_exp / jnp.sum(row_exp, axis=1, keepdims=True)).astype(BF)
-    combine_ref[...] = lax.dot_general(combine, order, NT, preferred_element_type=F32).astype(BF)
-
-
-def pool_kernel(rows_ref, own_ref, other_ref, part_ref):
-    width = own_ref.shape[1]
-    rows = rows_ref[...]
-    blocks = [own_ref[...], other_ref[...]]
-    logits = [lax.dot_general(rows, block, NT, preferred_element_type=F32) for block in blocks]
-    tops = [jnp.max(part, axis=1, keepdims=True) for part in logits]
-    m_hi, m_lo = split_pair(jnp.maximum(*tops))
-    shift = m_hi + m_lo
-    total = jnp.zeros_like(shift)
-    acc = jnp.zeros((rows.shape[0], width), F32)
-    for part, block in zip(logits, blocks):
-        weights = jnp.exp(part - shift)
-        total += jnp.sum(weights, axis=1, keepdims=True)
-        acc += jnp.dot(weights.astype(BF), block, preferred_element_type=F32)
-    part_ref[:, :width] = acc.astype(BF)
-    part_ref[:, width:] = tail_lanes(shift, total).astype(BF)
+    shift, total, acc = pool(rows, tok_ref[...])
+    acc_ref[...] = acc
+    stat_ref[...] = tail_lanes(shift, total)
+
+
+def pool_kernel(
+    core_ref, rows_ref, acc_ref, stat_ref, other_ref, tok_ref, emb_ref, part_ref, combine_ref
+):
+    width = acc_ref.shape[1]
+    shift_a, total_a = read_tail(stat_ref[...])
+    shift_b, total_b, acc_b = pool(rows_ref[...], other_ref[...])
+    top = jnp.maximum(shift_a, shift_b)
+    weight_a = jnp.exp(shift_a - top)
+    weight_b = jnp.exp(shift_b - top)
+    part_ref[:, :width] = (acc_ref[...] * weight_a + acc_b * weight_b).astype(BF)
+    part_ref[:, width:] = tail_lanes(top, total_a * weight_a + total_b * weight_b).astype(BF)
+
+    @pl.when(core_ref[0] == 1)
+    def _():
+        combine_ref[...] = combine_weights(tok_ref[...], emb_ref[...], core_ref[0])
 
 
 def plane_kernel(got_ref, part_ref):
@@ -142,20 +158,31 @@
     out_ref[...] = out * down_scale_ref[...]
 
 
-def mix_own_kernel(combine_ref, rows_ref, out_ref):
+def mix_own_kernel(core_ref, tok_ref, emb_ref, early_ref, rows_ref, out_ref, combine_ref, all_ref):
     half = rows_ref.shape[0]
-    out_ref[...] = jnp.dot(combine_ref[:, :half], rows_ref[...], preferred_element_type=F32)
+
+    @pl.when(core_ref[0] == 1)
+    def _():
+        all_ref[...] = early_ref[...]
+
+    @pl.when(core_ref[0] == 0)
+    def _():
+        all_ref[...] = combine_weights(tok_ref[...], emb_ref[...], core_ref[0])
+
+    combine_ref[...] = all_ref[:, half:]
+    out_ref[...] = jnp.dot(all_ref[:, :half], rows_ref[...], preferred_element_type=F32)
 
 
 def mix_kernel(own_ref, combine_ref, rows_ref, out_hbm, out_ref, sems):
-    half = rows_ref.shape[0]
+    count = sems.shape[0]
     copies = []
-    for k in range(4):
+    for k in range(count):
         mixed = jnp.dot(
-            piece(combine_ref, k, 4)[:, half:], rows_ref[...], preferred_element_type=F32
-        )
-        piece(out_ref, k, 4)[...] = (mixed + piece(own_ref, k, 4)[...]).astype(BF)
-        copies.append(pltpu.make_async_copy(piece(out_ref, k, 4), piece(out_hbm, k, 4), sems.at[k]))
+            piece(combine_ref, k, count)[...], rows_ref[...], preferred_element_type=F32
+        )
+        out = piece(out_ref, k, count)
+        out[...] = (mixed + piece(own_ref, k, count)[...]).astype(BF)
+        copies.append(pltpu.make_async_copy(out, piece(out_hbm, k, count), sems.at[k]))
         copies[-1].start()
     for copy in copies:
         copy.wait()
@@ -203,30 +230,37 @@
     with jax.named_scope("swap_tokens"):
         other = lax.ppermute(tokens, "c", swap)
     with jax.named_scope("front"):
-        combine, rows = call(
+        rows, acc, stat, tok, emb = call(
             front_kernel,
-            (shape((count, slots), BF), shape((half, width), BF)),
+            (
+                shape((half, width), BF),
+                shape((half, width), F32),
+                shape((half, TAIL), F32),
+                shape(tokens.shape, BF),
+                shape(slot_embed.shape, BF),
+            ),
             core,
             pltpu.with_memory_space_constraint(tokens, pltpu.HBM),
             pltpu.with_memory_space_constraint(slot_embed, pltpu.HBM),
             scalars=1,
             hbm=2,
-            scratch=(
-                pltpu.VMEM(tokens.shape, BF),
-                pltpu.VMEM(slot_embed.shape, BF),
-                pltpu.SemaphoreType.DMA((2, 4)),
-            ),
+            scratch=(pltpu.SemaphoreType.DMA((2, 4)),),
             mib=24,
             flops=10**9,
             moved=4 << 20,
         )
     with jax.named_scope("pool"):
-        part = call(
+        part, combine = call(
             pool_kernel,
-            shape((half, full), BF),
+            (shape((half, full), BF), shape((count, slots), BF)),
+            core,
             rows,
-            tokens,
+            acc,
+            stat,
             other,
+            tok,
+            emb,
+            scalars=1,
             mib=24,
             flops=10**9,
             moved=3 << 20,
@@ -271,8 +305,19 @@
     with jax.named_scope("out_core"):
         other = lax.ppermute(own, "c", swap)
     with jax.named_scope("mix"):
-        mixed = call(
-            mix_own_kernel, shape((count, width), F32), combine, own, flops=3 * 10**8, moved=3 << 20
+        mixed, combine = call(
+            mix_own_kernel,
+            (shape((count, width), F32), shape((count, half), BF)),
+            core,
+            tok,
+            emb,
+            combine,
+            own,
+            scalars=1,
+            scratch=(pltpu.VMEM((count, slots), BF),),
+            mib=24,
+            flops=10**9,
+            moved=3 << 20,
         )
         return call(
             mix_kernel,
@@ -281,7 +326,7 @@
             combine,
             other,
             hbm_out=True,
-            scratch=(pltpu.VMEM((count, width), BF), pltpu.SemaphoreType.DMA((4,))),
+            scratch=(pltpu.VMEM((count, width), BF), pltpu.SemaphoreType.DMA((8,))),
             moved=3 << 20,
         )
 

time: 112 us -> 113 us (level)
  Pallas kernels: 8.06 us -> 9.38 us
    pallas_call x7, Pallas kernels: 8.06 us -> 9.38 us  [call(): pl.pallas_call(kernel, out_shape=out_shape, in_specs=[smem] * scalars + [...]
where the time goes in v5:
time: 113 us; the launch traced here: 112 us
  blocking collectives  83.4 us (74%)
  starting transfers between devices  17 us (15%)
  Pallas kernels  9.38 us (8%)
  local copies, waits for them, and re-layouts  2.06 us (2%)
    all_to_all x1, blocking collectives, per_device(): lax.all_to_all(part.reshape(ZL * ZH, 2, full), ('zl', 'zh'), 0, 0, tiled=...  26.3 us
    all_to_all x1, blocking collectives, per_device(): got = lax.all_to_all(spread, ('zl', 'zh'), 0, 0, tiled=True)  15.8 us
    all_to_all x1, blocking collectives, per_device(): lax.all_to_all(part.reshape(X * Y, ZL * 2, full), ('x', 'y'), 0, 0, tiled...  15.6 us
    all_to_all x1, blocking collectives, per_device(): lax.all_to_all(spread, ('x', 'y'), 0, 0, tiled=True).reshape(half, width)  12.3 us
    pallas_call x7, Pallas kernels, call(): pl.pallas_call(kernel, out_shape=out_shape, in_specs=[smem] * scalars + [...  9.38 us
    ppermute x1, starting transfers between devices, per_device(): other = lax.ppermute(tokens, 'c', swap)  8.77 us
    ppermute x1, starting transfers between devices, per_device(): other = lax.ppermute(own, 'c', swap)  8.26 us
    all_to_all x1, blocking collectives, per_device(): lax.all_to_all(partial_out.reshape(Y, 2, width), 'y', 0, 0, tiled=True)  6.83 us
  transfers between devices with their start and end apart: 2, of which 1 were waited for; matrix products, arithmetic and copies ran while one was open for 0% of the time, Pallas kernels for 3%

profile of v5, /device:TPU:1, one launch (start us, length us, event | category | flops | bytes accessed | tf_op | source)
XLA Modules:
  0.0 112.4 jit_solution(17939232440022002486)
XLA Ops:
  0.0 8.8 %collective-permute-start = (bf16[384,1280]{1,0:T(8,128)(2,1)}, bf16[384,1280]{1,0:T(8,128)(2,1)S(1)}, u32[]{:S(2)}, u32[]{:S(2)}) collective-permute-start(bf16[384,1280]{1,0:T(8,128)(2,1)} %tok_hbm.1), channel_id=1, source_target_pairs={{0,8},{8,0},{1,9},{9,1},{2,10},{10,2},{3,11},{11,3},{4,12},{12,4},... | collective-permute-start | bytes 2949128 | tf_op jit(solution)/shard_map/swap_tokens/ppermute | solution.py:231
  8.8 3.2 %front.1 = (bf16[256,1280]{1,0:T(8,128)(2,1)S(1)}, f32[256,1280]{1,0:T(8,128)S(1)}, f32[256,128]{1,0:T(8,128)S(1)}, bf16[384,1280]{1,0:T(8,128)(2,1)S(1)}, bf16[1280,512]{1,0:T(8,128)(2,1)S(1)}) custom-call(s32[1]{0:T(128)} %bitcast.core_ref, bf16[384,1280]{1,0:T(8,128)(2,1)} %tok_hbm.1, bf16[1280,512]{1,0:T(8,128)(2,1)} %emb_hbm.1), custom_call_target="tpu_custom_call" | custom-call | flops 1000000000 | bytes 4194304 | tf_op jit(solution)/shard_map/front/pallas_call | solution.py:207
  12.0 0.0 copy-start.2
  12.0 0.0 copy-start.4
  12.0 0.0 collective-permute-done.other_ref
  12.0 0.0 copy-start.1
  12.0 2.7 %pool.1 = (bf16[256,1408]{1,0:T(8,128)(2,1)S(1)}, bf16[384,512]{1,0:T(8,128)(2,1)S(1)}) custom-call(s32[1]{0:T(128)} %bitcast.core_ref, bf16[256,1280]{1,0:T(8,128)(2,1)S(1)} %get-tuple-element.16.rows_ref, f32[256,1280]{1,0:T(8,128)S(1)} %get-tuple-element.17.acc_ref, f32[256,128]{1,0:T(8,128)S(1)} %get-tuple-element.18.stat_ref, ...), custom_call_target="tpu_custom_call" | custom-call | flops 1000000000 | bytes 3145728 | tf_op jit(solution)/shard_map/pool/pallas_call | solution.py:207
  14.8 0.0 copy-done.2
  14.8 0.0 copy-done.4
  14.8 0.0 copy-start.8
  14.8 0.7 copy-done.8
  15.5 0.0 copy-start
  15.6 0.0 copy-start.6
  15.6 0.0 copy-start.7
  15.6 15.6 %all_to_all.30 = bf16[16,16,1408]{2,1,0:T(8,128)(2,1)S(1)} all-to-all(bf16[16,16,1408]{2,1,0:T(8,128)(2,1)S(1)} %bitcast.12), channel_id=1, replica_groups=mesh['zl'=8,'x'=4,'c'=2,'y'=4,'zh'=2] {'x','y'}, dimensions={0} | all-to-all | bytes 1441792 | tf_op jit(solution)/shard_map/sum_xy/all_to_all | solution.py:269
  31.1 0.3 sum_xy.1
  31.5 0.1 broadcast_in_dim.21
  31.6 26.3 %all_to_all.31 = bf16[16,2,1408]{2,1,0:T(2,128)(2,1)S(1)} all-to-all(bf16[16,2,1408]{2,1,0:T(2,128)(2,1)S(1)} %bitcast.15), channel_id=1, replica_groups=mesh['zl'=8,'x'=4,'c'=2,'y'=4,'zh'=2] {'zl','zh'}, dimensions={0} | all-to-all | bytes 180224 | tf_op jit(solution)/shard_map/sum_z/all_to_all | solution.py:275
  57.9 0.2 sum_z.1
  58.2 6.6 %all_to_all.32 = bf16[4,2,1280]{2,1,0:T(2,128)(2,1)S(1)} all-to-all(bf16[4,2,1280]{2,1,0:T(2,128)(2,1)S(1)} %reshape.42), channel_id=1, replica_groups=mesh['zl'=8,'x'=4,'c'=2,'y'=4,'zh'=2] {'y'}, dimensions={0} | all-to-all | bytes 40960 | tf_op jit(solution)/shard_map/gather_y/all_to_all | solution.py:281
  64.8 0.0 copy-done.1
  64.8 0.0 copy-done
  64.8 0.0 copy-done.6
  64.8 0.0 copy-done.7
  64.8 0.7 expert.1
  65.5 0.0 copy-start.3
  65.5 0.0 copy-start.5
  65.5 6.8 %all_to_all.33 = f32[4,2,1280]{2,1,0:T(2,128)S(1)} all-to-all(f32[4,2,1280]{2,1,0:T(2,128)S(1)} %reshape.44), channel_id=1, replica_groups=mesh['zl'=8,'x'=4,'c'=2,'y'=4,'zh'=2] {'y'}, dimensions={0} | all-to-all | bytes 81920 | tf_op jit(solution)/shard_map/out_y/all_to_all | solution.py:295
  72.4 15.8 %all_to_all.34 = bf16[16,2,1280]{2,1,0:T(2,128)(2,1)S(1)} all-to-all(bf16[16,2,1280]{2,1,0:T(2,128)(2,1)S(1)} %broadcast_in_dim.22), channel_id=1, replica_groups=mesh['zl'=8,'x'=4,'c'=2,'y'=4,'zh'=2] {'zl','zh'}, dimensions={0} | all-to-all | bytes 163840 | tf_op jit(solution)/shard_map/out_z/all_to_all | solution.py:299
  88.2 0.1 bitcast_reduce_fusion
  88.4 12.3 %all_to_all.35 = bf16[16,16,1280]{2,1,0:T(8,128)(2,1)S(1)} all-to-all(bf16[16,16,1280]{2,1,0:T(8,128)(2,1)S(1)} %broadcast_in_dim.24), channel_id=1, replica_groups=mesh['zl'=8,'x'=4,'c'=2,'y'=4,'zh'=2] {'x','y'}, dimensions={0} | all-to-all | bytes 1310720 | tf_op jit(solution)/shard_map/out_xy/all_to_all | solution.py:304
  100.7 8.3 %collective-permute-start.1 = (bf16[256,1280]{1,0:T(8,128)(2,1)S(1)}, bf16[256,1280]{1,0:T(8,128)(2,1)S(1)}, u32[]{:S(2)}, u32[]{:S(2)}) collective-permute-start(bf16[256,1280]{1,0:T(8,128)(2,1)S(1)} %bitcast.13), channel_id=1, source_target_pairs={{0,8},{8,0},{1,9},{9,1},{2,10},{10,2},{3,11},{11,3},{4,12},{12,4},... | collective-permute-start | bytes 1966088 | tf_op jit(solution)/shard_map/out_core/ppermute | solution.py:306
  109.0 0.0 copy-done.3
  109.0 0.0 copy-done.5
  109.0 0.0 copy-start.9
  109.0 1.0 copy-done.9
  110.0 0.5 mix.2
  110.5 0.2 collective-permute-done.1.rows_ref
  110.7 1.7 %mix.3 = bf16[384,1280]{1,0:T(8,128)(2,1)} custom-call(f32[384,1280]{1,0:T(8,128)S(1)} %get-tuple-element.21.own_ref, bf16[384,256]{1,0:T(8,128)(2,1)S(1)} %get-tuple-element.22.combine_ref, bf16[256,1280]{1,0:T(8,128)(2,1)S(1)} %collective-permute-done.1.rows_ref), custom_call_target="tpu_custom_call" | custom-call | bytes 3145728 | tf_op jit(solution)/shard_map/mix/pallas_call | solution.py:207
  (10 shorter events, 0.3 us)
Async XLA Ops:
  0.0 12.0 %collective-permute-start = (bf16[384,1280]{1,0:T(8,128)(2,1)}, bf16[384,1280]{1,0:T(8,128)(2,1)S(1)}, u32[]{:S(2)}, u32[]{:S(2)}) collective-permute-start(bf16[384,1280]{1,0:T(8,128)(2,1)} %tok_hbm.1), channel_id=1, source_target_pairs={{0,8},{8,0},{1,9},{9,1},{2,10},{10,2},{3,11},{11,3},{4,12},{12,4},... | collective-permute-start | bytes 2949128 | tf_op jit(solution)/shard_map/swap_tokens/ppermute | solution.py:231
  12.0 2.8 %copy-start.2 = (bf16[1280,512]{1,0:T(8,128)(2,1)}, bf16[1280,512]{1,0:T(8,128)(2,1)S(1)}, u32[]{:S(2)}) copy-start(bf16[1280,512]{1,0:T(8,128)(2,1)S(1)} %get-tuple-element.15.emb_ref) | copy-start | bytes 3932164
  12.0 2.8 %copy-start.4 = (bf16[384,1280]{1,0:T(8,128)(2,1)}, bf16[384,1280]{1,0:T(8,128)(2,1)S(1)}, u32[]{:S(2)}) copy-start(bf16[384,1280]{1,0:T(8,128)(2,1)S(1)} %get-tuple-element.14.tok_ref) | copy-start | bytes 2949124
  12.0 52.7 %copy-start.1 = (bf16[1,640,1280]{2,1,0:T(8,128)(2,1)S(1)}, bf16[1,640,1280]{2,1,0:T(8,128)(2,1)}, u32[]{:S(2)}) copy-start(bf16[1,640,1280]{2,1,0:T(8,128)(2,1)} %param.10) | copy-start | bytes 4915204
  14.8 0.7 copy-start.8
  15.5 49.2 %copy-start = (bf16[1,1280,640]{2,1,0:T(8,128)(2,1)S(1)}, bf16[1,1280,640]{2,1,0:T(8,128)(2,1)}, u32[]{:S(2)}) copy-start(bf16[1,1280,640]{2,1,0:T(8,128)(2,1)} %param.8) | copy-start | bytes 4915204
  15.6 49.2 %copy-start.6 = (f32[1,1280]{1,0:T(1,128)S(1)}, f32[1,1280]{1,0:T(1,128)}, u32[]{:S(2)}) copy-start(f32[1,1280]{1,0:T(1,128)} %down_scale_ref.1) | copy-start | bytes 15364
  15.6 49.2 %copy-start.7 = (f32[1,640]{1,0:T(1,128)S(1)}, f32[1,640]{1,0:T(1,128)}, u32[]{:S(2)}) copy-start(f32[1,640]{1,0:T(1,128)} %up_scale_ref.1) | copy-start | bytes 7684
  65.5 43.5 %copy-start.3 = (bf16[1280,512]{1,0:T(8,128)(2,1)S(1)}, bf16[1280,512]{1,0:T(8,128)(2,1)}, u32[]{:S(2)}) copy-start(bf16[1280,512]{1,0:T(8,128)(2,1)} %copy-done.2) | copy-start | bytes 3932164
  65.5 43.5 %copy-start.5 = (bf16[384,1280]{1,0:T(8,128)(2,1)S(1)}, bf16[384,1280]{1,0:T(8,128)(2,1)}, u32[]{:S(2)}) copy-start(bf16[384,1280]{1,0:T(8,128)(2,1)} %copy-done.4) | copy-start | bytes 2949124
  100.7 10.0 %collective-permute-start.1 = (bf16[256,1280]{1,0:T(8,128)(2,1)S(1)}, bf16[256,1280]{1,0:T(8,128)(2,1)S(1)}, u32[]{:S(2)}, u32[]{:S(2)}) collective-permute-start(bf16[256,1280]{1,0:T(8,128)(2,1)S(1)} %bitcast.13), channel_id=1, source_target_pairs={{0,8},{8,0},{1,9},{9,1},{2,10},{10,2},{3,11},{11,3},{4,12},{12,4},... | collective-permute-start | bytes 1966088 | tf_op jit(solution)/shard_map/out_core/ppermute | solution.py:306
  109.0 1.0 copy-start.9

commit v6 on v5

--- a/solution.py
+++ b/solution.py
@@ -68,31 +68,36 @@
 
 
 def front_kernel(
-    core_ref, tok_hbm, emb_hbm, rows_ref, acc_ref, stat_ref, tok_ref, emb_ref, sems
+    core_ref, tok_hbm, emb_hbm, rows_ref, acc_ref, stat_ref, tok_ref, emb_ref, emb_sems, tok_sems
 ):
     slots = emb_ref.shape[1]
-    copies = [
-        pltpu.make_async_copy(piece(src, k, 4), piece(dst, k, 4), sems.at[i, k])
-        for i, (src, dst) in enumerate(((emb_hbm, emb_ref), (tok_hbm, tok_ref)))
-        for k in range(4)
+    count = emb_sems.shape[0]
+    loads = [
+        pltpu.make_async_copy(piece(emb_hbm, k, count), piece(emb_ref, k, count), emb_sems.at[k])
+        for k in range(count)
     ]
-    for copy in copies:
+    more = tok_sems.shape[0]
+    token_loads = [
+        pltpu.make_async_copy(piece(tok_hbm, k, more), piece(tok_ref, k, more), tok_sems.at[k])
+        for k in range(more)
+    ]
+    for copy in loads + token_loads:
         copy.start()
     order = slot_order(core_ref[0], slots, slots // 2)
-    for copy in copies[:4]:
+    step = emb_ref.shape[0] // count
+    for k, copy in enumerate(loads):
         copy.wait()
-    rows = lax.dot_general(order, emb_ref[...], NT, preferred_element_type=F32).astype(BF)
-    rows_ref[...] = rows
-    for copy in copies[4:]:
+        rows_ref[:, k * step : (k + 1) * step] = lax.dot_general(
+            order, piece(emb_ref, k, count)[...], NT, preferred_element_type=F32
+        ).astype(BF)
+    for copy in token_loads:
         copy.wait()
-    shift, total, acc = pool(rows, tok_ref[...])
+    shift, total, acc = pool(rows_ref[...], tok_ref[...])
     acc_ref[...] = acc
     stat_ref[...] = tail_lanes(shift, total)
 
 
-def pool_kernel(
-    core_ref, rows_ref, acc_ref, stat_ref, other_ref, tok_ref, emb_ref, part_ref, combine_ref
-):
+def pool_kernel(rows_ref, acc_ref, stat_ref, other_ref, part_ref):
     width = acc_ref.shape[1]
     shift_a, total_a = read_tail(stat_ref[...])
     shift_b, total_b, acc_b = pool(rows_ref[...], other_ref[...])
@@ -101,10 +106,6 @@
     weight_b = jnp.exp(shift_b - top)
     part_ref[:, :width] = (acc_ref[...] * weight_a + acc_b * weight_b).astype(BF)
     part_ref[:, width:] = tail_lanes(top, total_a * weight_a + total_b * weight_b).astype(BF)
-
-    @pl.when(core_ref[0] == 1)
-    def _():
-        combine_ref[...] = combine_weights(tok_ref[...], emb_ref[...], core_ref[0])
 
 
 def plane_kernel(got_ref, part_ref):
@@ -158,31 +159,23 @@
     out_ref[...] = out * down_scale_ref[...]
 
 
-def mix_own_kernel(core_ref, tok_ref, emb_ref, early_ref, rows_ref, out_ref, combine_ref, all_ref):
+def mix_own_kernel(core_ref, tok_ref, emb_ref, rows_ref, out_ref, combine_ref):
     half = rows_ref.shape[0]
-
-    @pl.when(core_ref[0] == 1)
-    def _():
-        all_ref[...] = early_ref[...]
-
-    @pl.when(core_ref[0] == 0)
-    def _():
-        all_ref[...] = combine_weights(tok_ref[...], emb_ref[...], core_ref[0])
-
-    combine_ref[...] = all_ref[:, half:]
-    out_ref[...] = jnp.dot(all_ref[:, :half], rows_ref[...], preferred_element_type=F32)
+    combine = combine_weights(tok_ref[...], emb_ref[...], core_ref[0])
+    combine_ref[...] = combine[:, half:]
+    out_ref[...] = jnp.dot(combine[:, :half], rows_ref[...], preferred_element_type=F32)
 
 
 def mix_kernel(own_ref, combine_ref, rows_ref, out_hbm, out_ref, sems):
     count = sems.shape[0]
+    step = rows_ref.shape[1] // count
+    combine = combine_ref[...]
     copies = []
     for k in range(count):
-        mixed = jnp.dot(
-            piece(combine_ref, k, count)[...], rows_ref[...], preferred_element_type=F32
-        )
-        out = piece(out_ref, k, count)
-        out[...] = (mixed + piece(own_ref, k, count)[...]).astype(BF)
-        copies.append(pltpu.make_async_copy(out, piece(out_hbm, k, count), sems.at[k]))
+        part = slice(k * step, (k + 1) * step)
+        mixed = jnp.dot(combine, rows_ref[:, part], preferred_element_type=F32)
+        out_ref[:, part] = (mixed + own_ref[:, part]).astype(BF)
+        copies.append(pltpu.make_async_copy(out_ref.at[:, part], out_hbm.at[:, part], sems.at[k]))
         copies[-1].start()
     for copy in copies:
         copy.wait()
@@ -230,37 +223,32 @@
     with jax.named_scope("swap_tokens"):
         other = lax.ppermute(tokens, "c", swap)
     with jax.named_scope("front"):
-        rows, acc, stat, tok, emb = call(
+        rows, acc, stat = call(
             front_kernel,
-            (
-                shape((half, width), BF),
-                shape((half, width), F32),
-                shape((half, TAIL), F32),
-                shape(tokens.shape, BF),
-                shape(slot_embed.shape, BF),
-            ),
+            (shape((half, width), BF), shape((half, width), F32), shape((half, TAIL), F32)),
             core,
             pltpu.with_memory_space_constraint(tokens, pltpu.HBM),
             pltpu.with_memory_space_constraint(slot_embed, pltpu.HBM),
             scalars=1,
             hbm=2,
-            scratch=(pltpu.SemaphoreType.DMA((2, 4)),),
+            scratch=(
+                pltpu.VMEM(tokens.shape, BF),
+                pltpu.VMEM(slot_embed.shape, BF),
+                pltpu.SemaphoreType.DMA((5,)),
+                pltpu.SemaphoreType.DMA((4,)),
+            ),
             mib=24,
             flops=10**9,
             moved=4 << 20,
         )
     with jax.named_scope("pool"):
-        part, combine = call(
+        part = call(
             pool_kernel,
-            (shape((half, full), BF), shape((count, slots), BF)),
-            core,
+            shape((half, full), BF),
             rows,
             acc,
             stat,
             other,
-            tok,
-            emb,
-            scalars=1,
             mib=24,
             flops=10**9,
             moved=3 << 20,
@@ -309,12 +297,10 @@
             mix_own_kernel,
             (shape((count, width), F32), shape((count, half), BF)),
             core,
-            tok,
-            emb,
-            combine,
+            tokens,
+            slot_embed,
             own,
             scalars=1,
-            scratch=(pltpu.VMEM((count, slots), BF),),
             mib=24,
             flops=10**9,
             moved=3 << 20,
@@ -326,7 +312,7 @@
             combine,
             other,
             hbm_out=True,
-            scratch=(pltpu.VMEM((count, width), BF), pltpu.SemaphoreType.DMA((8,))),
+            scratch=(pltpu.VMEM((count, width), BF), pltpu.SemaphoreType.DMA((5,))),
             moved=3 << 20,
         )
 

time: 113 us -> 111 us (0.982)
  local copies, waits for them, and re-layouts: 2.06 us -> 0.32 us
    unnamed x20 -> x12, local copies, waits for them, and re-layouts: 1.77 us -> 0.03 us
  transfers between devices with their start and end apart: 2 -> 2, of which waited for: 1 -> 0; matrix products, arithmetic and copies ran while one was open for 0% -> 0% of each run, Pallas kernels for 3% -> 5%
where the time goes in v6:
time: 111 us
  blocking collectives  82.6 us (74%)
  starting transfers between devices  17.9 us (16%)
  Pallas kernels  9.44 us (9%)
    all_to_all x1, blocking collectives, per_device(): lax.all_to_all(part.reshape(ZL * ZH, 2, full), ('zl', 'zh'), 0, 0, tiled=...  25.4 us
    all_to_all x1, blocking collectives, per_device(): lax.all_to_all(part.reshape(X * Y, ZL * 2, full), ('x', 'y'), 0, 0, tiled...  15.9 us
    all_to_all x1, blocking collectives, per_device(): got = lax.all_to_all(spread, ('zl', 'zh'), 0, 0, tiled=True)  14.8 us
    all_to_all x1, blocking collectives, per_device(): lax.all_to_all(spread, ('x', 'y'), 0, 0, tiled=True).reshape(half, width)  13 us
    pallas_call x7, Pallas kernels, call(): pl.pallas_call(kernel, out_shape=out_shape, in_specs=[smem] * scalars + [...  9.44 us
    ppermute x1, starting transfers between devices, per_device(): other = lax.ppermute(own, 'c', swap)  9.11 us
    ppermute x1, starting transfers between devices, per_device(): other = lax.ppermute(tokens, 'c', swap)  8.78 us
    all_to_all x1, blocking collectives, per_device(): lax.all_to_all(partial_out.reshape(Y, 2, width), 'y', 0, 0, tiled=True)  6.83 us
  transfers between devices with their start and end apart: 2, of which 0 were waited for; matrix products, arithmetic and copies ran while one was open for 0% of the time, Pallas kernels for 5%

profile of v6, /device:TPU:1, one launch (start us, length us, event | category | flops | bytes accessed | tf_op | source)
XLA Modules:
  0.0 110.5 jit_solution(14432897341420515903)
XLA Ops:
  0.0 8.8 %collective-permute-start = (bf16[384,1280]{1,0:T(8,128)(2,1)}, bf16[384,1280]{1,0:T(8,128)(2,1)S(1)}, u32[]{:S(2)}, u32[]{:S(2)}) collective-permute-start(bf16[384,1280]{1,0:T(8,128)(2,1)} %tok_ref.1), channel_id=1, source_target_pairs={{0,8},{8,0},{1,9},{9,1},{2,10},{10,2},{3,11},{11,3},{4,12},{12,4},... | collective-permute-start | bytes 2949128 | tf_op jit(solution)/shard_map/swap_tokens/ppermute | solution.py:224
  8.8 3.9 %front.1 = (bf16[256,1280]{1,0:T(8,128)(2,1)S(1)}, f32[256,1280]{1,0:T(8,128)S(1)}, f32[256,128]{1,0:T(8,128)S(1)}) custom-call(s32[1]{0:T(128)} %bitcast.core_ref, bf16[384,1280]{1,0:T(8,128)(2,1)} %tok_ref.1, bf16[1280,512]{1,0:T(8,128)(2,1)} %emb_ref.1), custom_call_target="tpu_custom_call" | custom-call | flops 1000000000 | bytes 4194304 | tf_op jit(solution)/shard_map/front/pallas_call | solution.py:200
  12.7 0.0 collective-permute-done.other_ref
  12.7 0.0 copy-start.1
  12.7 1.4 %pool.1 = bf16[256,1408]{1,0:T(8,128)(2,1)S(1)} custom-call(bf16[256,1280]{1,0:T(8,128)(2,1)S(1)} %get-tuple-element.10.rows_ref, f32[256,1280]{1,0:T(8,128)S(1)} %get-tuple-element.11.acc_ref, f32[256,128]{1,0:T(8,128)S(1)} %get-tuple-element.12.stat_ref, bf16[384,1280]{1,0:T(8,128)(2,1)S(1)} %collective-permute-done.other_ref), custom_call_target="tpu_custom_call" | custom-call | flops 1000000000 | bytes 3145728 | tf_op jit(solution)/shard_map/pool/pallas_call | solution.py:200
  14.1 0.0 copy-start
  14.1 0.0 copy-start.2
  14.1 0.0 copy-start.3
  14.1 15.9 %all_to_all.30 = bf16[16,16,1408]{2,1,0:T(8,128)(2,1)S(1)} all-to-all(bf16[16,16,1408]{2,1,0:T(8,128)(2,1)S(1)} %bitcast.10), channel_id=1, replica_groups=mesh['zl'=8,'x'=4,'c'=2,'y'=4,'zh'=2] {'x','y'}, dimensions={0} | all-to-all | bytes 1441792 | tf_op jit(solution)/shard_map/sum_xy/all_to_all | solution.py:257
  30.1 0.3 sum_xy.1
  30.5 0.1 broadcast_in_dim.21
  30.5 25.4 %all_to_all.31 = bf16[16,2,1408]{2,1,0:T(2,128)(2,1)S(1)} all-to-all(bf16[16,2,1408]{2,1,0:T(2,128)(2,1)S(1)} %bitcast.15), channel_id=1, replica_groups=mesh['zl'=8,'x'=4,'c'=2,'y'=4,'zh'=2] {'zl','zh'}, dimensions={0} | all-to-all | bytes 180224 | tf_op jit(solution)/shard_map/sum_z/all_to_all | solution.py:263
  55.9 0.2 sum_z.1
  56.2 6.6 %all_to_all.32 = bf16[4,2,1280]{2,1,0:T(2,128)(2,1)S(1)} all-to-all(bf16[4,2,1280]{2,1,0:T(2,128)(2,1)S(1)} %reshape.42), channel_id=1, replica_groups=mesh['zl'=8,'x'=4,'c'=2,'y'=4,'zh'=2] {'y'}, dimensions={0} | all-to-all | bytes 40960 | tf_op jit(solution)/shard_map/gather_y/all_to_all | solution.py:269
  62.8 0.0 copy-done.1
  62.8 0.0 copy-done
  62.8 0.0 copy-done.2
  62.9 0.0 copy-done.3
  62.9 0.7 expert.1
  63.5 0.0 copy-start.4
  63.5 0.0 copy-start.5
  63.6 6.8 %all_to_all.33 = f32[4,2,1280]{2,1,0:T(2,128)S(1)} all-to-all(f32[4,2,1280]{2,1,0:T(2,128)S(1)} %reshape.44), channel_id=1, replica_groups=mesh['zl'=8,'x'=4,'c'=2,'y'=4,'zh'=2] {'y'}, dimensions={0} | all-to-all | bytes 81920 | tf_op jit(solution)/shard_map/out_y/all_to_all | solution.py:283
  70.5 14.8 %all_to_all.34 = bf16[16,2,1280]{2,1,0:T(2,128)(2,1)S(1)} all-to-all(bf16[16,2,1280]{2,1,0:T(2,128)(2,1)S(1)} %broadcast_in_dim.22), channel_id=1, replica_groups=mesh['zl'=8,'x'=4,'c'=2,'y'=4,'zh'=2] {'zl','zh'}, dimensions={0} | all-to-all | bytes 163840 | tf_op jit(solution)/shard_map/out_z/all_to_all | solution.py:287
  85.3 0.1 bitcast_reduce_fusion
  85.5 13.0 %all_to_all.35 = bf16[16,16,1280]{2,1,0:T(8,128)(2,1)S(1)} all-to-all(bf16[16,16,1280]{2,1,0:T(8,128)(2,1)S(1)} %broadcast_in_dim.24), channel_id=1, replica_groups=mesh['zl'=8,'x'=4,'c'=2,'y'=4,'zh'=2] {'x','y'}, dimensions={0} | all-to-all | bytes 1310720 | tf_op jit(solution)/shard_map/out_xy/all_to_all | solution.py:292
  98.5 9.1 %collective-permute-start.1 = (bf16[256,1280]{1,0:T(8,128)(2,1)S(1)}, bf16[256,1280]{1,0:T(8,128)(2,1)S(1)}, u32[]{:S(2)}, u32[]{:S(2)}) collective-permute-start(bf16[256,1280]{1,0:T(8,128)(2,1)S(1)} %bitcast.13), channel_id=1, source_target_pairs={{0,8},{8,0},{1,9},{9,1},{2,10},{10,2},{3,11},{11,3},{4,12},{12,4},... | collective-permute-start | bytes 1966088 | tf_op jit(solution)/shard_map/out_core/ppermute | solution.py:294
  107.6 0.0 copy-done.4
  107.6 0.0 copy-done.5
  107.6 1.7 %mix.2 = (f32[384,1280]{1,0:T(8,128)S(1)}, bf16[384,256]{1,0:T(8,128)(2,1)S(1)}) custom-call(s32[1]{0:T(128)} %bitcast.core_ref, bf16[384,1280]{1,0:T(8,128)(2,1)S(1)} %copy-done.5, bf16[1280,512]{1,0:T(8,128)(2,1)S(1)} %copy-done.4, bf16[256,1280]{1,0:T(8,128)(2,1)S(1)} %bitcast.14), custom_call_target="tpu_custom_call" | custom-call | flops 1000000000 | bytes 3145728 | tf_op jit(solution)/shard_map/mix/pallas_call | solution.py:200
  109.3 0.0 collective-permute-done.1.rows_ref
  109.3 1.2 %mix.3 = bf16[384,1280]{1,0:T(8,128)(2,1)} custom-call(f32[384,1280]{1,0:T(8,128)S(1)} %get-tuple-element.13.own_ref, bf16[384,256]{1,0:T(8,128)(2,1)S(1)} %get-tuple-element.14.combine_ref, bf16[256,1280]{1,0:T(8,128)(2,1)S(1)} %collective-permute-done.1.rows_ref), custom_call_target="tpu_custom_call" | custom-call | bytes 3145728 | tf_op jit(solution)/shard_map/mix/pallas_call | solution.py:200
  (10 shorter events, 0.3 us)
Async XLA Ops:
  0.0 12.7 %collective-permute-start = (bf16[384,1280]{1,0:T(8,128)(2,1)}, bf16[384,1280]{1,0:T(8,128)(2,1)S(1)}, u32[]{:S(2)}, u32[]{:S(2)}) collective-permute-start(bf16[384,1280]{1,0:T(8,128)(2,1)} %tok_ref.1), channel_id=1, source_target_pairs={{0,8},{8,0},{1,9},{9,1},{2,10},{10,2},{3,11},{11,3},{4,12},{12,4},... | collective-permute-start | bytes 2949128 | tf_op jit(solution)/shard_map/swap_tokens/ppermute | solution.py:224
  12.7 50.2 %copy-start.1 = (bf16[1,640,1280]{2,1,0:T(8,128)(2,1)S(1)}, bf16[1,640,1280]{2,1,0:T(8,128)(2,1)}, u32[]{:S(2)}) copy-start(bf16[1,640,1280]{2,1,0:T(8,128)(2,1)} %param.10) | copy-start | bytes 4915204
  14.1 48.7 %copy-start = (bf16[1,1280,640]{2,1,0:T(8,128)(2,1)S(1)}, bf16[1,1280,640]{2,1,0:T(8,128)(2,1)}, u32[]{:S(2)}) copy-start(bf16[1,1280,640]{2,1,0:T(8,128)(2,1)} %param.8) | copy-start | bytes 4915204
  14.1 48.7 %copy-start.2 = (f32[1,1280]{1,0:T(1,128)S(1)}, f32[1,1280]{1,0:T(1,128)}, u32[]{:S(2)}) copy-start(f32[1,1280]{1,0:T(1,128)} %down_scale_ref.1) | copy-start | bytes 15364
  14.1 48.7 %copy-start.3 = (f32[1,640]{1,0:T(1,128)S(1)}, f32[1,640]{1,0:T(1,128)}, u32[]{:S(2)}) copy-start(f32[1,640]{1,0:T(1,128)} %up_scale_ref.1) | copy-start | bytes 7684
  63.5 44.1 %copy-start.4 = (bf16[1280,512]{1,0:T(8,128)(2,1)S(1)}, bf16[1280,512]{1,0:T(8,128)(2,1)}, u32[]{:S(2)}) copy-start(bf16[1280,512]{1,0:T(8,128)(2,1)} %emb_ref.1) | copy-start | bytes 3932164
  63.5 44.1 %copy-start.5 = (bf16[384,1280]{1,0:T(8,128)(2,1)S(1)}, bf16[384,1280]{1,0:T(8,128)(2,1)}, u32[]{:S(2)}) copy-start(bf16[384,1280]{1,0:T(8,128)(2,1)} %tok_ref.1) | copy-start | bytes 2949124
  98.5 10.8 %collective-permute-start.1 = (bf16[256,1280]{1,0:T(8,128)(2,1)S(1)}, bf16[256,1280]{1,0:T(8,128)(2,1)S(1)}, u32[]{:S(2)}, u32[]{:S(2)}) collective-permute-start(bf16[256,1280]{1,0:T(8,128)(2,1)S(1)} %bitcast.13), channel_id=1, source_target_pairs={{0,8},{8,0},{1,9},{9,1},{2,10},{10,2},{3,11},{11,3},{4,12},{12,4},... | collective-permute-start | bytes 1966088 | tf_op jit(solution)/shard_map/out_core/ppermute | solution.py:294

commit v7 on v6

--- a/solution.py
+++ b/solution.py
@@ -67,32 +67,30 @@
     return lax.dot_general(combine, order, NT, preferred_element_type=F32).astype(BF)
 
 
+def load(src, dst, sems):
+    count = sems.shape[0]
+    return [
+        pltpu.make_async_copy(piece(src, k, count), piece(dst, k, count), sems.at[k])
+        for k in range(count)
+    ]
+
+
 def front_kernel(
     core_ref, tok_hbm, emb_hbm, rows_ref, acc_ref, stat_ref, tok_ref, emb_ref, emb_sems, tok_sems
 ):
     slots = emb_ref.shape[1]
-    count = emb_sems.shape[0]
-    loads = [
-        pltpu.make_async_copy(piece(emb_hbm, k, count), piece(emb_ref, k, count), emb_sems.at[k])
-        for k in range(count)
-    ]
-    more = tok_sems.shape[0]
-    token_loads = [
-        pltpu.make_async_copy(piece(tok_hbm, k, more), piece(tok_ref, k, more), tok_sems.at[k])
-        for k in range(more)
-    ]
-    for copy in loads + token_loads:
+    emb_loads = load(emb_hbm, emb_ref, emb_sems)
+    tok_loads = load(tok_hbm, tok_ref, tok_sems)
+    for copy in emb_loads + tok_loads:
         copy.start()
     order = slot_order(core_ref[0], slots, slots // 2)
-    step = emb_ref.shape[0] // count
-    for k, copy in enumerate(loads):
+    for copy in emb_loads:
         copy.wait()
-        rows_ref[:, k * step : (k + 1) * step] = lax.dot_general(
-            order, piece(emb_ref, k, count)[...], NT, preferred_element_type=F32
-        ).astype(BF)
-    for copy in token_loads:
+    rows = lax.dot_general(order, emb_ref[...], NT, preferred_element_type=F32).astype(BF)
+    rows_ref[...] = rows
+    for copy in tok_loads:
         copy.wait()
-    shift, total, acc = pool(rows_ref[...], tok_ref[...])
+    shift, total, acc = pool(rows, tok_ref[...])
     acc_ref[...] = acc
     stat_ref[...] = tail_lanes(shift, total)
 
@@ -234,8 +232,8 @@
             scratch=(
                 pltpu.VMEM(tokens.shape, BF),
                 pltpu.VMEM(slot_embed.shape, BF),
-                pltpu.SemaphoreType.DMA((5,)),
-                pltpu.SemaphoreType.DMA((4,)),
+                pltpu.SemaphoreType.DMA((2,)),
+                pltpu.SemaphoreType.DMA((2,)),
             ),
             mib=24,
             flops=10**9,

time: 111 us -> 110 us (level)
  no operation moved by 1% of the time
where the time goes in v7:
time: 110 us
  blocking collectives  82.6 us (75%)
  starting transfers between devices  17.9 us (16%)
  Pallas kernels  8.89 us (8%)
    all_to_all x1, blocking collectives, per_device(): lax.all_to_all(part.reshape(ZL * ZH, 2, full), ('zl', 'zh'), 0, 0, tiled=...  25.4 us
    all_to_all x1, blocking collectives, per_device(): lax.all_to_all(part.reshape(X * Y, ZL * 2, full), ('x', 'y'), 0, 0, tiled...  15.9 us
    all_to_all x1, blocking collectives, per_device(): got = lax.all_to_all(spread, ('zl', 'zh'), 0, 0, tiled=True)  14.8 us
    all_to_all x1, blocking collectives, per_device(): lax.all_to_all(spread, ('x', 'y'), 0, 0, tiled=True).reshape(half, width)  13 us
    ppermute x1, starting transfers between devices, per_device(): other = lax.ppermute(own, 'c', swap)  9.1 us
    pallas_call x7, Pallas kernels, call(): pl.pallas_call(kernel, out_shape=out_shape, in_specs=[smem] * scalars + [...  8.89 us
    ppermute x1, starting transfers between devices, per_device(): other = lax.ppermute(tokens, 'c', swap)  8.78 us
    all_to_all x1, blocking collectives, per_device(): lax.all_to_all(partial_out.reshape(Y, 2, width), 'y', 0, 0, tiled=True)  6.83 us
  transfers between devices with their start and end apart: 2, of which 0 were waited for; matrix products, arithmetic and copies ran while one was open for 0% of the time, Pallas kernels for 5%

profile of v7, /device:TPU:1, one launch (start us, length us, event | category | flops | bytes accessed | tf_op | source)
XLA Modules:
  0.0 110.0 jit_solution(11956567123682478991)
XLA Ops:
  0.0 8.8 %collective-permute-start = (bf16[384,1280]{1,0:T(8,128)(2,1)}, bf16[384,1280]{1,0:T(8,128)(2,1)S(1)}, u32[]{:S(2)}, u32[]{:S(2)}) collective-permute-start(bf16[384,1280]{1,0:T(8,128)(2,1)} %tok_ref.1), channel_id=1, source_target_pairs={{0,8},{8,0},{1,9},{9,1},{2,10},{10,2},{3,11},{11,3},{4,12},{12,4},... | collective-permute-start | bytes 2949128 | tf_op jit(solution)/shard_map/swap_tokens/ppermute | solution.py:222
  8.8 3.3 %front.1 = (bf16[256,1280]{1,0:T(8,128)(2,1)S(1)}, f32[256,1280]{1,0:T(8,128)S(1)}, f32[256,128]{1,0:T(8,128)S(1)}) custom-call(s32[1]{0:T(128)} %bitcast.core_ref, bf16[384,1280]{1,0:T(8,128)(2,1)} %tok_ref.1, bf16[1280,512]{1,0:T(8,128)(2,1)} %emb_ref.1), custom_call_target="tpu_custom_call" | custom-call | flops 1000000000 | bytes 4194304 | tf_op jit(solution)/shard_map/front/pallas_call | solution.py:198
  12.1 0.0 collective-permute-done.other_ref
  12.1 0.0 copy-start.1
  12.1 1.4 %pool.1 = bf16[256,1408]{1,0:T(8,128)(2,1)S(1)} custom-call(bf16[256,1280]{1,0:T(8,128)(2,1)S(1)} %get-tuple-element.10.rows_ref, f32[256,1280]{1,0:T(8,128)S(1)} %get-tuple-element.11.acc_ref, f32[256,128]{1,0:T(8,128)S(1)} %get-tuple-element.12.stat_ref, bf16[384,1280]{1,0:T(8,128)(2,1)S(1)} %collective-permute-done.other_ref), custom_call_target="tpu_custom_call" | custom-call | flops 1000000000 | bytes 3145728 | tf_op jit(solution)/shard_map/pool/pallas_call | solution.py:198
  13.6 0.0 copy-start
  13.6 0.0 copy-start.2
  13.6 0.0 copy-start.3
  13.6 15.9 %all_to_all.30 = bf16[16,16,1408]{2,1,0:T(8,128)(2,1)S(1)} all-to-all(bf16[16,16,1408]{2,1,0:T(8,128)(2,1)S(1)} %bitcast.10), channel_id=1, replica_groups=mesh['zl'=8,'x'=4,'c'=2,'y'=4,'zh'=2] {'x','y'}, dimensions={0} | all-to-all | bytes 1441792 | tf_op jit(solution)/shard_map/sum_xy/all_to_all | solution.py:255
  29.5 0.3 sum_xy.1
  29.9 0.1 broadcast_in_dim.21
  30.0 25.4 %all_to_all.31 = bf16[16,2,1408]{2,1,0:T(2,128)(2,1)S(1)} all-to-all(bf16[16,2,1408]{2,1,0:T(2,128)(2,1)S(1)} %bitcast.15), channel_id=1, replica_groups=mesh['zl'=8,'x'=4,'c'=2,'y'=4,'zh'=2] {'zl','zh'}, dimensions={0} | all-to-all | bytes 180224 | tf_op jit(solution)/shard_map/sum_z/all_to_all | solution.py:261
  55.4 0.2 sum_z.1
  55.7 6.6 %all_to_all.32 = bf16[4,2,1280]{2,1,0:T(2,128)(2,1)S(1)} all-to-all(bf16[4,2,1280]{2,1,0:T(2,128)(2,1)S(1)} %reshape.42), channel_id=1, replica_groups=mesh['zl'=8,'x'=4,'c'=2,'y'=4,'zh'=2] {'y'}, dimensions={0} | all-to-all | bytes 40960 | tf_op jit(solution)/shard_map/gather_y/all_to_all | solution.py:267
  62.3 0.0 copy-done.1
  62.3 0.0 copy-done
  62.3 0.0 copy-done.2
  62.3 0.0 copy-done.3
  62.3 0.7 expert.1
  63.0 0.0 copy-start.4
  63.0 0.0 copy-start.5
  63.0 6.8 %all_to_all.33 = f32[4,2,1280]{2,1,0:T(2,128)S(1)} all-to-all(f32[4,2,1280]{2,1,0:T(2,128)S(1)} %reshape.44), channel_id=1, replica_groups=mesh['zl'=8,'x'=4,'c'=2,'y'=4,'zh'=2] {'y'}, dimensions={0} | all-to-all | bytes 81920 | tf_op jit(solution)/shard_map/out_y/all_to_all | solution.py:281
  69.9 14.8 %all_to_all.34 = bf16[16,2,1280]{2,1,0:T(2,128)(2,1)S(1)} all-to-all(bf16[16,2,1280]{2,1,0:T(2,128)(2,1)S(1)} %broadcast_in_dim.22), channel_id=1, replica_groups=mesh['zl'=8,'x'=4,'c'=2,'y'=4,'zh'=2] {'zl','zh'}, dimensions={0} | all-to-all | bytes 163840 | tf_op jit(solution)/shard_map/out_z/all_to_all | solution.py:285
  84.8 0.1 bitcast_reduce_fusion
  84.9 13.0 %all_to_all.35 = bf16[16,16,1280]{2,1,0:T(8,128)(2,1)S(1)} all-to-all(bf16[16,16,1280]{2,1,0:T(8,128)(2,1)S(1)} %broadcast_in_dim.24), channel_id=1, replica_groups=mesh['zl'=8,'x'=4,'c'=2,'y'=4,'zh'=2] {'x','y'}, dimensions={0} | all-to-all | bytes 1310720 | tf_op jit(solution)/shard_map/out_xy/all_to_all | solution.py:290
  97.9 9.1 %collective-permute-start.1 = (bf16[256,1280]{1,0:T(8,128)(2,1)S(1)}, bf16[256,1280]{1,0:T(8,128)(2,1)S(1)}, u32[]{:S(2)}, u32[]{:S(2)}) collective-permute-start(bf16[256,1280]{1,0:T(8,128)(2,1)S(1)} %bitcast.13), channel_id=1, source_target_pairs={{0,8},{8,0},{1,9},{9,1},{2,10},{10,2},{3,11},{11,3},{4,12},{12,4},... | collective-permute-start | bytes 1966088 | tf_op jit(solution)/shard_map/out_core/ppermute | solution.py:292
  107.1 0.0 copy-done.4
  107.1 0.0 copy-done.5
  107.1 1.7 %mix.2 = (f32[384,1280]{1,0:T(8,128)S(1)}, bf16[384,256]{1,0:T(8,128)(2,1)S(1)}) custom-call(s32[1]{0:T(128)} %bitcast.core_ref, bf16[384,1280]{1,0:T(8,128)(2,1)S(1)} %copy-done.5, bf16[1280,512]{1,0:T(8,128)(2,1)S(1)} %copy-done.4, bf16[256,1280]{1,0:T(8,128)(2,1)S(1)} %bitcast.14), custom_call_target="tpu_custom_call" | custom-call | flops 1000000000 | bytes 3145728 | tf_op jit(solution)/shard_map/mix/pallas_call | solution.py:198
  108.8 0.0 collective-permute-done.1.rows_ref
  108.8 1.2 %mix.3 = bf16[384,1280]{1,0:T(8,128)(2,1)} custom-call(f32[384,1280]{1,0:T(8,128)S(1)} %get-tuple-element.13.own_ref, bf16[384,256]{1,0:T(8,128)(2,1)S(1)} %get-tuple-element.14.combine_ref, bf16[256,1280]{1,0:T(8,128)(2,1)S(1)} %collective-permute-done.1.rows_ref), custom_call_target="tpu_custom_call" | custom-call | bytes 3145728 | tf_op jit(solution)/shard_map/mix/pallas_call | solution.py:198
  (10 shorter events, 0.3 us)
Async XLA Ops:
  0.0 12.1 %collective-permute-start = (bf16[384,1280]{1,0:T(8,128)(2,1)}, bf16[384,1280]{1,0:T(8,128)(2,1)S(1)}, u32[]{:S(2)}, u32[]{:S(2)}) collective-permute-start(bf16[384,1280]{1,0:T(8,128)(2,1)} %tok_ref.1), channel_id=1, source_target_pairs={{0,8},{8,0},{1,9},{9,1},{2,10},{10,2},{3,11},{11,3},{4,12},{12,4},... | collective-permute-start | bytes 2949128 | tf_op jit(solution)/shard_map/swap_tokens/ppermute | solution.py:222
  12.1 50.2 %copy-start.1 = (bf16[1,640,1280]{2,1,0:T(8,128)(2,1)S(1)}, bf16[1,640,1280]{2,1,0:T(8,128)(2,1)}, u32[]{:S(2)}) copy-start(bf16[1,640,1280]{2,1,0:T(8,128)(2,1)} %param.10) | copy-start | bytes 4915204
  13.6 48.7 %copy-start = (bf16[1,1280,640]{2,1,0:T(8,128)(2,1)S(1)}, bf16[1,1280,640]{2,1,0:T(8,128)(2,1)}, u32[]{:S(2)}) copy-start(bf16[1,1280,640]{2,1,0:T(8,128)(2,1)} %param.8) | copy-start | bytes 4915204
  13.6 48.7 %copy-start.2 = (f32[1,1280]{1,0:T(1,128)S(1)}, f32[1,1280]{1,0:T(1,128)}, u32[]{:S(2)}) copy-start(f32[1,1280]{1,0:T(1,128)} %down_scale_ref.1) | copy-start | bytes 15364
  13.6 48.7 %copy-start.3 = (f32[1,640]{1,0:T(1,128)S(1)}, f32[1,640]{1,0:T(1,128)}, u32[]{:S(2)}) copy-start(f32[1,640]{1,0:T(1,128)} %up_scale_ref.1) | copy-start | bytes 7684
  63.0 44.1 %copy-start.4 = (bf16[1280,512]{1,0:T(8,128)(2,1)S(1)}, bf16[1280,512]{1,0:T(8,128)(2,1)}, u32[]{:S(2)}) copy-start(bf16[1280,512]{1,0:T(8,128)(2,1)} %emb_ref.1) | copy-start | bytes 3932164
  63.0 44.1 %copy-start.5 = (bf16[384,1280]{1,0:T(8,128)(2,1)S(1)}, bf16[384,1280]{1,0:T(8,128)(2,1)}, u32[]{:S(2)}) copy-start(bf16[384,1280]{1,0:T(8,128)(2,1)} %tok_ref.1) | copy-start | bytes 2949124
  97.9 10.8 %collective-permute-start.1 = (bf16[256,1280]{1,0:T(8,128)(2,1)S(1)}, bf16[256,1280]{1,0:T(8,128)(2,1)S(1)}, u32[]{:S(2)}, u32[]{:S(2)}) collective-permute-start(bf16[256,1280]{1,0:T(8,128)(2,1)S(1)} %bitcast.13), channel_id=1, source_target_pairs={{0,8},{8,0},{1,9},{9,1},{2,10},{10,2},{3,11},{11,3},{4,12},{12,4},... | collective-permute-start | bytes 1966088 | tf_op jit(solution)/shard_map/out_core/ppermute | solution.py:292

commit v8 on v7

--- a/solution.py
+++ b/solution.py
@@ -95,7 +95,21 @@
     stat_ref[...] = tail_lanes(shift, total)
 
 
-def pool_kernel(rows_ref, acc_ref, stat_ref, other_ref, part_ref):
+def pool_kernel(
+    core_ref,
+    tok_hbm,
+    emb_hbm,
+    rows_ref,
+    acc_ref,
+    stat_ref,
+    other_ref,
+    part_ref,
+    combine_hbm,
+    tok_ref,
+    emb_ref,
+    combine_ref,
+    sems,
+):
     width = acc_ref.shape[1]
     shift_a, total_a = read_tail(stat_ref[...])
     shift_b, total_b, acc_b = pool(rows_ref[...], other_ref[...])
@@ -104,6 +118,21 @@
     weight_b = jnp.exp(shift_b - top)
     part_ref[:, :width] = (acc_ref[...] * weight_a + acc_b * weight_b).astype(BF)
     part_ref[:, width:] = tail_lanes(top, total_a * weight_a + total_b * weight_b).astype(BF)
+
+    @pl.when(core_ref[0] == 1)
+    def _():
+        loads = [
+            pltpu.make_async_copy(tok_hbm, tok_ref, sems.at[0]),
+            pltpu.make_async_copy(emb_hbm, emb_ref, sems.at[1]),
+        ]
+        for copy in loads:
+            copy.start()
+        for copy in loads:
+            copy.wait()
+        combine_ref[...] = combine_weights(tok_ref[...], emb_ref[...], core_ref[0])
+        store = pltpu.make_async_copy(combine_ref, combine_hbm, sems.at[2])
+        store.start()
+        store.wait()
 
 
 def plane_kernel(got_ref, part_ref):
@@ -157,11 +186,23 @@
     out_ref[...] = out * down_scale_ref[...]
 
 
-def mix_own_kernel(core_ref, tok_ref, emb_ref, rows_ref, out_ref, combine_ref):
+def mix_own_kernel(
+    core_ref, early_hbm, tok_ref, emb_ref, rows_ref, out_ref, combine_ref, all_ref, sems
+):
     half = rows_ref.shape[0]
-    combine = combine_weights(tok_ref[...], emb_ref[...], core_ref[0])
-    combine_ref[...] = combine[:, half:]
-    out_ref[...] = jnp.dot(combine[:, :half], rows_ref[...], preferred_element_type=F32)
+
+    @pl.when(core_ref[0] == 1)
+    def _():
+        copy = pltpu.make_async_copy(early_hbm, all_ref, sems.at[0])
+        copy.start()
+        copy.wait()
+
+    @pl.when(core_ref[0] == 0)
+    def _():
+        all_ref[...] = combine_weights(tok_ref[...], emb_ref[...], core_ref[0])
+
+    combine_ref[...] = all_ref[:, half:]
+    out_ref[...] = jnp.dot(all_ref[:, :half], rows_ref[...], preferred_element_type=F32)
 
 
 def mix_kernel(own_ref, combine_ref, rows_ref, out_hbm, out_ref, sems):
@@ -195,11 +236,14 @@
     smem = pl.BlockSpec(memory_space=pltpu.SMEM)
     far = pl.BlockSpec(memory_space=pltpu.HBM)
     many = isinstance(out_shape, (list, tuple))
+    outs = [vmem] * (len(out_shape) if many else 1)
+    if hbm_out:
+        outs[-1] = far
     return pl.pallas_call(
         kernel,
         out_shape=out_shape,
         in_specs=[smem] * scalars + [far] * hbm + [vmem] * (len(args) - scalars - hbm),
-        out_specs=[vmem] * len(out_shape) if many else (far if hbm_out else vmem),
+        out_specs=outs if many else outs[0],
         scratch_shapes=list(scratch),
         compiler_params=pltpu.CompilerParams(vmem_limit_bytes=mib << 20),
         cost_estimate=pl.CostEstimate(flops=flops, bytes_accessed=moved, transcendentals=0),
@@ -208,6 +252,10 @@
 
 def shape(dims, dtype):
     return jax.ShapeDtypeStruct(dims, dtype)
+
+
+def in_hbm(array):
+    return pltpu.with_memory_space_constraint(array, pltpu.HBM)
 
 
 def per_device(tokens, slot_embed, up_codes, up_scale, down_codes, down_scale):
@@ -225,8 +273,8 @@
             front_kernel,
             (shape((half, width), BF), shape((half, width), F32), shape((half, TAIL), F32)),
             core,
-            pltpu.with_memory_space_constraint(tokens, pltpu.HBM),
-            pltpu.with_memory_space_constraint(slot_embed, pltpu.HBM),
+            in_hbm(tokens),
+            in_hbm(slot_embed),
             scalars=1,
             hbm=2,
             scratch=(
@@ -240,13 +288,25 @@
             moved=4 << 20,
         )
     with jax.named_scope("pool"):
-        part = call(
+        part, early = call(
             pool_kernel,
-            shape((half, full), BF),
+            (shape((half, full), BF), pltpu.HBM((count, slots), BF)),
+            core,
+            in_hbm(tokens),
+            in_hbm(slot_embed),
             rows,
             acc,
             stat,
             other,
+            scalars=1,
+            hbm=2,
+            hbm_out=True,
+            scratch=(
+                pltpu.VMEM(tokens.shape, BF),
+                pltpu.VMEM(slot_embed.shape, BF),
+                pltpu.VMEM((count, slots), BF),
+                pltpu.SemaphoreType.DMA((3,)),
+            ),
             mib=24,
             flops=10**9,
             moved=3 << 20,
@@ -295,10 +355,13 @@
             mix_own_kernel,
             (shape((count, width), F32), shape((count, half), BF)),
             core,
+            in_hbm(early),
             tokens,
             slot_embed,
             own,
             scalars=1,
+            hbm=1,
+            scratch=(pltpu.VMEM((count, slots), BF), pltpu.SemaphoreType.DMA((1,))),
             mib=24,
             flops=10**9,
             moved=3 << 20,

time: 110 us -> 110 us (level)
  Pallas kernels: 8.89 us -> 12.4 us
  blocking collectives: 82.6 us -> 80.2 us
  starting transfers between devices: 17.9 us -> 15.8 us
    pallas_call x7, Pallas kernels: 8.89 us -> 12.4 us  [call(): pl.pallas_call(kernel, out_shape=out_shape, in_specs=[smem] * scalars + [...]
    all_to_all x1, blocking collectives: 15.9 us -> 13.3 us  [per_device(): lax.all_to_all(part.reshape(X * Y, ZL * 2, full), ('x', 'y'), 0, 0, tiled...]
    ppermute x1, starting transfers between devices: 9.1 us -> 7.06 us  [per_device(): other = lax.ppermute(own, 'c', swap)]
  transfers between devices with their start and end apart: 2 -> 2, of which waited for: 0 -> 1; matrix products, arithmetic and copies ran while one was open for 0% -> 0% of each run, Pallas kernels for 5% -> 4%
where the time goes in v8:
time: 110 us; the launch traced here: 109 us
  blocking collectives  80.2 us (73%)
  starting transfers between devices  15.8 us (14%)
  Pallas kernels  12.4 us (11%)
    all_to_all x1, blocking collectives, per_device(): lax.all_to_all(part.reshape(ZL * ZH, 2, full), ('zl', 'zh'), 0, 0, tiled=...  26.3 us
    all_to_all x1, blocking collectives, per_device(): got = lax.all_to_all(spread, ('zl', 'zh'), 0, 0, tiled=True)  14.6 us
    all_to_all x1, blocking collectives, per_device(): lax.all_to_all(part.reshape(X * Y, ZL * 2, full), ('x', 'y'), 0, 0, tiled...  13.3 us
    all_to_all x1, blocking collectives, per_device(): lax.all_to_all(spread, ('x', 'y'), 0, 0, tiled=True).reshape(half, width)  12.6 us
    pallas_call x7, Pallas kernels, call(): pl.pallas_call(kernel, out_shape=out_shape, in_specs=[smem] * scalars + [...  12.4 us
    ppermute x1, starting transfers between devices, per_device(): other = lax.ppermute(tokens, 'c', swap)  8.78 us
    ppermute x1, starting transfers between devices, per_device(): other = lax.ppermute(own, 'c', swap)  7.06 us
    all_to_all x1, blocking collectives, per_device(): lax.all_to_all(partial_out.reshape(Y, 2, width), 'y', 0, 0, tiled=True)  6.83 us
  transfers between devices with their start and end apart: 2, of which 1 were waited for; matrix products, arithmetic and copies ran while one was open for 0% of the time, Pallas kernels for 4%

profile of v8, /device:TPU:1, one launch (start us, length us, event | category | flops | bytes accessed | tf_op | source)
XLA Modules:
  0.0 109.3 jit_solution(16101446059999985669)
XLA Ops:
  0.0 8.8 %collective-permute-start = (bf16[384,1280]{1,0:T(8,128)(2,1)}, bf16[384,1280]{1,0:T(8,128)(2,1)S(1)}, u32[]{:S(2)}, u32[]{:S(2)}) collective-permute-start(bf16[384,1280]{1,0:T(8,128)(2,1)} %tok_ref.1), channel_id=1, source_target_pairs={{0,8},{8,0},{1,9},{9,1},{2,10},{10,2},{3,11},{11,3},{4,12},{12,4},... | collective-permute-start | bytes 2949128 | tf_op jit(solution)/shard_map/swap_tokens/ppermute | solution.py:270
  8.8 3.3 %front.1 = (bf16[256,1280]{1,0:T(8,128)(2,1)S(1)}, f32[256,1280]{1,0:T(8,128)S(1)}, f32[256,128]{1,0:T(8,128)S(1)}) custom-call(s32[1]{0:T(128)} %bitcast.core_ref, bf16[384,1280]{1,0:T(8,128)(2,1)} %tok_ref.1, bf16[1280,512]{1,0:T(8,128)(2,1)} %emb_ref.1), custom_call_target="tpu_custom_call" | custom-call | flops 1000000000 | bytes 4194304 | tf_op jit(solution)/shard_map/front/pallas_call | solution.py:242
  12.1 0.0 collective-permute-done.other_ref
  12.1 0.0 copy-start.1
  12.1 5.1 %pool.1 = (bf16[256,1408]{1,0:T(8,128)(2,1)S(1)}, bf16[384,512]{1,0:T(8,128)(2,1)}) custom-call(s32[1]{0:T(128)} %bitcast.core_ref, bf16[384,1280]{1,0:T(8,128)(2,1)} %tok_ref.1, bf16[1280,512]{1,0:T(8,128)(2,1)} %emb_ref.1, bf16[256,1280]{1,0:T(8,128)(2,1)S(1)} %get-tuple-element.12.rows_ref, f32[256,1280]{1,0:T(8,128)S(1)} %get-tuple-element.13.acc_ref, ...), custom_call_target="tpu_custom_call" | custom-call | flops 1000000000 | bytes 3145728 | tf_op jit(solution)/shard_map/pool/pallas_call | solution.py:242
  17.3 0.0 copy-start
  17.3 0.0 copy-start.4
  17.3 0.0 copy-start.5
  17.3 13.3 %all_to_all.30 = bf16[16,16,1408]{2,1,0:T(8,128)(2,1)S(1)} all-to-all(bf16[16,16,1408]{2,1,0:T(8,128)(2,1)S(1)} %bitcast.12), channel_id=1, replica_groups=mesh['zl'=8,'x'=4,'c'=2,'y'=4,'zh'=2] {'x','y'}, dimensions={0} | all-to-all | bytes 1441792 | tf_op jit(solution)/shard_map/sum_xy/all_to_all | solution.py:315
  30.6 0.3 sum_xy.1
  30.9 0.1 broadcast_in_dim.21
  31.0 26.3 %all_to_all.31 = bf16[16,2,1408]{2,1,0:T(2,128)(2,1)S(1)} all-to-all(bf16[16,2,1408]{2,1,0:T(2,128)(2,1)S(1)} %bitcast.15), channel_id=1, replica_groups=mesh['zl'=8,'x'=4,'c'=2,'y'=4,'zh'=2] {'zl','zh'}, dimensions={0} | all-to-all | bytes 180224 | tf_op jit(solution)/shard_map/sum_z/all_to_all | solution.py:321
  57.3 0.2 sum_z.1
  57.6 6.6 %all_to_all.32 = bf16[4,2,1280]{2,1,0:T(2,128)(2,1)S(1)} all-to-all(bf16[4,2,1280]{2,1,0:T(2,128)(2,1)S(1)} %reshape.42), channel_id=1, replica_groups=mesh['zl'=8,'x'=4,'c'=2,'y'=4,'zh'=2] {'y'}, dimensions={0} | all-to-all | bytes 40960 | tf_op jit(solution)/shard_map/gather_y/all_to_all | solution.py:327
  64.2 0.0 copy-done.1
  64.2 0.0 copy-done
  64.2 0.0 copy-done.4
  64.2 0.0 copy-done.5
  64.2 0.7 expert.1
  64.9 0.0 copy-start.2
  64.9 0.0 copy-start.3
  64.9 6.8 %all_to_all.33 = f32[4,2,1280]{2,1,0:T(2,128)S(1)} all-to-all(f32[4,2,1280]{2,1,0:T(2,128)S(1)} %reshape.44), channel_id=1, replica_groups=mesh['zl'=8,'x'=4,'c'=2,'y'=4,'zh'=2] {'y'}, dimensions={0} | all-to-all | bytes 81920 | tf_op jit(solution)/shard_map/out_y/all_to_all | solution.py:341
  71.8 14.6 %all_to_all.34 = bf16[16,2,1280]{2,1,0:T(2,128)(2,1)S(1)} all-to-all(bf16[16,2,1280]{2,1,0:T(2,128)(2,1)S(1)} %broadcast_in_dim.22), channel_id=1, replica_groups=mesh['zl'=8,'x'=4,'c'=2,'y'=4,'zh'=2] {'zl','zh'}, dimensions={0} | all-to-all | bytes 163840 | tf_op jit(solution)/shard_map/out_z/all_to_all | solution.py:345
  86.5 0.1 bitcast_reduce_fusion
  86.6 12.6 %all_to_all.35 = bf16[16,16,1280]{2,1,0:T(8,128)(2,1)S(1)} all-to-all(bf16[16,16,1280]{2,1,0:T(8,128)(2,1)S(1)} %broadcast_in_dim.24), channel_id=1, replica_groups=mesh['zl'=8,'x'=4,'c'=2,'y'=4,'zh'=2] {'x','y'}, dimensions={0} | all-to-all | bytes 1310720 | tf_op jit(solution)/shard_map/out_xy/all_to_all | solution.py:350
  99.3 7.1 %collective-permute-start.1 = (bf16[256,1280]{1,0:T(8,128)(2,1)S(1)}, bf16[256,1280]{1,0:T(8,128)(2,1)S(1)}, u32[]{:S(2)}, u32[]{:S(2)}) collective-permute-start(bf16[256,1280]{1,0:T(8,128)(2,1)S(1)} %bitcast.13), channel_id=1, source_target_pairs={{0,8},{8,0},{1,9},{9,1},{2,10},{10,2},{3,11},{11,3},{4,12},{12,4},... | collective-permute-start | bytes 1966088 | tf_op jit(solution)/shard_map/out_core/ppermute | solution.py:352
  106.3 0.0 copy-done.2
  106.3 0.0 copy-done.3
  106.3 1.5 %mix.2 = (f32[384,1280]{1,0:T(8,128)S(1)}, bf16[384,256]{1,0:T(8,128)(2,1)S(1)}) custom-call(s32[1]{0:T(128)} %bitcast.core_ref, bf16[384,512]{1,0:T(8,128)(2,1)} %get-tuple-element.15.early_hbm, bf16[384,1280]{1,0:T(8,128)(2,1)S(1)} %copy-done.3, bf16[1280,512]{1,0:T(8,128)(2,1)S(1)} %copy-done.2, bf16[256,1280]{1,0:T(8,128)(2,1)S(1)} %bitcast.14), custom_call_target="tpu_custom_call" | custom-call | flops 1000000000 | bytes 3145728 | tf_op jit(solution)/shard_map/mix/pallas_call | solution.py:242
  107.8 0.2 collective-permute-done.1.rows_ref
  108.0 1.2 %mix.3 = bf16[384,1280]{1,0:T(8,128)(2,1)} custom-call(f32[384,1280]{1,0:T(8,128)S(1)} %get-tuple-element.17.own_ref, bf16[384,256]{1,0:T(8,128)(2,1)S(1)} %get-tuple-element.18.combine_ref, bf16[256,1280]{1,0:T(8,128)(2,1)S(1)} %collective-permute-done.1.rows_ref), custom_call_target="tpu_custom_call" | custom-call | bytes 3145728 | tf_op jit(solution)/shard_map/mix/pallas_call | solution.py:242
  (10 shorter events, 0.3 us)
Async XLA Ops:
  0.0 12.1 %collective-permute-start = (bf16[384,1280]{1,0:T(8,128)(2,1)}, bf16[384,1280]{1,0:T(8,128)(2,1)S(1)}, u32[]{:S(2)}, u32[]{:S(2)}) collective-permute-start(bf16[384,1280]{1,0:T(8,128)(2,1)} %tok_ref.1), channel_id=1, source_target_pairs={{0,8},{8,0},{1,9},{9,1},{2,10},{10,2},{3,11},{11,3},{4,12},{12,4},... | collective-permute-start | bytes 2949128 | tf_op jit(solution)/shard_map/swap_tokens/ppermute | solution.py:270
  12.1 52.1 %copy-start.1 = (bf16[1,640,1280]{2,1,0:T(8,128)(2,1)S(1)}, bf16[1,640,1280]{2,1,0:T(8,128)(2,1)}, u32[]{:S(2)}) copy-start(bf16[1,640,1280]{2,1,0:T(8,128)(2,1)} %param.10) | copy-start | bytes 4915204
  17.3 46.9 %copy-start = (bf16[1,1280,640]{2,1,0:T(8,128)(2,1)S(1)}, bf16[1,1280,640]{2,1,0:T(8,128)(2,1)}, u32[]{:S(2)}) copy-start(bf16[1,1280,640]{2,1,0:T(8,128)(2,1)} %param.8) | copy-start | bytes 4915204
  17.3 46.9 %copy-start.4 = (f32[1,1280]{1,0:T(1,128)S(1)}, f32[1,1280]{1,0:T(1,128)}, u32[]{:S(2)}) copy-start(f32[1,1280]{1,0:T(1,128)} %down_scale_ref.1) | copy-start | bytes 15364
  17.3 46.9 %copy-start.5 = (f32[1,640]{1,0:T(1,128)S(1)}, f32[1,640]{1,0:T(1,128)}, u32[]{:S(2)}) copy-start(f32[1,640]{1,0:T(1,128)} %up_scale_ref.1) | copy-start | bytes 7684
  64.9 41.4 %copy-start.2 = (bf16[1280,512]{1,0:T(8,128)(2,1)S(1)}, bf16[1280,512]{1,0:T(8,128)(2,1)}, u32[]{:S(2)}) copy-start(bf16[1280,512]{1,0:T(8,128)(2,1)} %emb_ref.1) | copy-start | bytes 3932164
  64.9 41.5 %copy-start.3 = (bf16[384,1280]{1,0:T(8,128)(2,1)S(1)}, bf16[384,1280]{1,0:T(8,128)(2,1)}, u32[]{:S(2)}) copy-start(bf16[384,1280]{1,0:T(8,128)(2,1)} %tok_ref.1) | copy-start | bytes 2949124
  99.3 8.8 %collective-permute-start.1 = (bf16[256,1280]{1,0:T(8,128)(2,1)S(1)}, bf16[256,1280]{1,0:T(8,128)(2,1)S(1)}, u32[]{:S(2)}, u32[]{:S(2)}) collective-permute-start(bf16[256,1280]{1,0:T(8,128)(2,1)S(1)} %bitcast.13), channel_id=1, source_target_pairs={{0,8},{8,0},{1,9},{9,1},{2,10},{10,2},{3,11},{11,3},{4,12},{12,4},... | collective-permute-start | bytes 1966088 | tf_op jit(solution)/shard_map/out_core/ppermute | solution.py:352

commit v9 on v8

--- a/solution.py
+++ b/solution.py
@@ -157,10 +157,11 @@
 
 def line_kernel(got_ref, out_ref):
     width = out_ref.shape[1]
-    groups = [slice(8 * g, 8 * g + 8) for g in range(got_ref.shape[0] // 8)]
+    got = got_ref[...].astype(F32)
+    groups = [got[8 * g : 8 * g + 8] for g in range(got.shape[0] // 8)]
     stats = []
-    for g in groups:
-        shift, total = read_tail(got_ref[g, width:].astype(F32))
+    for group in groups:
+        shift, total = read_tail(group[:, width:])
         stats.append((jnp.broadcast_to(shift, (8, TAIL)), jnp.broadcast_to(total, (8, TAIL))))
     top = stats[0][0]
     for shift, _ in stats[1:]:
@@ -169,9 +170,9 @@
         top = jnp.maximum(top, pltpu.roll(top, step, 0))
     acc = jnp.zeros((8, width), F32)
     total = jnp.zeros((8, TAIL), F32)
-    for g, (shift, part_total) in zip(groups, stats):
+    for group, (shift, part_total) in zip(groups, stats):
         weight = jnp.exp(shift - top)
-        acc += got_ref[g, :width].astype(F32) * weight[:, 0:1]
+        acc += group[:, :width] * weight[:, 0:1]
         total += part_total * weight
     for step in (2, 4):
         acc += pltpu.roll(acc, step, 0)

time: 110 us -> 110 us (level)
  no operation moved by 1% of the time
where the time goes in v9:
time: 110 us; the launch traced here: 109 us
  blocking collectives  80.2 us (73%)
  starting transfers between devices  15.8 us (14%)
  Pallas kernels  12.4 us (11%)
    all_to_all x1, blocking collectives, per_device(): lax.all_to_all(part.reshape(ZL * ZH, 2, full), ('zl', 'zh'), 0, 0, tiled=...  26.3 us
    all_to_all x1, blocking collectives, per_device(): got = lax.all_to_all(spread, ('zl', 'zh'), 0, 0, tiled=True)  14.6 us
    all_to_all x1, blocking collectives, per_device(): lax.all_to_all(part.reshape(X * Y, ZL * 2, full), ('x', 'y'), 0, 0, tiled...  13.3 us
    all_to_all x1, blocking collectives, per_device(): lax.all_to_all(spread, ('x', 'y'), 0, 0, tiled=True).reshape(half, width)  12.6 us
    pallas_call x7, Pallas kernels, call(): pl.pallas_call(kernel, out_shape=out_shape, in_specs=[smem] * scalars + [...  12.4 us
    ppermute x1, starting transfers between devices, per_device(): other = lax.ppermute(tokens, 'c', swap)  8.78 us
    ppermute x1, starting transfers between devices, per_device(): other = lax.ppermute(own, 'c', swap)  7.06 us
    all_to_all x1, blocking collectives, per_device(): lax.all_to_all(partial_out.reshape(Y, 2, width), 'y', 0, 0, tiled=True)  6.83 us
  transfers between devices with their start and end apart: 2, of which 1 were waited for; matrix products, arithmetic and copies ran while one was open for 0% of the time, Pallas kernels for 4%

profile of v9, /device:TPU:1, one launch (start us, length us, event | category | flops | bytes accessed | tf_op | source)
XLA Modules:
  0.0 109.3 jit_solution(18022112421367402564)
XLA Ops:
  0.0 8.8 %collective-permute-start = (bf16[384,1280]{1,0:T(8,128)(2,1)}, bf16[384,1280]{1,0:T(8,128)(2,1)S(1)}, u32[]{:S(2)}, u32[]{:S(2)}) collective-permute-start(bf16[384,1280]{1,0:T(8,128)(2,1)} %tok_ref.1), channel_id=1, source_target_pairs={{0,8},{8,0},{1,9},{9,1},{2,10},{10,2},{3,11},{11,3},{4,12},{12,4},... | collective-permute-start | bytes 2949128 | tf_op jit(solution)/shard_map/swap_tokens/ppermute | solution.py:271
  8.8 3.3 %front.1 = (bf16[256,1280]{1,0:T(8,128)(2,1)S(1)}, f32[256,1280]{1,0:T(8,128)S(1)}, f32[256,128]{1,0:T(8,128)S(1)}) custom-call(s32[1]{0:T(128)} %bitcast.core_ref, bf16[384,1280]{1,0:T(8,128)(2,1)} %tok_ref.1, bf16[1280,512]{1,0:T(8,128)(2,1)} %emb_ref.1), custom_call_target="tpu_custom_call" | custom-call | flops 1000000000 | bytes 4194304 | tf_op jit(solution)/shard_map/front/pallas_call | solution.py:243
  12.1 0.0 collective-permute-done.other_ref
  12.1 0.0 copy-start.1
  12.1 5.1 %pool.1 = (bf16[256,1408]{1,0:T(8,128)(2,1)S(1)}, bf16[384,512]{1,0:T(8,128)(2,1)}) custom-call(s32[1]{0:T(128)} %bitcast.core_ref, bf16[384,1280]{1,0:T(8,128)(2,1)} %tok_ref.1, bf16[1280,512]{1,0:T(8,128)(2,1)} %emb_ref.1, bf16[256,1280]{1,0:T(8,128)(2,1)S(1)} %get-tuple-element.12.rows_ref, f32[256,1280]{1,0:T(8,128)S(1)} %get-tuple-element.13.acc_ref, ...), custom_call_target="tpu_custom_call" | custom-call | flops 1000000000 | bytes 3145728 | tf_op jit(solution)/shard_map/pool/pallas_call | solution.py:243
  17.3 0.0 copy-start
  17.3 0.0 copy-start.4
  17.3 0.0 copy-start.5
  17.3 13.3 %all_to_all.30 = bf16[16,16,1408]{2,1,0:T(8,128)(2,1)S(1)} all-to-all(bf16[16,16,1408]{2,1,0:T(8,128)(2,1)S(1)} %bitcast.12), channel_id=1, replica_groups=mesh['zl'=8,'x'=4,'c'=2,'y'=4,'zh'=2] {'x','y'}, dimensions={0} | all-to-all | bytes 1441792 | tf_op jit(solution)/shard_map/sum_xy/all_to_all | solution.py:316
  30.6 0.3 sum_xy.1
  30.9 0.1 broadcast_in_dim.21
  31.0 26.3 %all_to_all.31 = bf16[16,2,1408]{2,1,0:T(2,128)(2,1)S(1)} all-to-all(bf16[16,2,1408]{2,1,0:T(2,128)(2,1)S(1)} %bitcast.15), channel_id=1, replica_groups=mesh['zl'=8,'x'=4,'c'=2,'y'=4,'zh'=2] {'zl','zh'}, dimensions={0} | all-to-all | bytes 180224 | tf_op jit(solution)/shard_map/sum_z/all_to_all | solution.py:322
  57.3 0.2 sum_z.1
  57.6 6.6 %all_to_all.32 = bf16[4,2,1280]{2,1,0:T(2,128)(2,1)S(1)} all-to-all(bf16[4,2,1280]{2,1,0:T(2,128)(2,1)S(1)} %reshape.42), channel_id=1, replica_groups=mesh['zl'=8,'x'=4,'c'=2,'y'=4,'zh'=2] {'y'}, dimensions={0} | all-to-all | bytes 40960 | tf_op jit(solution)/shard_map/gather_y/all_to_all | solution.py:328
  64.2 0.0 copy-done.1
  64.2 0.0 copy-done
  64.2 0.0 copy-done.4
  64.2 0.0 copy-done.5
  64.2 0.7 expert.1
  64.9 0.0 copy-start.2
  64.9 0.0 copy-start.3
  64.9 6.8 %all_to_all.33 = f32[4,2,1280]{2,1,0:T(2,128)S(1)} all-to-all(f32[4,2,1280]{2,1,0:T(2,128)S(1)} %reshape.44), channel_id=1, replica_groups=mesh['zl'=8,'x'=4,'c'=2,'y'=4,'zh'=2] {'y'}, dimensions={0} | all-to-all | bytes 81920 | tf_op jit(solution)/shard_map/out_y/all_to_all | solution.py:342
  71.8 14.6 %all_to_all.34 = bf16[16,2,1280]{2,1,0:T(2,128)(2,1)S(1)} all-to-all(bf16[16,2,1280]{2,1,0:T(2,128)(2,1)S(1)} %broadcast_in_dim.22), channel_id=1, replica_groups=mesh['zl'=8,'x'=4,'c'=2,'y'=4,'zh'=2] {'zl','zh'}, dimensions={0} | all-to-all | bytes 163840 | tf_op jit(solution)/shard_map/out_z/all_to_all | solution.py:346
  86.5 0.1 bitcast_reduce_fusion
  86.6 12.6 %all_to_all.35 = bf16[16,16,1280]{2,1,0:T(8,128)(2,1)S(1)} all-to-all(bf16[16,16,1280]{2,1,0:T(8,128)(2,1)S(1)} %broadcast_in_dim.24), channel_id=1, replica_groups=mesh['zl'=8,'x'=4,'c'=2,'y'=4,'zh'=2] {'x','y'}, dimensions={0} | all-to-all | bytes 1310720 | tf_op jit(solution)/shard_map/out_xy/all_to_all | solution.py:351
  99.3 7.1 %collective-permute-start.1 = (bf16[256,1280]{1,0:T(8,128)(2,1)S(1)}, bf16[256,1280]{1,0:T(8,128)(2,1)S(1)}, u32[]{:S(2)}, u32[]{:S(2)}) collective-permute-start(bf16[256,1280]{1,0:T(8,128)(2,1)S(1)} %bitcast.13), channel_id=1, source_target_pairs={{0,8},{8,0},{1,9},{9,1},{2,10},{10,2},{3,11},{11,3},{4,12},{12,4},... | collective-permute-start | bytes 1966088 | tf_op jit(solution)/shard_map/out_core/ppermute | solution.py:353
  106.3 0.0 copy-done.2
  106.3 0.0 copy-done.3
  106.3 1.5 %mix.2 = (f32[384,1280]{1,0:T(8,128)S(1)}, bf16[384,256]{1,0:T(8,128)(2,1)S(1)}) custom-call(s32[1]{0:T(128)} %bitcast.core_ref, bf16[384,512]{1,0:T(8,128)(2,1)} %get-tuple-element.15.early_hbm, bf16[384,1280]{1,0:T(8,128)(2,1)S(1)} %copy-done.3, bf16[1280,512]{1,0:T(8,128)(2,1)S(1)} %copy-done.2, bf16[256,1280]{1,0:T(8,128)(2,1)S(1)} %bitcast.14), custom_call_target="tpu_custom_call" | custom-call | flops 1000000000 | bytes 3145728 | tf_op jit(solution)/shard_map/mix/pallas_call | solution.py:243
  107.8 0.2 collective-permute-done.1.rows_ref
  108.0 1.2 %mix.3 = bf16[384,1280]{1,0:T(8,128)(2,1)} custom-call(f32[384,1280]{1,0:T(8,128)S(1)} %get-tuple-element.17.own_ref, bf16[384,256]{1,0:T(8,128)(2,1)S(1)} %get-tuple-element.18.combine_ref, bf16[256,1280]{1,0:T(8,128)(2,1)S(1)} %collective-permute-done.1.rows_ref), custom_call_target="tpu_custom_call" | custom-call | bytes 3145728 | tf_op jit(solution)/shard_map/mix/pallas_call | solution.py:243
  (10 shorter events, 0.3 us)
Async XLA Ops:
  0.0 12.1 %collective-permute-start = (bf16[384,1280]{1,0:T(8,128)(2,1)}, bf16[384,1280]{1,0:T(8,128)(2,1)S(1)}, u32[]{:S(2)}, u32[]{:S(2)}) collective-permute-start(bf16[384,1280]{1,0:T(8,128)(2,1)} %tok_ref.1), channel_id=1, source_target_pairs={{0,8},{8,0},{1,9},{9,1},{2,10},{10,2},{3,11},{11,3},{4,12},{12,4},... | collective-permute-start | bytes 2949128 | tf_op jit(solution)/shard_map/swap_tokens/ppermute | solution.py:271
  12.1 52.1 %copy-start.1 = (bf16[1,640,1280]{2,1,0:T(8,128)(2,1)S(1)}, bf16[1,640,1280]{2,1,0:T(8,128)(2,1)}, u32[]{:S(2)}) copy-start(bf16[1,640,1280]{2,1,0:T(8,128)(2,1)} %param.10) | copy-start | bytes 4915204
  17.3 46.9 %copy-start = (bf16[1,1280,640]{2,1,0:T(8,128)(2,1)S(1)}, bf16[1,1280,640]{2,1,0:T(8,128)(2,1)}, u32[]{:S(2)}) copy-start(bf16[1,1280,640]{2,1,0:T(8,128)(2,1)} %param.8) | copy-start | bytes 4915204
  17.3 46.9 %copy-start.4 = (f32[1,1280]{1,0:T(1,128)S(1)}, f32[1,1280]{1,0:T(1,128)}, u32[]{:S(2)}) copy-start(f32[1,1280]{1,0:T(1,128)} %down_scale_ref.1) | copy-start | bytes 15364
  17.3 46.9 %copy-start.5 = (f32[1,640]{1,0:T(1,128)S(1)}, f32[1,640]{1,0:T(1,128)}, u32[]{:S(2)}) copy-start(f32[1,640]{1,0:T(1,128)} %up_scale_ref.1) | copy-start | bytes 7684
  64.9 41.4 %copy-start.2 = (bf16[1280,512]{1,0:T(8,128)(2,1)S(1)}, bf16[1280,512]{1,0:T(8,128)(2,1)}, u32[]{:S(2)}) copy-start(bf16[1280,512]{1,0:T(8,128)(2,1)} %emb_ref.1) | copy-start | bytes 3932164
  64.9 41.5 %copy-start.3 = (bf16[384,1280]{1,0:T(8,128)(2,1)S(1)}, bf16[384,1280]{1,0:T(8,128)(2,1)}, u32[]{:S(2)}) copy-start(bf16[384,1280]{1,0:T(8,128)(2,1)} %tok_ref.1) | copy-start | bytes 2949124
  99.3 8.8 %collective-permute-start.1 = (bf16[256,1280]{1,0:T(8,128)(2,1)S(1)}, bf16[256,1280]{1,0:T(8,128)(2,1)S(1)}, u32[]{:S(2)}, u32[]{:S(2)}) collective-permute-start(bf16[256,1280]{1,0:T(8,128)(2,1)S(1)} %bitcast.13), channel_id=1, source_target_pairs={{0,8},{8,0},{1,9},{9,1},{2,10},{10,2},{3,11},{11,3},{4,12},{12,4},... | collective-permute-start | bytes 1966088 | tf_op jit(solution)/shard_map/out_core/ppermute | solution.py:353

commit v10 on v9

--- a/solution.py
+++ b/solution.py
@@ -177,7 +177,7 @@
     for step in (2, 4):
         acc += pltpu.roll(acc, step, 0)
         total += pltpu.roll(total, step, 0)
-    out_ref[...] = acc / total[:, 0:1]
+    out_ref[...] = (acc / total[:, 0:1]).astype(BF)
 
 
 def expert_kernel(in_ref, up_ref, up_scale_ref, down_ref, down_scale_ref, out_ref):
@@ -321,10 +321,10 @@
         part = jnp.broadcast_to(part.reshape(ZL, 1, 2, full), (ZL, ZH, 2, full))
         got = lax.all_to_all(part.reshape(ZL * ZH, 2, full), ("zl", "zh"), 0, 0, tiled=True)
         pairs = call(
-            line_kernel, shape((Y * 2, width), F32), got.reshape(ZL * ZH * 2, full), mib=8
+            line_kernel, shape((Y * 2, width), BF), got.reshape(ZL * ZH * 2, full), mib=8
         )
     with jax.named_scope("gather_y"):
-        spread = pairs.astype(BF).reshape(Y, 2, width)
+        spread = pairs.reshape(Y, 2, width)
         slot_inputs = lax.all_to_all(spread, "y", 0, 0, tiled=True).reshape(Y * 2, width)
 
     with jax.named_scope("expert"):

time: 110 us -> 110 us (level)
  no operation moved by 1% of the time
where the time goes in v10:
time: 110 us; the launch traced here: 109 us
  blocking collectives  80.2 us (73%)
  starting transfers between devices  15.8 us (14%)
  Pallas kernels  12.4 us (11%)
    all_to_all x1, blocking collectives, per_device(): lax.all_to_all(part.reshape(ZL * ZH, 2, full), ('zl', 'zh'), 0, 0, tiled=...  26.3 us
    all_to_all x1, blocking collectives, per_device(): got = lax.all_to_all(spread, ('zl', 'zh'), 0, 0, tiled=True)  14.6 us
    all_to_all x1, blocking collectives, per_device(): lax.all_to_all(part.reshape(X * Y, ZL * 2, full), ('x', 'y'), 0, 0, tiled...  13.3 us
    all_to_all x1, blocking collectives, per_device(): lax.all_to_all(spread, ('x', 'y'), 0, 0, tiled=True).reshape(half, width)  12.6 us
    pallas_call x7, Pallas kernels, call(): pl.pallas_call(kernel, out_shape=out_shape, in_specs=[smem] * scalars + [...  12.4 us
    ppermute x1, starting transfers between devices, per_device(): other = lax.ppermute(tokens, 'c', swap)  8.78 us
    ppermute x1, starting transfers between devices, per_device(): other = lax.ppermute(own, 'c', swap)  7.06 us
    all_to_all x1, blocking collectives, per_device(): lax.all_to_all(partial_out.reshape(Y, 2, width), 'y', 0, 0, tiled=True)  6.83 us
  transfers between devices with their start and end apart: 2, of which 1 were waited for; matrix products, arithmetic and copies ran while one was open for 0% of the time, Pallas kernels for 4%

profile of v10, /device:TPU:1, one launch (start us, length us, event | category | flops | bytes accessed | tf_op | source)
XLA Modules:
  0.0 109.3 jit_solution(11330188023788265745)
XLA Ops:
  0.0 8.8 %collective-permute-start = (bf16[384,1280]{1,0:T(8,128)(2,1)}, bf16[384,1280]{1,0:T(8,128)(2,1)S(1)}, u32[]{:S(2)}, u32[]{:S(2)}) collective-permute-start(bf16[384,1280]{1,0:T(8,128)(2,1)} %tok_ref.1), channel_id=1, source_target_pairs={{0,8},{8,0},{1,9},{9,1},{2,10},{10,2},{3,11},{11,3},{4,12},{12,4},... | collective-permute-start | bytes 2949128 | tf_op jit(solution)/shard_map/swap_tokens/ppermute | solution.py:271
  8.8 3.3 %front.1 = (bf16[256,1280]{1,0:T(8,128)(2,1)S(1)}, f32[256,1280]{1,0:T(8,128)S(1)}, f32[256,128]{1,0:T(8,128)S(1)}) custom-call(s32[1]{0:T(128)} %bitcast.core_ref, bf16[384,1280]{1,0:T(8,128)(2,1)} %tok_ref.1, bf16[1280,512]{1,0:T(8,128)(2,1)} %emb_ref.1), custom_call_target="tpu_custom_call" | custom-call | flops 1000000000 | bytes 4194304 | tf_op jit(solution)/shard_map/front/pallas_call | solution.py:243
  12.1 0.0 collective-permute-done.other_ref
  12.1 0.0 copy-start.1
  12.1 5.1 %pool.1 = (bf16[256,1408]{1,0:T(8,128)(2,1)S(1)}, bf16[384,512]{1,0:T(8,128)(2,1)}) custom-call(s32[1]{0:T(128)} %bitcast.core_ref, bf16[384,1280]{1,0:T(8,128)(2,1)} %tok_ref.1, bf16[1280,512]{1,0:T(8,128)(2,1)} %emb_ref.1, bf16[256,1280]{1,0:T(8,128)(2,1)S(1)} %get-tuple-element.12.rows_ref, f32[256,1280]{1,0:T(8,128)S(1)} %get-tuple-element.13.acc_ref, ...), custom_call_target="tpu_custom_call" | custom-call | flops 1000000000 | bytes 3145728 | tf_op jit(solution)/shard_map/pool/pallas_call | solution.py:243
  17.3 0.0 copy-start
  17.3 0.0 copy-start.4
  17.3 0.0 copy-start.5
  17.3 13.3 %all_to_all.30 = bf16[16,16,1408]{2,1,0:T(8,128)(2,1)S(1)} all-to-all(bf16[16,16,1408]{2,1,0:T(8,128)(2,1)S(1)} %bitcast.12), channel_id=1, replica_groups=mesh['zl'=8,'x'=4,'c'=2,'y'=4,'zh'=2] {'x','y'}, dimensions={0} | all-to-all | bytes 1441792 | tf_op jit(solution)/shard_map/sum_xy/all_to_all | solution.py:316
  30.6 0.3 sum_xy.1
  30.9 0.1 broadcast_in_dim.21
  31.0 26.3 %all_to_all.31 = bf16[16,2,1408]{2,1,0:T(2,128)(2,1)S(1)} all-to-all(bf16[16,2,1408]{2,1,0:T(2,128)(2,1)S(1)} %bitcast.15), channel_id=1, replica_groups=mesh['zl'=8,'x'=4,'c'=2,'y'=4,'zh'=2] {'zl','zh'}, dimensions={0} | all-to-all | bytes 180224 | tf_op jit(solution)/shard_map/sum_z/all_to_all | solution.py:322
  57.3 0.2 sum_z.1
  57.6 6.6 %all_to_all.32 = bf16[4,2,1280]{2,1,0:T(2,128)(2,1)S(1)} all-to-all(bf16[4,2,1280]{2,1,0:T(2,128)(2,1)S(1)} %reshape.42), channel_id=1, replica_groups=mesh['zl'=8,'x'=4,'c'=2,'y'=4,'zh'=2] {'y'}, dimensions={0} | all-to-all | bytes 40960 | tf_op jit(solution)/shard_map/gather_y/all_to_all | solution.py:328
  64.2 0.0 copy-done.1
  64.2 0.0 copy-done
  64.2 0.0 copy-done.4
  64.2 0.0 copy-done.5
  64.2 0.7 expert.1
  64.9 0.0 copy-start.2
  64.9 0.0 copy-start.3
  64.9 6.8 %all_to_all.33 = f32[4,2,1280]{2,1,0:T(2,128)S(1)} all-to-all(f32[4,2,1280]{2,1,0:T(2,128)S(1)} %reshape.44), channel_id=1, replica_groups=mesh['zl'=8,'x'=4,'c'=2,'y'=4,'zh'=2] {'y'}, dimensions={0} | all-to-all | bytes 81920 | tf_op jit(solution)/shard_map/out_y/all_to_all | solution.py:342
  71.8 14.6 %all_to_all.34 = bf16[16,2,1280]{2,1,0:T(2,128)(2,1)S(1)} all-to-all(bf16[16,2,1280]{2,1,0:T(2,128)(2,1)S(1)} %broadcast_in_dim.22), channel_id=1, replica_groups=mesh['zl'=8,'x'=4,'c'=2,'y'=4,'zh'=2] {'zl','zh'}, dimensions={0} | all-to-all | bytes 163840 | tf_op jit(solution)/shard_map/out_z/all_to_all | solution.py:346
  86.5 0.1 bitcast_reduce_fusion
  86.6 12.6 %all_to_all.35 = bf16[16,16,1280]{2,1,0:T(8,128)(2,1)S(1)} all-to-all(bf16[16,16,1280]{2,1,0:T(8,128)(2,1)S(1)} %broadcast_in_dim.24), channel_id=1, replica_groups=mesh['zl'=8,'x'=4,'c'=2,'y'=4,'zh'=2] {'x','y'}, dimensions={0} | all-to-all | bytes 1310720 | tf_op jit(solution)/shard_map/out_xy/all_to_all | solution.py:351
  99.2 7.1 %collective-permute-start.1 = (bf16[256,1280]{1,0:T(8,128)(2,1)S(1)}, bf16[256,1280]{1,0:T(8,128)(2,1)S(1)}, u32[]{:S(2)}, u32[]{:S(2)}) collective-permute-start(bf16[256,1280]{1,0:T(8,128)(2,1)S(1)} %bitcast.13), channel_id=1, source_target_pairs={{0,8},{8,0},{1,9},{9,1},{2,10},{10,2},{3,11},{11,3},{4,12},{12,4},... | collective-permute-start | bytes 1966088 | tf_op jit(solution)/shard_map/out_core/ppermute | solution.py:353
  106.3 0.0 copy-done.2
  106.3 0.0 copy-done.3
  106.3 1.5 %mix.2 = (f32[384,1280]{1,0:T(8,128)S(1)}, bf16[384,256]{1,0:T(8,128)(2,1)S(1)}) custom-call(s32[1]{0:T(128)} %bitcast.core_ref, bf16[384,512]{1,0:T(8,128)(2,1)} %get-tuple-element.15.early_hbm, bf16[384,1280]{1,0:T(8,128)(2,1)S(1)} %copy-done.3, bf16[1280,512]{1,0:T(8,128)(2,1)S(1)} %copy-done.2, bf16[256,1280]{1,0:T(8,128)(2,1)S(1)} %bitcast.14), custom_call_target="tpu_custom_call" | custom-call | flops 1000000000 | bytes 3145728 | tf_op jit(solution)/shard_map/mix/pallas_call | solution.py:243
  107.8 0.2 collective-permute-done.1.rows_ref
  108.0 1.2 %mix.3 = bf16[384,1280]{1,0:T(8,128)(2,1)} custom-call(f32[384,1280]{1,0:T(8,128)S(1)} %get-tuple-element.17.own_ref, bf16[384,256]{1,0:T(8,128)(2,1)S(1)} %get-tuple-element.18.combine_ref, bf16[256,1280]{1,0:T(8,128)(2,1)S(1)} %collective-permute-done.1.rows_ref), custom_call_target="tpu_custom_call" | custom-call | bytes 3145728 | tf_op jit(solution)/shard_map/mix/pallas_call | solution.py:243
  (9 shorter events, 0.3 us)
Async XLA Ops:
  0.0 12.1 %collective-permute-start = (bf16[384,1280]{1,0:T(8,128)(2,1)}, bf16[384,1280]{1,0:T(8,128)(2,1)S(1)}, u32[]{:S(2)}, u32[]{:S(2)}) collective-permute-start(bf16[384,1280]{1,0:T(8,128)(2,1)} %tok_ref.1), channel_id=1, source_target_pairs={{0,8},{8,0},{1,9},{9,1},{2,10},{10,2},{3,11},{11,3},{4,12},{12,4},... | collective-permute-start | bytes 2949128 | tf_op jit(solution)/shard_map/swap_tokens/ppermute | solution.py:271
  12.1 52.0 %copy-start.1 = (bf16[1,640,1280]{2,1,0:T(8,128)(2,1)S(1)}, bf16[1,640,1280]{2,1,0:T(8,128)(2,1)}, u32[]{:S(2)}) copy-start(bf16[1,640,1280]{2,1,0:T(8,128)(2,1)} %param.10) | copy-start | bytes 4915204
  17.3 46.9 %copy-start = (bf16[1,1280,640]{2,1,0:T(8,128)(2,1)S(1)}, bf16[1,1280,640]{2,1,0:T(8,128)(2,1)}, u32[]{:S(2)}) copy-start(bf16[1,1280,640]{2,1,0:T(8,128)(2,1)} %param.8) | copy-start | bytes 4915204
  17.3 46.9 %copy-start.4 = (f32[1,1280]{1,0:T(1,128)S(1)}, f32[1,1280]{1,0:T(1,128)}, u32[]{:S(2)}) copy-start(f32[1,1280]{1,0:T(1,128)} %down_scale_ref.1) | copy-start | bytes 15364
  17.3 46.9 %copy-start.5 = (f32[1,640]{1,0:T(1,128)S(1)}, f32[1,640]{1,0:T(1,128)}, u32[]{:S(2)}) copy-start(f32[1,640]{1,0:T(1,128)} %up_scale_ref.1) | copy-start | bytes 7684
  64.9 41.4 %copy-start.2 = (bf16[1280,512]{1,0:T(8,128)(2,1)S(1)}, bf16[1280,512]{1,0:T(8,128)(2,1)}, u32[]{:S(2)}) copy-start(bf16[1280,512]{1,0:T(8,128)(2,1)} %emb_ref.1) | copy-start | bytes 3932164
  64.9 41.5 %copy-start.3 = (bf16[384,1280]{1,0:T(8,128)(2,1)S(1)}, bf16[384,1280]{1,0:T(8,128)(2,1)}, u32[]{:S(2)}) copy-start(bf16[384,1280]{1,0:T(8,128)(2,1)} %tok_ref.1) | copy-start | bytes 2949124
  99.2 8.8 %collective-permute-start.1 = (bf16[256,1280]{1,0:T(8,128)(2,1)S(1)}, bf16[256,1280]{1,0:T(8,128)(2,1)S(1)}, u32[]{:S(2)}, u32[]{:S(2)}) collective-permute-start(bf16[256,1280]{1,0:T(8,128)(2,1)S(1)} %bitcast.13), channel_id=1, source_target_pairs={{0,8},{8,0},{1,9},{9,1},{2,10},{10,2},{3,11},{11,3},{4,12},{12,4},... | collective-permute-start | bytes 1966088 | tf_op jit(solution)/shard_map/out_core/ppermute | solution.py:353
